TPU v7x, 32 devices: a whole 2x2x4 slice. The times are simulated.
32 devices in a mesh: groups: 2 (over y), patch: 16 (over z, x, core).
Axes of the slice: x: 2, y: 2, z: 4, core: 2. Of those that a mesh axis runs over, the one named last changes fastest.
Arguments:
- queries: bfloat16 [2, 768, 4096], P(None, ('groups', 'patch')), parts along dimension 1, may hold values from -44 to 44
- current_pairs: bfloat16 [2, 2, 768, 4096], P(None, None, ('groups', 'patch')), parts along dimension 2, may hold values from -5 to 5
- earlier_pairs: bfloat16 [2, 2, 768, 4096], P(None, None, ('groups', 'patch')), parts along dimension 2, may hold values from -5 to 5
- stale_cache: bfloat16 [2, 2, 32, 16, 24, 256], P(None, None, ('groups', 'patch')), parts along dimension 2, may hold values from -4 to 4
- block_exponents: int32 [2, 2, 768, 32], P(None, None, ('groups', 'patch')), parts along dimension 2, may hold values from 0 to 8
- step_index: int32 [2], P('groups'), parts along dimension 0, may hold values from 0 to 49
Outputs:
- attended: bfloat16 [2, 768, 4096], P(None, ('groups', 'patch')), parts along dimension 1
- renewed_cache: bfloat16 [2, 2, 32, 16, 24, 256], P(None, None, ('groups', 'patch')), parts along dimension 2
There are 2 independent parts, one for each index of `groups`. A program takes and returns all parts, laid end to end along the dimension named above; each array names one. Nothing has to cross between parts.
All inputs are finite; a program needn't handle non-finite values.
Results may differ from a plain program's by a relative error of at most 0.0086.
Values may be sent and summed in bfloat16 or wider, within the bound.
No kernel may reach another device: no remote copies, remote signals or barrier semaphores. Data moves between devices by JAX's collectives and lax.ppermute only.
A program may use at most 64 MiB of HBM per device.

v0:
```python
from functools import partial

import jax
import jax.numpy as jnp
import numpy as np
from jax import lax
from jax.sharding import PartitionSpec as P

STEPS = 50


saturation = 448.0
level_count = 9
gain_table = np.array([2.0**power for power in range(level_count)])
shrink_table = np.array([2.0 ** (-power) for power in range(level_count)])


def table_lookup(exponents, table):
    levels = jnp.arange(level_count, dtype=jnp.int32)
    values = jnp.asarray(table, dtype=jnp.float32)
    return jnp.sum(jnp.where(exponents[..., None] == levels, values, 0.0), -1)


def add_update(stale_part, arrived, blend):
    return (
        stale_part.astype(jnp.float32) + blend * arrived.transpose(1, 0, 2, 3).astype(jnp.float32)
    ).astype(jnp.bfloat16)


def block_width(sources, row_count):
    block_span = 1
    while (
        block_span < sources and block_span * row_count < 512 and (sources % (2 * block_span) == 0)
    ):
        block_span = block_span * 2
    return block_span


def answer_rows(arrived, key_rows, value_rows, group_count, part_count):
    sources, row_count, channel_count = arrived.shape
    group_heads = key_rows.shape[1]
    head_dim = key_rows.shape[2]
    score_scale = head_dim ** (-0.5)
    block_span = block_width(sources, row_count)
    blocks = arrived.reshape(sources // block_span, block_span * row_count, group_heads, head_dim)

    def one_block(query_block):
        scores = (
            jnp.einsum("qhd,khd->hqk", query_block, key_rows, preferred_element_type=jnp.float32)
            * score_scale
        )
        row_peak = jnp.max(scores, -1, keepdims=True)
        weights = jnp.exp(scores - row_peak)
        row_total = jnp.sum(weights, -1)
        partial_out = jnp.einsum(
            "hqk,khd->qhd",
            weights.astype(jnp.bfloat16),
            value_rows,
            preferred_element_type=jnp.float32,
        )
        partial_out = partial_out / row_total.T[..., None]
        log_total = (row_peak[..., 0] + jnp.log(row_total)).T
        return (partial_out, log_total)

    partial_out, log_total = lax.map(one_block, blocks)
    partial_out = partial_out.reshape(sources, row_count, channel_count)
    log_total = log_total.reshape(sources, row_count, group_heads)
    back_out, back_log = (
        lax.all_to_all(
            partial_out.astype(jnp.bfloat16), "patch", split_axis=0, concat_axis=0, tiled=True
        ).astype(partial_out.dtype),
        lax.all_to_all(
            log_total.astype(jnp.bfloat16), "patch", split_axis=0, concat_axis=0, tiled=True
        ).astype(log_total.dtype),
    )
    back_out = back_out.reshape(group_count, part_count, row_count, group_heads, head_dim)
    back_log = back_log.reshape(group_count, part_count, row_count, group_heads)
    highest = jnp.max(back_log, 1, keepdims=True)
    factor = jnp.exp(back_log - highest)
    merged = jnp.sum(factor[..., None] * back_out, 1) / jnp.sum(factor, 1)[..., None]
    return (
        merged.transpose(1, 0, 2, 3)
        .reshape(row_count, group_count * group_heads * head_dim)
        .astype(jnp.bfloat16)
    )


def body(queries, current_pairs, earlier_pairs, stale_cache, block_exponents, step_index):
    devices = lax.axis_size("patch")
    layer_count, token_count, channel_count = queries.shape
    head_count = block_exponents.shape[-1]
    head_dim = channel_count // head_count
    group_count = min(head_count, devices)
    part_count = devices // group_count
    group_heads = head_count // group_count
    part_rows = token_count // part_count
    group_width = group_heads * head_dim
    gains = table_lookup(block_exponents, gain_table)
    shrinks = table_lookup(block_exponents, shrink_table)
    residual = (current_pairs.astype(jnp.float32) - earlier_pairs.astype(jnp.float32)).reshape(
        layer_count, 2, token_count, head_count, head_dim
    )
    coded = lax.optimization_barrier(
        jnp.clip(residual * gains[..., None], -saturation, saturation).astype(jnp.bfloat16)
    )
    update = (coded.astype(jnp.float32) * shrinks[..., None]).astype(jnp.bfloat16)
    pieces_all = update.reshape(layer_count, 2, part_count, part_rows, group_count, group_width)
    pieces_all = pieces_all.transpose(0, 4, 2, 1, 3, 5).reshape(
        layer_count, devices, 2, part_rows, group_width
    )
    query_all = queries.reshape(layer_count, token_count, group_count, 1, group_width).transpose(
        0, 2, 3, 1, 4
    )
    query_all = jnp.broadcast_to(
        query_all, (layer_count, group_count, part_count, token_count, group_width)
    )
    query_all = query_all.reshape(layer_count, devices, token_count, group_width)
    selector = step_index[0] % 2
    blend = 1.0 - step_index[0].astype(jnp.float32) / (2.0 * STEPS)
    attended_list = []
    renewed_list = []
    for layer_index in range(layer_count):
        refresh = selector != layer_index % 2
        stale_part = stale_cache[layer_index, :, 0]
        pieces = pieces_all[layer_index]
        queries_out = query_all[layer_index]
        outgoing = jnp.where(refresh, pieces, jnp.zeros_like(pieces))
        arrived = lax.all_to_all(outgoing, "patch", split_axis=0, concat_axis=0, tiled=True)
        renewed = add_update(stale_part, arrived, blend)
        key_rows = renewed[0].reshape(devices * part_rows, group_heads, head_dim)
        value_rows = renewed[1].reshape(devices * part_rows, group_heads, head_dim)
        answer_fn = partial(
            answer_rows,
            key_rows=key_rows,
            value_rows=value_rows,
            group_count=group_count,
            part_count=part_count,
        )
        attended = answer_fn(
            lax.all_to_all(queries_out, "patch", split_axis=0, concat_axis=0, tiled=True)
        )
        attended_list.append(attended)
        renewed_list.append(renewed)
    return (jnp.stack(attended_list), jnp.stack(renewed_list)[:, :, None])


def solution(mesh):
    in_specs = (
        P(None, ("groups", "patch"), None),
        P(None, None, ("groups", "patch"), None),
        P(None, None, ("groups", "patch"), None),
        P(None, None, ("groups", "patch"), None, None, None),
        P(None, None, ("groups", "patch"), None),
        P("groups"),
    )
    out_specs = (
        P(None, ("groups", "patch"), None),
        P(None, None, ("groups", "patch"), None, None, None),
    )
    return jax.shard_map(body, mesh=mesh, in_specs=in_specs, out_specs=out_specs, check_vma=False)
```

profile of v0, /device:TPU:0, one launch (start us, length us, event | category | flops | bytes accessed | tf_op | source)
XLA Modules:
  0.0 110.3 jit_solution(3774303176612357366)
XLA Ops:
  0.6 1.1 copy.137
  2.6 7.4 %all-to-all-start.1 = ((bf16[16,24,256]{2,1,0:T(8,128)(2,1)}), bf16[16,24,256]{2,1,0:T(8,128)(2,1)S(1)}, u32[]{:S(2)}, u32[]{:S(2)}) async-start(bf16[16,24,256]{2,1,0:T(8,128)(2,1)} %get-tuple-element.56), calls=%async_computation.1 | async-start | bytes 393216 | tf_op jit(solution)/shard_map/all_to_all | solution.py:140
  11.7 7.3 %all-to-all-done.1 = bf16[16,24,256]{2,1,0:T(8,128)(2,1)S(1)} async-done(((bf16[16,24,256]{2,1,0:T(8,128)(2,1)}), bf16[16,24,256]{2,1,0:T(8,128)(2,1)S(1)}, u32[]{:S(2)}, u32[]{:S(2)}) %all-to-all-start.1) | async-done | bytes 196640 | tf_op jit(solution)/shard_map/all_to_all | solution.py:140
  19.0 3.5 %all-to-all-start.5 = ((bf16[16,24,256]{2,1,0:T(8,128)(2,1)}), bf16[16,24,256]{2,1,0:T(8,128)(2,1)S(1)}, u32[]{:S(2)}, u32[]{:S(2)}) async-start(bf16[16,24,256]{2,1,0:T(8,128)(2,1)} %get-tuple-element.57), calls=%async_computation.5 | async-start | bytes 393216 | tf_op jit(solution)/shard_map/all_to_all | solution.py:140
  24.0 0.9 copy.109
  24.9 6.6 %all-to-all-done.5 = bf16[16,24,256]{2,1,0:T(8,128)(2,1)S(1)} async-done(((bf16[16,24,256]{2,1,0:T(8,128)(2,1)}), bf16[16,24,256]{2,1,0:T(8,128)(2,1)S(1)}, u32[]{:S(2)}, u32[]{:S(2)}) %all-to-all-start.5) | async-done | bytes 196640 | tf_op jit(solution)/shard_map/all_to_all | solution.py:140
  31.5 3.6 %all-to-all-start = ((bf16[16,2,24,256]{3,2,1,0:T(8,128)(2,1)}), bf16[16,2,24,256]{3,2,1,0:T(8,128)(2,1)S(1)}, u32[]{:S(2)}, u32[]{:S(2)}) async-start(bf16[16,2,24,256]{3,2,1,0:T(8,128)(2,1)} %copy.109), calls=%async_computation | async-start | bytes 786432 | tf_op jit(solution)/shard_map/all_to_all | solution.py:128
  35.0 0.9 copy.121
  36.7 10.5 %all-to-all-done = bf16[16,2,24,256]{3,2,1,0:T(8,128)(2,1)S(1)} async-done(((bf16[16,2,24,256]{3,2,1,0:T(8,128)(2,1)}), bf16[16,2,24,256]{3,2,1,0:T(8,128)(2,1)S(1)}, u32[]{:S(2)}, u32[]{:S(2)}) %all-to-all-start) | async-done | bytes 393248 | tf_op jit(solution)/shard_map/all_to_all | solution.py:128
  47.2 3.6 %all-to-all-start.4 = ((bf16[16,2,24,256]{3,2,1,0:T(8,128)(2,1)}), bf16[16,2,24,256]{3,2,1,0:T(8,128)(2,1)S(1)}, u32[]{:S(2)}, u32[]{:S(2)}) async-start(bf16[16,2,24,256]{3,2,1,0:T(8,128)(2,1)} %copy.121), calls=%async_computation.4 | async-start | bytes 786432 | tf_op jit(solution)/shard_map/all_to_all | solution.py:128
  53.2 9.7 %all-to-all-done.4 = bf16[16,2,24,256]{3,2,1,0:T(8,128)(2,1)S(1)} async-done(((bf16[16,2,24,256]{3,2,1,0:T(8,128)(2,1)}), bf16[16,2,24,256]{3,2,1,0:T(8,128)(2,1)S(1)}, u32[]{:S(2)}, u32[]{:S(2)}) %all-to-all-start.4) | async-done | bytes 393248 | tf_op jit(solution)/shard_map/all_to_all | solution.py:128
  62.9 3.5 %all-to-all-start.2 = ((bf16[16,24,2]{1,2,0:T(2,128)(2,1)}), bf16[16,24,2]{1,2,0:T(2,128)(2,1)S(1)}, u32[]{:S(2)}, u32[]{:S(2)}) async-start(bf16[16,24,2]{1,2,0:T(2,128)(2,1)} %copy.113), calls=%async_computation.2 | async-start | bytes 16384 | tf_op jit(solution)/shard_map/all_to_all | solution.py:72
  67.3 1.4 %fusion.33 = (f32[2,384]{1,0:T(2,128)S(1)}, f32[2,384,384]{1,2,0:T(8,128)S(1)}) fusion(bf16[384,2,128]{2,1,0:T(2,128)(2,1)} %squeeze.27, bf16[384,2,128]{2,1,0:T(2,128)(2,1)} %reshape_squeeze.14), kind=kOutput, calls=%fused_computation.60 | convolution fusion | flops 76086528 | bytes 1575936 | tf_op jit(solution)/shard_map/while/body/eval_jaxpr/qhd,khd->hqk/dot_general | solution.py:49
  71.3 1.5 %all-to-all-done.2 = bf16[16,24,2]{1,2,0:T(2,128)(2,1)S(1)} async-done(((bf16[16,24,2]{1,2,0:T(2,128)(2,1)}), bf16[16,24,2]{1,2,0:T(2,128)(2,1)S(1)}, u32[]{:S(2)}, u32[]{:S(2)}) %all-to-all-start.2) | async-done | bytes 1568 | tf_op jit(solution)/shard_map/all_to_all | solution.py:72
  72.8 4.5 %all-to-all-start.6 = ((bf16[16,24,2]{1,2,0:T(2,128)(2,1)}), bf16[16,24,2]{1,2,0:T(2,128)(2,1)S(1)}, u32[]{:S(2)}, u32[]{:S(2)}) async-start(bf16[16,24,2]{1,2,0:T(2,128)(2,1)} %copy.124), calls=%async_computation.6 | async-start | bytes 16384 | tf_op jit(solution)/shard_map/all_to_all | solution.py:72
  77.3 1.3 %fusion.5 = bf16[384,2,128]{0,2,1:T(8,128)(2,1)S(1)} fusion(f32[2,384,384]{1,2,0:T(8,128)S(1)} %get-tuple-element.63, f32[2,384]{1,0:T(2,128)} %copy-done.4, bf16[384,2,128]{2,1,0:T(2,128)(2,1)} %reshape_squeeze.13, f32[384,2]{0,1:T(2,128)} %bitcast.107), kind=kOutput, calls=%fused_computation.14 | convolution fusion | flops 76283904 | bytes 1579008 | tf_op jit(solution)/shard_map/while/body/eval_jaxpr/hqk,khd->qhd/dot_general | solution.py:55
  78.8 0.8 convert_element_type.131
  79.6 4.0 %all-to-all-done.6 = bf16[16,24,2]{1,2,0:T(2,128)(2,1)S(1)} async-done(((bf16[16,24,2]{1,2,0:T(2,128)(2,1)}), bf16[16,24,2]{1,2,0:T(2,128)(2,1)S(1)}, u32[]{:S(2)}, u32[]{:S(2)}) %all-to-all-start.6) | async-done | bytes 1568 | tf_op jit(solution)/shard_map/all_to_all | solution.py:72
  83.6 3.5 %all-to-all-start.3 = ((bf16[16,24,256]{2,1,0:T(8,128)(2,1)}), bf16[16,24,256]{2,1,0:T(8,128)(2,1)S(1)}, u32[]{:S(2)}, u32[]{:S(2)}) async-start(bf16[16,24,256]{2,1,0:T(8,128)(2,1)} %convert_element_type.131), calls=%async_computation.3 | async-start | bytes 393216 | tf_op jit(solution)/shard_map/all_to_all | solution.py:69
  87.7 0.8 convert_element_type.144
  88.6 0.9 copy.131
  89.5 6.6 %all-to-all-done.3 = bf16[16,24,256]{2,1,0:T(8,128)(2,1)S(1)} async-done(((bf16[16,24,256]{2,1,0:T(8,128)(2,1)}), bf16[16,24,256]{2,1,0:T(8,128)(2,1)S(1)}, u32[]{:S(2)}, u32[]{:S(2)}) %all-to-all-start.3) | async-done | bytes 196640 | tf_op jit(solution)/shard_map/all_to_all | solution.py:69
  96.1 3.5 %all-to-all-start.7 = ((bf16[16,24,256]{2,1,0:T(8,128)(2,1)}), bf16[16,24,256]{2,1,0:T(8,128)(2,1)S(1)}, u32[]{:S(2)}, u32[]{:S(2)}) async-start(bf16[16,24,256]{2,1,0:T(8,128)(2,1)} %convert_element_type.144), calls=%async_computation.7 | async-start | bytes 393216 | tf_op jit(solution)/shard_map/all_to_all | solution.py:69
  101.0 7.6 %all-to-all-done.7 = bf16[16,24,256]{2,1,0:T(8,128)(2,1)S(1)} async-done(((bf16[16,24,256]{2,1,0:T(8,128)(2,1)}), bf16[16,24,256]{2,1,0:T(8,128)(2,1)S(1)}, u32[]{:S(2)}, u32[]{:S(2)}) %all-to-all-start.7) | async-done | bytes 196640 | tf_op jit(solution)/shard_map/all_to_all | solution.py:69
  (70 shorter events, 13.9 us)
Async XLA Ops:
  1.7 8.3 %copy-start.1 = (bf16[2,2,24,4096]{3,2,1,0:T(8,128)(2,1)S(1)}, bf16[2,2,24,4096]{3,2,1,0:T(8,128)(2,1)}, u32[]{:S(2)}) copy-start(bf16[2,2,24,4096]{3,2,1,0:T(8,128)(2,1)} %param.10) | copy-start | bytes 2359300
  1.7 8.3 %copy-start.2 = (bf16[2,2,24,4096]{3,2,1,0:T(8,128)(2,1)S(1)}, bf16[2,2,24,4096]{3,2,1,0:T(8,128)(2,1)}, u32[]{:S(2)}) copy-start(bf16[2,2,24,4096]{3,2,1,0:T(8,128)(2,1)} %param.9) | copy-start | bytes 2359300
  2.6 16.4 %all-to-all-start.1 = ((bf16[16,24,256]{2,1,0:T(8,128)(2,1)}), bf16[16,24,256]{2,1,0:T(8,128)(2,1)S(1)}, u32[]{:S(2)}, u32[]{:S(2)}) async-start(bf16[16,24,256]{2,1,0:T(8,128)(2,1)} %get-tuple-element.56), calls=%async_computation.1 | async-start | bytes 393216 | tf_op jit(solution)/shard_map/all_to_all | solution.py:140
  10.2 0.8 copy-start.3
  10.2 0.8 copy-start.10
  10.2 0.8 copy-start.11
  19.0 12.5 %all-to-all-start.5 = ((bf16[16,24,256]{2,1,0:T(8,128)(2,1)}), bf16[16,24,256]{2,1,0:T(8,128)(2,1)S(1)}, u32[]{:S(2)}, u32[]{:S(2)}) async-start(bf16[16,24,256]{2,1,0:T(8,128)(2,1)} %get-tuple-element.57), calls=%async_computation.5 | async-start | bytes 393216 | tf_op jit(solution)/shard_map/all_to_all | solution.py:140
  24.0 11.9 %copy-start = (bf16[2,2,1,16,24,256]{5,4,3,2,1,0:T(8,128)(2,1)S(1)}, bf16[2,2,1,16,24,256]{5,4,3,2,1,0:T(8,128)(2,1)}, u32[]{:S(2)}) copy-start(bf16[2,2,1,16,24,256]{5,4,3,2,1,0:T(8,128)(2,1)} %param.11) | copy-start | bytes 2359300
  31.5 15.7 %all-to-all-start = ((bf16[16,2,24,256]{3,2,1,0:T(8,128)(2,1)}), bf16[16,2,24,256]{3,2,1,0:T(8,128)(2,1)S(1)}, u32[]{:S(2)}, u32[]{:S(2)}) async-start(bf16[16,2,24,256]{3,2,1,0:T(8,128)(2,1)} %copy.109), calls=%async_computation | async-start | bytes 786432 | tf_op jit(solution)/shard_map/all_to_all | solution.py:128
  47.2 15.7 %all-to-all-start.4 = ((bf16[16,2,24,256]{3,2,1,0:T(8,128)(2,1)}), bf16[16,2,24,256]{3,2,1,0:T(8,128)(2,1)S(1)}, u32[]{:S(2)}, u32[]{:S(2)}) async-start(bf16[16,2,24,256]{3,2,1,0:T(8,128)(2,1)} %copy.121), calls=%async_computation.4 | async-start | bytes 786432 | tf_op jit(solution)/shard_map/all_to_all | solution.py:128
  51.3 0.6 copy-start.4
  51.9 0.6 copy-start.7
  62.9 9.9 %all-to-all-start.2 = ((bf16[16,24,2]{1,2,0:T(2,128)(2,1)}), bf16[16,24,2]{1,2,0:T(2,128)(2,1)S(1)}, u32[]{:S(2)}, u32[]{:S(2)}) async-start(bf16[16,24,2]{1,2,0:T(2,128)(2,1)} %copy.113), calls=%async_computation.2 | async-start | bytes 16384 | tf_op jit(solution)/shard_map/all_to_all | solution.py:72
  68.6 0.6 copy-start.5
  69.2 0.6 copy-start.8
  72.8 10.8 %all-to-all-start.6 = ((bf16[16,24,2]{1,2,0:T(2,128)(2,1)}), bf16[16,24,2]{1,2,0:T(2,128)(2,1)S(1)}, u32[]{:S(2)}, u32[]{:S(2)}) async-start(bf16[16,24,2]{1,2,0:T(2,128)(2,1)} %copy.124), calls=%async_computation.6 | async-start | bytes 16384 | tf_op jit(solution)/shard_map/all_to_all | solution.py:72
  78.6 8.6 %copy-start.6 = (f32[2,384]{1,0:T(2,128)S(1)}, f32[2,384]{1,0:T(2,128)}, u32[]{:S(2)}) copy-start(f32[2,384]{1,0:T(2,128)} %copy-done.5) | copy-start | bytes 9220
  78.6 8.6 %copy-start.9 = (f32[2,384]{1,0:T(2,128)S(1)}, f32[2,384]{1,0:T(2,128)}, u32[]{:S(2)}) copy-start(f32[2,384]{1,0:T(2,128)} %copy-done.8) | copy-start | bytes 9220
  83.6 12.5 %all-to-all-start.3 = ((bf16[16,24,256]{2,1,0:T(8,128)(2,1)}), bf16[16,24,256]{2,1,0:T(8,128)(2,1)S(1)}, u32[]{:S(2)}, u32[]{:S(2)}) async-start(bf16[16,24,256]{2,1,0:T(8,128)(2,1)} %convert_element_type.131), calls=%async_computation.3 | async-start | bytes 393216 | tf_op jit(solution)/shard_map/all_to_all | solution.py:69
  96.1 12.5 %all-to-all-start.7 = ((bf16[16,24,256]{2,1,0:T(8,128)(2,1)}), bf16[16,24,256]{2,1,0:T(8,128)(2,1)S(1)}, u32[]{:S(2)}, u32[]{:S(2)}) async-start(bf16[16,24,256]{2,1,0:T(8,128)(2,1)} %convert_element_type.144), calls=%async_computation.7 | async-start | bytes 393216 | tf_op jit(solution)/shard_map/all_to_all | solution.py:69
where the time goes:
time: 111 us; the launch traced here: 110 us
  waiting for transfers between devices  53.8 us (48%)
  starting transfers between devices  33 us (30%)
  local copies, waits for them, and re-layouts  14.7 us (13%)
  other arithmetic  3.82 us (3%)
  matrix products  3.36 us (3%)
  between operations  1.71 us (2%)
    all_to_all x2, waiting for transfers between devices, body(): lax.all_to_all(outgoing, 'patch', split_axis=0, concat_axis=0, tiled=True)  20.2 us
    all_to_all x2, waiting for transfers between devices, answer_rows(): lax.all_to_all(partial_out.astype(jnp.bfloat16), 'patch', split_axis=0, c...  14.2 us
    all_to_all x2, waiting for transfers between devices, body(): lax.all_to_all(queries_out, 'patch', split_axis=0, concat_axis=0, tiled=T...  13.9 us
    all_to_all x2, starting transfers between devices, body(): lax.all_to_all(queries_out, 'patch', split_axis=0, concat_axis=0, tiled=T...  10.9 us
    all_to_all x2, starting transfers between devices, answer_rows(): lax.all_to_all(log_total.astype(jnp.bfloat16), 'patch', split_axis=0, con...  7.94 us
    all_to_all x2, starting transfers between devices, body(): lax.all_to_all(outgoing, 'patch', split_axis=0, concat_axis=0, tiled=True)  7.11 us
    all_to_all x2, starting transfers between devices, answer_rows(): lax.all_to_all(partial_out.astype(jnp.bfloat16), 'patch', split_axis=0, c...  7.04 us
    all_to_all x2, waiting for transfers between devices, answer_rows(): lax.all_to_all(log_total.astype(jnp.bfloat16), 'patch', split_axis=0, con...  5.5 us
  transfers between devices with their start and end apart: 8, of which 8 were waited for; matrix products, arithmetic and copies ran while one was open for 14% of the time, Pallas kernels for 0%

commit v1 on v0

v1 whole, which is shorter than its diff:
```python
from functools import partial

import jax
import jax.numpy as jnp
from jax import lax
from jax.experimental import pallas as pl
from jax.experimental.pallas import tpu as pltpu
from jax.sharding import PartitionSpec as P

STEPS = 50
SATURATION = 448
TOP_LEVEL = 8
VMEM_BYTES = 40 * 1024 * 1024


def block_limits(exponents):
    return ((SATURATION << TOP_LEVEL) >> exponents).astype(jnp.float32) * (2.0**-TOP_LEVEL)


def blend_of(step):
    return 1.0 - step.astype(jnp.float32) / (2.0 * STEPS)


def exchange(rows):
    return lax.all_to_all(rows, "patch", split_axis=0, concat_axis=0, tiled=True)


def pack_kernel(step_ref, query_ref, current_ref, earlier_ref, exponent_ref, out_ref):
    layer_count = query_ref.shape[0]
    devices, _, _ = out_ref.shape
    head_count = exponent_ref.shape[-1]
    channel_count = query_ref.shape[-1]
    head_dim = channel_count // head_count
    width = channel_count // devices
    for layer in range(layer_count):
        for device in range(devices):
            out_ref[device, :, layer * width : (layer + 1) * width] = query_ref[
                layer, :, device * width : (device + 1) * width
            ]
    for side in range(2):
        limits = block_limits(exponent_ref[0, side])
        first = (layer_count + side) * width
        for head in range(head_count):
            span = slice(head * head_dim, (head + 1) * head_dim)
            residual = current_ref[0, side, :, span].astype(jnp.float32) - earlier_ref[
                0, side, :, span
            ].astype(jnp.float32)
            limit = limits[:, head : head + 1]
            update = jnp.minimum(jnp.maximum(residual, -limit), limit).astype(jnp.bfloat16)
            device, inner = divmod(head * head_dim, width)
            out_ref[device, :, first + inner : first + inner + head_dim] = update


def pack(step_index, queries, current_pairs, earlier_pairs, block_exponents, devices):
    layer_count, token_count, channel_count = queries.shape
    head_count = block_exponents.shape[-1]
    width = channel_count // devices

    def renewed_layer(i, step):
        return (1 - lax.rem(step[0], 2), 0, 0, 0)

    pair_spec = pl.BlockSpec((1, 2, token_count, channel_count), renewed_layer)
    return pl.pallas_call(
        pack_kernel,
        grid_spec=pltpu.PrefetchScalarGridSpec(
            num_scalar_prefetch=1,
            grid=(1,),
            in_specs=[
                pl.BlockSpec(queries.shape, lambda i, step: (0, 0, 0)),
                pair_spec,
                pair_spec,
                pl.BlockSpec((1, 2, token_count, head_count), renewed_layer),
            ],
            out_specs=pl.BlockSpec(
                (devices, token_count, (layer_count + 2) * width), lambda i, step: (0, 0, 0)
            ),
        ),
        out_shape=jax.ShapeDtypeStruct(
            (devices, token_count, (layer_count + 2) * width), jnp.bfloat16
        ),
        compiler_params=pltpu.CompilerParams(vmem_limit_bytes=VMEM_BYTES),
    )(step_index, queries, current_pairs, earlier_pairs, block_exponents)


def attend_kernel(head_dim, step_ref, arrived_ref, stale_ref, out_ref, renewed_ref):
    layer_count = stale_ref.shape[0]
    width = stale_ref.shape[-1]
    step = step_ref[0]
    blend = blend_of(step)
    score_scale = head_dim ** (-0.5)
    for layer in range(layer_count):
        weight = jnp.where(lax.rem(step, 2) != layer % 2, blend, 0.0)
        rows = []
        for side in range(2):
            first = (layer_count + side) * width
            update = arrived_ref[:, first : first + width].astype(jnp.float32)
            renewed = (stale_ref[layer, side].astype(jnp.float32) + weight * update).astype(
                jnp.bfloat16
            )
            renewed_ref[layer, side] = renewed
            rows.append(renewed)
        for head in range(width // head_dim):
            span = slice(head * head_dim, (head + 1) * head_dim)
            place = slice(layer * width + head * head_dim, layer * width + (head + 1) * head_dim)
            scores = lax.dot_general(
                arrived_ref[:, place],
                rows[0][:, span],
                (((1,), (1,)), ((), ())),
                preferred_element_type=jnp.float32,
            )
            peak = jnp.max(scores, -1, keepdims=True)
            weights = jnp.exp((scores - peak) * score_scale)
            total = jnp.sum(weights, -1, keepdims=True)
            mixed = jnp.dot(
                weights.astype(jnp.bfloat16),
                rows[1][:, span],
                preferred_element_type=jnp.float32,
            )
            out_ref[:, place] = (mixed / total).astype(jnp.bfloat16)


def attend(step_index, arrived, stale, head_dim):
    layer_count, _, row_count, width = stale.shape
    whole = pl.BlockSpec(memory_space=pltpu.VMEM)
    return pl.pallas_call(
        partial(attend_kernel, head_dim),
        in_specs=[pl.BlockSpec(memory_space=pltpu.SMEM), whole, whole],
        out_specs=[whole, whole],
        out_shape=[
            jax.ShapeDtypeStruct((row_count, layer_count * width), jnp.bfloat16),
            jax.ShapeDtypeStruct(stale.shape, jnp.bfloat16),
        ],
        compiler_params=pltpu.CompilerParams(vmem_limit_bytes=VMEM_BYTES),
    )(step_index, arrived, stale)


def whole_key_body(
    queries, current_pairs, earlier_pairs, stale_cache, block_exponents, step_index
):
    devices = lax.axis_size("patch")
    layer_count, token_count, channel_count = queries.shape
    head_dim = channel_count // block_exponents.shape[-1]
    width = channel_count // devices
    packed = pack(
        step_index, queries, current_pairs, earlier_pairs, block_exponents, devices
    )
    arrived = exchange(packed.reshape(devices * token_count, -1))
    stale = stale_cache.reshape(layer_count, 2, devices * token_count, width)
    partial_out, renewed = attend(step_index, arrived, stale, head_dim)
    back = exchange(partial_out)
    attended = (
        back.reshape(devices, token_count, layer_count, width)
        .transpose(2, 1, 0, 3)
        .reshape(layer_count, token_count, channel_count)
    )
    return attended, renewed.reshape(stale_cache.shape)


def answer_part(blocks, key_rows, value_rows):
    score_scale = key_rows.shape[-1] ** (-0.5)

    def one_block(query_block):
        scores = (
            jnp.einsum("qhd,khd->hqk", query_block, key_rows, preferred_element_type=jnp.float32)
            * score_scale
        )
        peak = jnp.max(scores, -1, keepdims=True)
        weights = jnp.exp(scores - peak)
        total = jnp.sum(weights, -1)
        mixed = jnp.einsum(
            "hqk,khd->qhd",
            weights.astype(jnp.bfloat16),
            value_rows,
            preferred_element_type=jnp.float32,
        )
        return mixed / total.T[..., None], (peak[..., 0] + jnp.log(total)).T

    return lax.map(one_block, blocks)


def split_key_body(
    queries, current_pairs, earlier_pairs, stale_cache, block_exponents, step_index
):
    devices = lax.axis_size("patch")
    layer_count, token_count, channel_count = queries.shape
    head_count = block_exponents.shape[-1]
    head_dim = channel_count // head_count
    group_count = min(head_count, devices)
    part_count = devices // group_count
    group_heads = head_count // group_count
    part_rows = token_count // part_count
    width = group_heads * head_dim
    selector = step_index[0] % 2
    blend = blend_of(step_index[0])
    limits = block_limits(block_exponents)[..., None]
    residual = (current_pairs.astype(jnp.float32) - earlier_pairs.astype(jnp.float32)).reshape(
        layer_count, 2, token_count, head_count, head_dim
    )
    update = jnp.clip(residual, -limits, limits).astype(jnp.bfloat16)
    pieces = update.reshape(layer_count, 2, part_count, part_rows, group_count, width)
    pieces = pieces.transpose(0, 4, 2, 1, 3, 5).reshape(
        layer_count, devices, 2 * part_rows, width
    )
    asked = queries.reshape(layer_count, token_count, group_count, 1, width)
    asked = jnp.broadcast_to(
        asked.transpose(0, 2, 3, 1, 4),
        (layer_count, group_count, part_count, token_count, width),
    ).reshape(layer_count, devices, token_count, width)
    attended_list = []
    renewed_list = []
    for layer in range(layer_count):
        refresh = selector != layer % 2
        outgoing = jnp.where(refresh, pieces[layer], jnp.zeros_like(pieces[layer]))
        arrived = exchange(jnp.concatenate([outgoing, asked[layer]], 1))
        arrived_update = arrived[:, : 2 * part_rows].reshape(devices, 2, part_rows, width)
        renewed = (
            stale_cache[layer, :, 0].astype(jnp.float32)
            + blend * arrived_update.transpose(1, 0, 2, 3).astype(jnp.float32)
        ).astype(jnp.bfloat16)
        key_rows = renewed[0].reshape(devices * part_rows, group_heads, head_dim)
        value_rows = renewed[1].reshape(devices * part_rows, group_heads, head_dim)
        block_span = 1
        while (
            block_span * token_count < 512 and devices % (2 * block_span) == 0
        ):
            block_span = block_span * 2
        blocks = arrived[:, 2 * part_rows :].reshape(
            devices // block_span, block_span * token_count, group_heads, head_dim
        )
        partial_out, log_total = answer_part(blocks, key_rows, value_rows)
        back_out = exchange(
            partial_out.astype(jnp.bfloat16).reshape(devices, token_count, width)
        ).astype(jnp.float32)
        back_log = exchange(
            log_total.astype(jnp.bfloat16).reshape(devices, token_count, group_heads)
        ).astype(jnp.float32)
        back_out = back_out.reshape(group_count, part_count, token_count, group_heads, head_dim)
        back_log = back_log.reshape(group_count, part_count, token_count, group_heads)
        factor = jnp.exp(back_log - jnp.max(back_log, 1, keepdims=True))
        merged = jnp.sum(factor[..., None] * back_out, 1) / jnp.sum(factor, 1)[..., None]
        attended_list.append(
            merged.transpose(1, 0, 2, 3)
            .reshape(token_count, channel_count)
            .astype(jnp.bfloat16)
        )
        renewed_list.append(renewed)
    return jnp.stack(attended_list), jnp.stack(renewed_list)[:, :, None]


def body(queries, current_pairs, earlier_pairs, stale_cache, block_exponents, step_index):
    layer_count = queries.shape[0]
    head_count = block_exponents.shape[-1]
    one_part = lax.axis_size("patch") <= head_count and layer_count == 2
    chosen = whole_key_body if one_part else split_key_body
    return chosen(
        queries, current_pairs, earlier_pairs, stale_cache, block_exponents, step_index
    )


def solution(mesh):
    in_specs = (
        P(None, ("groups", "patch"), None),
        P(None, None, ("groups", "patch"), None),
        P(None, None, ("groups", "patch"), None),
        P(None, None, ("groups", "patch"), None, None, None),
        P(None, None, ("groups", "patch"), None),
        P("groups"),
    )
    out_specs = (
        P(None, ("groups", "patch"), None),
        P(None, None, ("groups", "patch"), None, None, None),
    )
    return jax.shard_map(body, mesh=mesh, in_specs=in_specs, out_specs=out_specs, check_vma=False)
```

time: 111 us -> 52.8 us (0.48)
  waiting for transfers between devices: 53.8 us -> 0 us
  blocking collectives: 0 us -> 43.5 us
  starting transfers between devices: 33 us -> 0 us
  local copies, waits for them, and re-layouts: 14.7 us -> 5.2 us
  other arithmetic: 3.82 us -> 0 us
  matrix products: 3.36 us -> 0 us
  Pallas kernels: 0 us -> 2.49 us
    all_to_all x8 -> x0, waiting for transfers between devices: 53.8 us -> none  [the longest x2 20.2 us: body(): lax.all_to_all(outgoing, 'patch', split_axis=0, concat_axis=0, tiled=True)]
    all_to_all x0 -> x2, blocking collectives: none -> 43.5 us  [exchange(): lax.all_to_all(rows, 'patch', split_axis=0, concat_axis=0, tiled=True)]
    all_to_all x8 -> x0, starting transfers between devices: 33 us -> none  [the longest x2 10.9 us: body(): lax.all_to_all(queries_out, 'patch', split_axis=0, concat_axis=0, tiled=T...]
    convert_element_type x12 -> x0, local copies, waits for them, and re-layouts: 3.89 us -> none  [the longest x4 1.95 us: answer_rows(): partial_out.astype(jnp.bfloat16)]
    dot_general x4 -> x0, matrix products: 3.36 us -> none  [the longest x2 1.69 us: one_block(): jnp.einsum('qhd,khd->hqk', query_block, key_rows, preferred_element_type=...]
    pallas_call x0 -> x2, Pallas kernels: none -> 2.49 us  [the longest x1 2.09 us: attend(): pl.pallas_call(partial(attend_kernel, head_dim), in_specs=[pl.BlockSpec(m...]
    convert_element_type x8 -> x0, other arithmetic: 2.19 us -> none  [the longest x2 0.95 us: answer_rows(): return merged.transpose(1, 0, 2, 3).reshape(row_count, group_count * grou...]
    select_n x2 -> x0, local copies, waits for them, and re-layouts: 1.73 us -> none  [body(): outgoing = jnp.where(refresh, pieces, jnp.zeros_like(pieces))]
  transfers between devices with their start and end apart: 8 -> 0, of which waited for: 8 -> 0; matrix products, arithmetic and copies ran while one was open for 14% -> 0% of each run, Pallas kernels for 0% -> 0%
where the time goes in v1:
time: 52.8 us; the launch traced here: 52.5 us
  blocking collectives  43.5 us (82%)
  local copies, waits for them, and re-layouts  5.2 us (10%)
  Pallas kernels  2.49 us (5%)
  between operations  1.32 us (2%)
    all_to_all x2, blocking collectives, exchange(): lax.all_to_all(rows, 'patch', split_axis=0, concat_axis=0, tiled=True)  43.5 us
    unnamed x10, local copies, waits for them, and re-layouts  4.06 us
    pallas_call x1, Pallas kernels, attend(): pl.pallas_call(partial(attend_kernel, head_dim), in_specs=[pl.BlockSpec(m...  2.09 us

profile of v1, /device:TPU:0, one launch (start us, length us, event | category | flops | bytes accessed | tf_op | source)
XLA Modules:
  0.0 52.5 jit_solution(7574621065533038532)
XLA Ops:
  1.3 0.0 copy-start.1
  1.3 1.1 %copy-done.1 = bf16[2,2,24,4096]{3,2,1,0:T(8,128)(2,1)S(1)} copy-done((bf16[2,2,24,4096]{3,2,1,0:T(8,128)(2,1)S(1)}, bf16[2,2,24,4096]{3,2,1,0:T(8,128)(2,1)}, u32[]{:S(2)}) %copy-start.1) | copy-done | bytes 786456
  2.4 0.0 copy-start.2
  2.4 1.1 %copy-done.2 = bf16[2,2,24,4096]{3,2,1,0:T(8,128)(2,1)S(1)} copy-done((bf16[2,2,24,4096]{3,2,1,0:T(8,128)(2,1)S(1)}, bf16[2,2,24,4096]{3,2,1,0:T(8,128)(2,1)}, u32[]{:S(2)}) %copy-start.2) | copy-done | bytes 786456
  3.5 0.0 copy-start.3
  3.5 1.0 %copy-done.3 = bf16[2,24,4096]{2,1,0:T(8,128)(2,1)S(1)} copy-done((bf16[2,24,4096]{2,1,0:T(8,128)(2,1)S(1)}, bf16[2,24,4096]{2,1,0:T(8,128)(2,1)}, u32[]{:S(2)}) %copy-start.3) | copy-done | bytes 393240
  4.5 0.0 copy-start.4
  4.5 0.8 %copy-done.4 = s32[2,2,24,32]{3,2,1,0:T(8,128)S(1)} copy-done((s32[2,2,24,32]{3,2,1,0:T(8,128)S(1)}, s32[2,2,24,32]{3,2,1,0:T(8,128)}, u32[]{:S(2)}) %copy-start.4) | copy-done | bytes 12312
  5.3 0.4 shard_map.77
  5.7 0.0 copy-start
  5.8 27.6 %all_to_all.17 = bf16[16,24,1024]{2,1,0:T(8,128)(2,1)S(1)} all-to-all(bf16[16,24,1024]{2,1,0:T(8,128)(2,1)S(1)} %shard_map.77), channel_id=1, replica_groups=mesh['groups'=2,'patch'=16] {'patch'}, dimensions={0} | all-to-all | bytes 1572864 | tf_op jit(solution)/shard_map/all_to_all | solution.py:25
  33.3 0.0 copy-done
  33.3 2.1 %shard_map.78 = (bf16[384,512]{1,0:T(8,128)(2,1)S(1)}, bf16[2,2,384,256]{3,2,1,0:T(8,128)(2,1)}) custom-call(s32[1]{0:T(128)S(6)} %copy.12.step_ref, bf16[384,1024]{1,0:T(8,128)(2,1)S(1)} %bitcast.11, bf16[2,2,384,256]{3,2,1,0:T(8,128)(2,1)S(1)} %bitcast.12), custom_call_target="tpu_custom_call" | custom-call | tf_op jit(solution)/shard_map/pallas_call | solution.py:125
  35.4 15.9 %all_to_all.18 = bf16[16,24,512]{2,1,0:T(8,128)(2,1)S(1)} all-to-all(bf16[16,24,512]{2,1,0:T(8,128)(2,1)S(1)} %bitcast.13), channel_id=1, replica_groups=mesh['groups'=2,'patch'=16] {'patch'}, dimensions={0} | all-to-all | bytes 786432 | tf_op jit(solution)/shard_map/all_to_all | solution.py:25
  51.3 0.1 reshape.24
  51.4 0.1 copy.11
  51.5 0.9 %reshape.25 = bf16[2,24,4096]{2,1,0:T(8,128)(2,1)} reshape(bf16[2,24,16,256]{3,2,1,0:T(8,128)(2,1)S(1)} %bitcast.14) | data formatting | bytes 786432 | tf_op jit(solution)/shard_map/reshape | solution.py:154
Async XLA Ops:
  1.3 1.1 %copy-start.1 = (bf16[2,2,24,4096]{3,2,1,0:T(8,128)(2,1)S(1)}, bf16[2,2,24,4096]{3,2,1,0:T(8,128)(2,1)}, u32[]{:S(2)}) copy-start(bf16[2,2,24,4096]{3,2,1,0:T(8,128)(2,1)} %current_ref.1) | copy-start | bytes 2359300
  2.4 1.1 %copy-start.2 = (bf16[2,2,24,4096]{3,2,1,0:T(8,128)(2,1)S(1)}, bf16[2,2,24,4096]{3,2,1,0:T(8,128)(2,1)}, u32[]{:S(2)}) copy-start(bf16[2,2,24,4096]{3,2,1,0:T(8,128)(2,1)} %earlier_ref.1) | copy-start | bytes 2359300
  3.5 1.0 %copy-start.3 = (bf16[2,24,4096]{2,1,0:T(8,128)(2,1)S(1)}, bf16[2,24,4096]{2,1,0:T(8,128)(2,1)}, u32[]{:S(2)}) copy-start(bf16[2,24,4096]{2,1,0:T(8,128)(2,1)} %query_ref.1) | copy-start | bytes 1179652
  4.5 0.8 %copy-start.4 = (s32[2,2,24,32]{3,2,1,0:T(8,128)S(1)}, s32[2,2,24,32]{3,2,1,0:T(8,128)}, u32[]{:S(2)}) copy-start(s32[2,2,24,32]{3,2,1,0:T(8,128)} %exponent_ref.1) | copy-start | bytes 36868
  5.7 27.6 %copy-start = (bf16[2,2,1,16,24,256]{5,4,3,2,1,0:T(8,128)(2,1)S(1)}, bf16[2,2,1,16,24,256]{5,4,3,2,1,0:T(8,128)(2,1)}, u32[]{:S(2)}) copy-start(bf16[2,2,1,16,24,256]{5,4,3,2,1,0:T(8,128)(2,1)} %param.9) | copy-start | bytes 2359300

commit v2 on v1

--- a/solution.py
+++ b/solution.py
@@ -11,6 +11,7 @@
 SATURATION = 448
 TOP_LEVEL = 8
 VMEM_BYTES = 40 * 1024 * 1024
+PACK_BYTES = 60 * 1024 * 1024
 
 
 def block_limits(exponents):
@@ -25,71 +26,95 @@
     return lax.all_to_all(rows, "patch", split_axis=0, concat_axis=0, tiled=True)
 
 
-def pack_kernel(step_ref, query_ref, current_ref, earlier_ref, exponent_ref, out_ref):
-    layer_count = query_ref.shape[0]
-    devices, _, _ = out_ref.shape
+def pack_kernel(
+    step_ref,
+    query_ref,
+    current_ref,
+    earlier_ref,
+    exponent_ref,
+    packed_ref,
+    weight_ref,
+    queries,
+    current,
+    earlier,
+    exponents,
+    sems,
+):
+    layer_count, _, channel_count = query_ref.shape
+    devices = packed_ref.shape[0]
     head_count = exponent_ref.shape[-1]
-    channel_count = query_ref.shape[-1]
     head_dim = channel_count // head_count
     width = channel_count // devices
+    step = step_ref[0]
+    renewed_layer = 1 - lax.rem(step, 2)
+    pairs = (
+        (query_ref, queries),
+        (current_ref.at[renewed_layer], current),
+        (earlier_ref.at[renewed_layer], earlier),
+        (exponent_ref.at[renewed_layer], exponents),
+    )
+    copies = [
+        pltpu.make_async_copy(source, target, sems.at[index])
+        for index, (source, target) in enumerate(pairs)
+    ]
+    for copy in copies:
+        copy.start()
+    for layer in range(layer_count):
+        weight = jnp.where(lax.rem(step, 2) != layer % 2, blend_of(step), 0.0)
+        weight_ref[layer] = jnp.zeros(weight_ref.shape[1:], jnp.float32) + weight
+    copies[0].wait()
     for layer in range(layer_count):
         for device in range(devices):
-            out_ref[device, :, layer * width : (layer + 1) * width] = query_ref[
+            packed_ref[device, :, layer * width : (layer + 1) * width] = queries[
                 layer, :, device * width : (device + 1) * width
             ]
+    for copy in copies[1:]:
+        copy.wait()
     for side in range(2):
-        limits = block_limits(exponent_ref[0, side])
+        limits = block_limits(exponents[side])
         first = (layer_count + side) * width
         for head in range(head_count):
             span = slice(head * head_dim, (head + 1) * head_dim)
-            residual = current_ref[0, side, :, span].astype(jnp.float32) - earlier_ref[
-                0, side, :, span
+            residual = current[side, :, span].astype(jnp.float32) - earlier[
+                side, :, span
             ].astype(jnp.float32)
             limit = limits[:, head : head + 1]
             update = jnp.minimum(jnp.maximum(residual, -limit), limit).astype(jnp.bfloat16)
             device, inner = divmod(head * head_dim, width)
-            out_ref[device, :, first + inner : first + inner + head_dim] = update
+            packed_ref[device, :, first + inner : first + inner + head_dim] = update
 
 
 def pack(step_index, queries, current_pairs, earlier_pairs, block_exponents, devices):
     layer_count, token_count, channel_count = queries.shape
-    head_count = block_exponents.shape[-1]
     width = channel_count // devices
-
-    def renewed_layer(i, step):
-        return (1 - lax.rem(step[0], 2), 0, 0, 0)
-
-    pair_spec = pl.BlockSpec((1, 2, token_count, channel_count), renewed_layer)
+    far = pl.BlockSpec(memory_space=pl.ANY)
+    packed = jax.ShapeDtypeStruct(
+        (devices, token_count, (layer_count + 2) * width), jnp.bfloat16
+    )
+    layers = [current_pairs, earlier_pairs, block_exponents]
     return pl.pallas_call(
         pack_kernel,
-        grid_spec=pltpu.PrefetchScalarGridSpec(
-            num_scalar_prefetch=1,
-            grid=(1,),
-            in_specs=[
-                pl.BlockSpec(queries.shape, lambda i, step: (0, 0, 0)),
-                pair_spec,
-                pair_spec,
-                pl.BlockSpec((1, 2, token_count, head_count), renewed_layer),
-            ],
-            out_specs=pl.BlockSpec(
-                (devices, token_count, (layer_count + 2) * width), lambda i, step: (0, 0, 0)
-            ),
-        ),
-        out_shape=jax.ShapeDtypeStruct(
-            (devices, token_count, (layer_count + 2) * width), jnp.bfloat16
-        ),
-        compiler_params=pltpu.CompilerParams(vmem_limit_bytes=VMEM_BYTES),
+        in_specs=[pl.BlockSpec(memory_space=pltpu.SMEM)] + [far] * 4,
+        out_specs=[pl.BlockSpec(memory_space=pltpu.VMEM)]*2,
+        out_shape=[packed, jax.ShapeDtypeStruct((layer_count, 8, 128), jnp.float32)],
+        scratch_shapes=[pltpu.VMEM(queries.shape, queries.dtype)]
+        + [pltpu.VMEM(array.shape[1:], array.dtype) for array in layers]
+        + [
+            pltpu.SemaphoreType.DMA((4,)),
+        ],
+        compiler_params=pltpu.CompilerParams(vmem_limit_bytes=PACK_BYTES),
     )(step_index, queries, current_pairs, earlier_pairs, block_exponents)
 
 
-def attend_kernel(head_dim, step_ref, arrived_ref, stale_ref, out_ref, renewed_ref):
+def attend_kernel(
+    head_dim, weight_ref, arrived_ref, stale_ref, out_ref, renewed_out, renewed_ref, sems
+):
     layer_count = stale_ref.shape[0]
     width = stale_ref.shape[-1]
-    step = step_ref[0]
-    blend = blend_of(step)
     score_scale = head_dim ** (-0.5)
+    copies = []
     for layer in range(layer_count):
-        weight = jnp.where(lax.rem(step, 2) != layer % 2, blend, 0.0)
+        weight = weight_ref[layer, 0:1, 0:1]
         rows = []
         for side in range(2):
             first = (layer_count + side) * width
@@ -99,6 +124,12 @@
             )
             renewed_ref[layer, side] = renewed
             rows.append(renewed)
+        copies.append(
+            pltpu.make_async_copy(
+                renewed_ref.at[layer], renewed_out.at[layer], sems.at[layer]
+            )
+        )
+        copies[-1].start()
         for head in range(width // head_dim):
             span = slice(head * head_dim, (head + 1) * head_dim)
             place = slice(layer * width + head * head_dim, layer * width + (head + 1) * head_dim)
@@ -116,22 +147,34 @@
                 rows[1][:, span],
                 preferred_element_type=jnp.float32,
             )
-            out_ref[:, place] = (mixed / total).astype(jnp.bfloat16)
-
-
-def attend(step_index, arrived, stale, head_dim):
+            out_ref[:, layer, :, span] = (
+                (mixed / total)
+                .reshape(out_ref.shape[0], out_ref.shape[2], head_dim)
+                .astype(jnp.bfloat16)
+            )
+    for copy in copies:
+        copy.wait()
+
+
+def attend(weights, arrived, stale, devices, head_dim):
     layer_count, _, row_count, width = stale.shape
     whole = pl.BlockSpec(memory_space=pltpu.VMEM)
     return pl.pallas_call(
         partial(attend_kernel, head_dim),
-        in_specs=[pl.BlockSpec(memory_space=pltpu.SMEM), whole, whole],
-        out_specs=[whole, whole],
+        in_specs=[whole] * 3,
+        out_specs=[whole, pl.BlockSpec(memory_space=pl.ANY)],
         out_shape=[
-            jax.ShapeDtypeStruct((row_count, layer_count * width), jnp.bfloat16),
+            jax.ShapeDtypeStruct(
+                (devices, layer_count, row_count // devices, width), jnp.bfloat16
+            ),
             jax.ShapeDtypeStruct(stale.shape, jnp.bfloat16),
         ],
+        scratch_shapes=[
+            pltpu.VMEM(stale.shape, jnp.bfloat16),
+            pltpu.SemaphoreType.DMA((layer_count,)),
+        ],
         compiler_params=pltpu.CompilerParams(vmem_limit_bytes=VMEM_BYTES),
-    )(step_index, arrived, stale)
+    )(weights, arrived, stale)
 
 
 def whole_key_body(
@@ -141,18 +184,14 @@
     layer_count, token_count, channel_count = queries.shape
     head_dim = channel_count // block_exponents.shape[-1]
     width = channel_count // devices
-    packed = pack(
+    packed, weights = pack(
         step_index, queries, current_pairs, earlier_pairs, block_exponents, devices
     )
     arrived = exchange(packed.reshape(devices * token_count, -1))
     stale = stale_cache.reshape(layer_count, 2, devices * token_count, width)
-    partial_out, renewed = attend(step_index, arrived, stale, head_dim)
+    partial_out, renewed = attend(weights, arrived, stale, devices, head_dim)
     back = exchange(partial_out)
-    attended = (
-        back.reshape(devices, token_count, layer_count, width)
-        .transpose(2, 1, 0, 3)
-        .reshape(layer_count, token_count, channel_count)
-    )
+    attended = back.transpose(1, 2, 0, 3).reshape(layer_count, token_count, channel_count)
     return attended, renewed.reshape(stale_cache.shape)
 
 

time: 52.8 us -> 50.2 us (0.951)
  local copies, waits for them, and re-layouts: 5.2 us -> 0.78 us
  Pallas kernels: 2.49 us -> 4.19 us
    unnamed x10 -> x4, local copies, waits for them, and re-layouts: 4.06 us -> 0.01 us
    pallas_call x2, Pallas kernels: 2.49 us -> 4.19 us  [the longest x1 2.53 us: pack(): pl.pallas_call(pack_kernel, in_specs=[pl.BlockSpec(memory_space=pltpu.SME...]
    reshape x3 -> x1, local copies, waits for them, and re-layouts: 1.14 us -> 0.77 us  [whole_key_body(): back.transpose(1, 2, 0, 3).reshape(layer_count, token_count, channel_count)]
where the time goes in v2:
time: 50.2 us; the launch traced here: 50 us
  blocking collectives  43.7 us (87%)
  Pallas kernels  4.19 us (8%)
  between operations  1.31 us (3%)
  local copies, waits for them, and re-layouts  0.78 us (2%)
    all_to_all x2, blocking collectives, exchange(): lax.all_to_all(rows, 'patch', split_axis=0, concat_axis=0, tiled=True)  43.7 us
    pallas_call x1, Pallas kernels, pack(): pl.pallas_call(pack_kernel, in_specs=[pl.BlockSpec(memory_space=pltpu.SME...  2.53 us
    pallas_call x1, Pallas kernels, attend(): pl.pallas_call(partial(attend_kernel, head_dim), in_specs=[whole] * 3, ou...  1.66 us

profile of v2, /device:TPU:0, one launch (start us, length us, event | category | flops | bytes accessed | tf_op | source)
XLA Modules:
  0.0 50.0 jit_solution(10489709157254210709)
XLA Ops:
  1.3 2.5 %shard_map.77 = (bf16[16,24,1024]{2,1,0:T(8,128)(2,1)}, f32[2,8,128]{2,1,0:T(8,128)}) custom-call(s32[1]{0:T(128)S(6)} %copy.12.step_ref, bf16[2,24,4096]{2,1,0:T(8,128)(2,1)} %query_ref.1, bf16[2,2,24,4096]{3,2,1,0:T(8,128)(2,1)} %current_ref.1, bf16[2,2,24,4096]{3,2,1,0:T(8,128)(2,1)} %earlier_ref.1, s32[2,2,24,32]{3,2,1,0:T(8,128)} %exponent_ref.1), custom_call_target="tpu_custom_call" | custom-call | tf_op jit(solution)/shard_map/pallas_call | solution.py:95
  3.8 0.0 copy-start
  3.8 0.0 copy-start.1
  3.8 27.8 %all_to_all.13 = bf16[16,24,1024]{2,1,0:T(8,128)(2,1)S(1)} all-to-all(bf16[16,24,1024]{2,1,0:T(8,128)(2,1)} %get-tuple-element.7), channel_id=1, replica_groups=mesh['groups'=2,'patch'=16] {'patch'}, dimensions={0} | all-to-all | bytes 1572864 | tf_op jit(solution)/shard_map/all_to_all | solution.py:26
  31.6 0.0 copy-done
  31.6 0.0 copy-done.1
  31.6 1.7 %shard_map.78 = (bf16[16,2,24,256]{3,2,1,0:T(8,128)(2,1)S(1)}, bf16[2,2,384,256]{3,2,1,0:T(8,128)(2,1)}) custom-call(f32[2,8,128]{2,1,0:T(8,128)S(1)} %copy-done.1, bf16[384,1024]{1,0:T(8,128)(2,1)S(1)} %bitcast.8, bf16[2,2,384,256]{3,2,1,0:T(8,128)(2,1)S(1)} %bitcast.9), custom_call_target="tpu_custom_call" | custom-call | tf_op jit(solution)/shard_map/pallas_call | solution.py:162
  33.3 15.9 %all_to_all.14 = bf16[16,2,24,256]{3,2,1,0:T(8,128)(2,1)S(1)} all-to-all(bf16[16,2,24,256]{3,2,1,0:T(8,128)(2,1)S(1)} %get-tuple-element.8), channel_id=1, replica_groups=mesh['groups'=2,'patch'=16] {'patch'}, dimensions={0} | all-to-all | bytes 786432 | tf_op jit(solution)/shard_map/all_to_all | solution.py:26
  49.2 0.8 %copy.11 = bf16[16,2,3,8,256]{4,3,0,2,1:T(8,128)(2,1)} copy(bf16[16,2,3,8,256]{4,3,2,1,0:T(8,128)(2,1)S(1)} %bitcast.10) | data formatting | bytes 786432 | tf_op jit(solution)/shard_map/reshape | solution.py:194
Async XLA Ops:
  3.8 27.8 %copy-start = (bf16[2,2,1,16,24,256]{5,4,3,2,1,0:T(8,128)(2,1)S(1)}, bf16[2,2,1,16,24,256]{5,4,3,2,1,0:T(8,128)(2,1)}, u32[]{:S(2)}) copy-start(bf16[2,2,1,16,24,256]{5,4,3,2,1,0:T(8,128)(2,1)} %param.9) | copy-start | bytes 2359300
  3.8 27.8 %copy-start.1 = (f32[2,8,128]{2,1,0:T(8,128)S(1)}, f32[2,8,128]{2,1,0:T(8,128)}, u32[]{:S(2)}) copy-start(f32[2,8,128]{2,1,0:T(8,128)} %get-tuple-element.6.weight_ref) | copy-start | bytes 24580

commit v3 on v1

v3 whole, which is shorter than its diff:
```python
from functools import partial

import jax
import jax.numpy as jnp
from jax import lax
from jax.experimental import pallas as pl
from jax.experimental.pallas import tpu as pltpu
from jax.sharding import PartitionSpec as P

STEPS = 50
SATURATION = 448
TOP_LEVEL = 8
VMEM_BYTES = 40 * 1024 * 1024
PACK_BYTES = 60 * 1024 * 1024


def block_limits(exponents):
    return ((SATURATION << TOP_LEVEL) >> exponents).astype(jnp.float32) * (2.0**-TOP_LEVEL)


def blend_of(step):
    return 1.0 - step.astype(jnp.float32) / (2.0 * STEPS)


def layers_of(step):
    kept = lax.rem(step, 2)
    return kept, 1 - kept


def pairwise(array, distance, devices):
    pairs = [(device, device ^ distance) for device in range(devices)]
    return lax.ppermute(array, "patch", pairs)


def start_all(copies):
    for copy in copies:
        copy.start()
    return copies


def wait_all(copies):
    for copy in copies:
        copy.wait()


def pack_kernel(chips, step_ref, query_ref, current_ref, earlier_ref, exponent_ref, *refs):
    messages = refs[:chips]
    queries, current, earlier, exponents, packed, sems, out_sems = refs[chips:]
    _, _, channel_count = query_ref.shape
    head_count = exponent_ref.shape[-1]
    head_dim = channel_count // head_count
    width = channel_count // chips
    kept, refreshed = layers_of(step_ref[0])
    here = lax.div(lax.axis_index("patch"), 2)
    pairs = (
        (query_ref, queries),
        (current_ref.at[refreshed], current),
        (earlier_ref.at[refreshed], earlier),
        (exponent_ref.at[refreshed], exponents),
    )
    copies = start_all(
        [
            pltpu.make_async_copy(source, target, sems.at[index])
            for index, (source, target) in enumerate(pairs)
        ]
    )
    places = [lax.bitwise_xor(here, chip) for chip in range(chips)]
    copies[0].wait()
    for slot, layer in enumerate((kept, refreshed)):
        for chip in range(chips):
            packed[places[chip], :, slot * width : (slot + 1) * width] = queries[
                layer, :, chip * width : (chip + 1) * width
            ]
    wait_all(copies[1:])
    for side in range(2):
        limits = block_limits(exponents[side])
        first = (2 + side) * width
        for head in range(head_count):
            span = slice(head * head_dim, (head + 1) * head_dim)
            residual = current[side, :, span].astype(jnp.float32) - earlier[
                side, :, span
            ].astype(jnp.float32)
            limit = limits[:, head : head + 1]
            update = jnp.minimum(jnp.maximum(residual, -limit), limit).astype(jnp.bfloat16)
            chip, inner = divmod(head * head_dim, width)
            packed[places[chip], :, first + inner : first + inner + head_dim] = update
    wait_all(
        start_all(
            [
                pltpu.make_async_copy(packed.at[chip], messages[chip], out_sems.at[chip])
                for chip in range(chips)
            ]
        )
    )


def pack(step_index, queries, current_pairs, earlier_pairs, block_exponents, chips):
    _, token_count, channel_count = queries.shape
    columns = 4 * (channel_count // chips)
    far = pl.BlockSpec(memory_space=pl.ANY)
    layers = [current_pairs, earlier_pairs, block_exponents]
    return pl.pallas_call(
        partial(pack_kernel, chips),
        in_specs=[pl.BlockSpec(memory_space=pltpu.SMEM)] + [far] * 4,
        out_specs=[far] * chips,
        out_shape=[jax.ShapeDtypeStruct((token_count, columns), jnp.bfloat16)] * chips,
        scratch_shapes=[pltpu.VMEM(queries.shape, queries.dtype)]
        + [pltpu.VMEM(array.shape[1:], array.dtype) for array in layers]
        + [
            pltpu.VMEM((chips, token_count, columns), jnp.bfloat16),
            pltpu.SemaphoreType.DMA((4,)),
            pltpu.SemaphoreType.DMA((chips,)),
        ],
        compiler_params=pltpu.CompilerParams(vmem_limit_bytes=PACK_BYTES),
    )(step_index, queries, current_pairs, earlier_pairs, block_exponents)


def stacked(blocks):
    return jnp.concatenate([block.astype(jnp.float32) for block in blocks], 0).astype(
        jnp.bfloat16
    )


def answer(queries, keys, values, head_dim):
    spans = [
        slice(first, first + head_dim) for first in range(0, queries.shape[-1], head_dim)
    ]
    scores = [
        lax.dot_general(
            queries[:, span],
            keys[:, span],
            (((1,), (1,)), ((), ())),
            preferred_element_type=jnp.float32,
        )
        for span in spans
    ]
    weights = [
        jnp.exp((score - jnp.max(score, -1, keepdims=True)) * head_dim ** (-0.5))
        for score in scores
    ]
    return [
        jnp.dot(weight.astype(jnp.bfloat16), values[:, span], preferred_element_type=jnp.float32)
        / jnp.sum(weight, -1, keepdims=True)
        for weight, span in zip(weights, spans)
    ]


def kept_kernel(order, head_dim, step_ref, query_ref, *refs):
    messages = dict(zip([chip for chip in order if chip], refs))
    own_ref, other_ref, out_ref = refs[len(messages) :]
    width = own_ref.shape[-1]
    kept, _ = layers_of(step_ref[0])
    here, core = lax.div(lax.axis_index("patch"), 2), lax.rem(lax.axis_index("patch"), 2)
    for group, cache_ref in ((core, own_ref), (1 - core, other_ref)):
        first = pl.multiple_of(group * width, width)
        blocks = []
        for chip in order:
            if chip:
                blocks.append(messages[chip][:, pl.ds(first, width)])
            else:
                place = pl.multiple_of((2 * here + group) * width, width)
                blocks.append(query_ref[kept, :, pl.ds(place, width)])
        queries = stacked(blocks)
        keys, values = cache_ref[kept, 0], cache_ref[kept, 1]
        for head, result in enumerate(answer(queries, keys, values, head_dim)):
            place = pl.ds(pl.multiple_of(first + head * head_dim, head_dim), head_dim)
            out_ref[:, place] = result.astype(jnp.bfloat16)


def attend_kept(step_index, queries, arrived, order, stale, other_stale, head_dim):
    chips = len(order)
    messages = [arrived[chip] for chip in order if chip]
    _, token_count, channel_count = queries.shape
    whole = pl.BlockSpec(memory_space=pltpu.VMEM)
    return pl.pallas_call(
        partial(kept_kernel, order, head_dim),
        in_specs=[pl.BlockSpec(memory_space=pltpu.SMEM)] + [whole] * (chips + 2),
        out_specs=whole,
        out_shape=jax.ShapeDtypeStruct(
            (chips * token_count, channel_count // chips), jnp.bfloat16
        ),
        compiler_params=pltpu.CompilerParams(vmem_limit_bytes=VMEM_BYTES),
    )(step_index, queries, *messages, stale, other_stale)


def refreshed_kernel(order, head_dim, step_ref, *refs):
    chips = len(order)
    messages, relayed = refs[:chips], refs[chips : 2 * chips]
    kept_out, own_ref, other_ref = refs[2 * chips : 2 * chips + 3]
    answers = refs[2 * chips + 3 : 3 * chips + 3]
    renewed, updates = refs[3 * chips + 3 :]
    width = own_ref.shape[-1]
    token_count = messages[0].shape[0]
    step = step_ref[0]
    _, refreshed = layers_of(step)
    blend = blend_of(step)
    me = lax.axis_index("patch")
    core = lax.rem(me, 2)
    for slot, chip in enumerate(order):
        for source, message in ((2 * chip, messages[slot]), (2 * chip + 1, relayed[slot])):
            row = pl.multiple_of(lax.bitwise_xor(me, source) * token_count, 8)
            updates[pl.ds(row, token_count), :] = message[:, 4 * width :].astype(jnp.float32)
    results = []
    for turn, (group, cache_ref) in enumerate(((core, own_ref), (1 - core, other_ref))):
        pair = []
        for side in range(2):
            place = pl.ds(pl.multiple_of((2 * side + group) * width, width), width)
            rows = (
                cache_ref[refreshed, side].astype(jnp.float32)
                + blend * updates[:, place]
            ).astype(jnp.bfloat16)
            if turn == 0:
                renewed[side] = rows
            pair.append(rows)
        keys, values = pair
        first = pl.multiple_of(group * width, width)
        queries = stacked(
            [message[:, pl.ds(pl.multiple_of(2 * width + first, width), width)] for message in messages]
        )
        for head, result in enumerate(answer(queries, keys, values, head_dim)):
            place = pl.ds(
                pl.multiple_of(2 * width + first + head * head_dim, head_dim), head_dim
            )
            for slot in range(chips):
                answers[slot][:, place] = result[
                    slot * token_count : (slot + 1) * token_count
                ].astype(jnp.bfloat16)
    earlier = kept_out[...].astype(jnp.float32)
    for slot in range(chips):
        answers[slot][:, : 2 * width] = earlier[
            slot * token_count : (slot + 1) * token_count
        ].astype(jnp.bfloat16)


def attend_refreshed(
    step_index, messages, relayed, order, kept_out, stale, other_stale, head_dim
):
    chips = len(messages)
    token_count, columns = messages[0].shape
    whole = pl.BlockSpec(memory_space=pltpu.VMEM)
    *answers, renewed = pl.pallas_call(
        partial(refreshed_kernel, order, head_dim),
        in_specs=[pl.BlockSpec(memory_space=pltpu.SMEM)] + [whole] * (2 * chips + 3),
        out_specs=[whole] * (chips + 1),
        out_shape=[jax.ShapeDtypeStruct((token_count, columns // 2), jnp.bfloat16)] * chips
        + [jax.ShapeDtypeStruct(stale.shape[1:], jnp.bfloat16)],
        scratch_shapes=[pltpu.VMEM((stale.shape[2], columns // 2), jnp.float32)],
        compiler_params=pltpu.CompilerParams(vmem_limit_bytes=VMEM_BYTES),
    )(step_index, *messages, *relayed, kept_out, stale, other_stale)
    return answers, renewed


def store_kernel(step_ref, stale_ref, renewed_ref, out_ref, sems):
    kept, refreshed = layers_of(step_ref[0])
    wait_all(
        start_all(
            [
                pltpu.make_async_copy(stale_ref.at[kept], out_ref.at[kept], sems.at[0]),
                pltpu.make_async_copy(renewed_ref, out_ref.at[refreshed], sems.at[1]),
            ]
        )
    )


def store(step_index, stale, renewed):
    far = pl.BlockSpec(memory_space=pl.ANY)
    return pl.pallas_call(
        store_kernel,
        in_specs=[pl.BlockSpec(memory_space=pltpu.SMEM)]
        + [pl.BlockSpec(memory_space=pltpu.VMEM)] * 2,
        out_specs=far,
        out_shape=jax.ShapeDtypeStruct(stale.shape, stale.dtype),
        scratch_shapes=[pltpu.SemaphoreType.DMA((2,))],
        compiler_params=pltpu.CompilerParams(vmem_limit_bytes=VMEM_BYTES),
    )(step_index, stale, renewed)


def after(array, *others):
    return lax.optimization_barrier((array, *others))[0]


def place_kernel(order, step_ref, *refs):
    chips = len(order)
    answers = refs[:chips]
    out_ref, placed, sem = refs[chips:]
    width = answers[0].shape[-1] // 2
    here = lax.div(lax.axis_index("patch"), 2)
    for slot, chip in enumerate(order):
        first = pl.multiple_of(lax.bitwise_xor(here, chip) * width, width)
        for half, layer in enumerate(layers_of(step_ref[0])):
            placed[layer, :, pl.ds(first, width)] = answers[slot][
                :, half * width : (half + 1) * width
            ]
    copy = pltpu.make_async_copy(placed, out_ref, sem)
    copy.start()
    copy.wait()


def place(step_index, answers, order):
    token_count, columns = answers[0].shape
    attended = jax.ShapeDtypeStruct((2, token_count, len(order) * columns // 2), jnp.bfloat16)
    return pl.pallas_call(
        partial(place_kernel, order),
        in_specs=[pl.BlockSpec(memory_space=pltpu.SMEM)]
        + [pl.BlockSpec(memory_space=pltpu.VMEM)] * len(order),
        out_specs=pl.BlockSpec(memory_space=pl.ANY),
        out_shape=attended,
        scratch_shapes=[
            pltpu.VMEM(attended.shape, attended.dtype),
            pltpu.SemaphoreType.DMA(()),
        ],
        compiler_params=pltpu.CompilerParams(vmem_limit_bytes=VMEM_BYTES),
    )(step_index, *answers)


def distances(chips):
    if chips == 8:
        return [5, 1, 3, 6, 4, 2, 7, 0], [7, 6, 5, 2, 4, 3, 1, 0]
    order = list(range(chips - 1, -1, -1))
    return order, order


def whole_key_body(
    queries, current_pairs, earlier_pairs, stale_cache, block_exponents, step_index
):
    devices = lax.axis_size("patch")
    chips = devices // 2
    layer_count, token_count, channel_count = queries.shape
    head_dim = channel_count // block_exponents.shape[-1]
    stale = stale_cache.reshape(layer_count, 2, devices * token_count, -1)
    other_stale = pairwise(stale, 1, devices)
    messages = pack(
        step_index, queries, current_pairs, earlier_pairs, block_exponents, chips
    )
    *messages, other_stale = lax.optimization_barrier((*messages, other_stale))
    order, back_order = distances(chips)
    arrived = {
        chip: pairwise(messages[chip], 2 * chip, devices) for chip in order if chip
    }
    arrived[0] = messages[0]
    kept_out = attend_kept(
        step_index, queries, arrived, order, stale, other_stale, head_dim
    )
    arrived = [arrived[chip] for chip in order]
    relayed = [pairwise(message, 1, devices) for message in arrived]
    answers, renewed = attend_refreshed(
        step_index, arrived, relayed, order, kept_out, stale, other_stale, head_dim
    )
    by_chip = [answers[order.index(chip)] for chip in range(chips)]
    returned = [
        pairwise(by_chip[chip], 2 * chip, devices) if chip else by_chip[0] for chip in back_order
    ]
    renewed = store(step_index, stale, after(renewed, returned[0]))
    attended = place(step_index, returned, back_order)
    return attended, renewed.reshape(stale_cache.shape)


def exchange(rows):
    return lax.all_to_all(rows, "patch", split_axis=0, concat_axis=0, tiled=True)


def answer_part(blocks, key_rows, value_rows):
    score_scale = key_rows.shape[-1] ** (-0.5)

    def one_block(query_block):
        scores = (
            jnp.einsum("qhd,khd->hqk", query_block, key_rows, preferred_element_type=jnp.float32)
            * score_scale
        )
        peak = jnp.max(scores, -1, keepdims=True)
        weights = jnp.exp(scores - peak)
        total = jnp.sum(weights, -1)
        mixed = jnp.einsum(
            "hqk,khd->qhd",
            weights.astype(jnp.bfloat16),
            value_rows,
            preferred_element_type=jnp.float32,
        )
        return mixed / total.T[..., None], (peak[..., 0] + jnp.log(total)).T

    return lax.map(one_block, blocks)


def split_key_body(
    queries, current_pairs, earlier_pairs, stale_cache, block_exponents, step_index
):
    devices = lax.axis_size("patch")
    layer_count, token_count, channel_count = queries.shape
    head_count = block_exponents.shape[-1]
    head_dim = channel_count // head_count
    group_count = min(head_count, devices)
    part_count = devices // group_count
    group_heads = head_count // group_count
    part_rows = token_count // part_count
    width = group_heads * head_dim
    selector = step_index[0] % 2
    blend = blend_of(step_index[0])
    limits = block_limits(block_exponents)[..., None]
    residual = (current_pairs.astype(jnp.float32) - earlier_pairs.astype(jnp.float32)).reshape(
        layer_count, 2, token_count, head_count, head_dim
    )
    update = jnp.clip(residual, -limits, limits).astype(jnp.bfloat16)
    pieces = update.reshape(layer_count, 2, part_count, part_rows, group_count, width)
    pieces = pieces.transpose(0, 4, 2, 1, 3, 5).reshape(
        layer_count, devices, 2 * part_rows, width
    )
    asked = queries.reshape(layer_count, token_count, group_count, 1, width)
    asked = jnp.broadcast_to(
        asked.transpose(0, 2, 3, 1, 4),
        (layer_count, group_count, part_count, token_count, width),
    ).reshape(layer_count, devices, token_count, width)
    attended_list = []
    renewed_list = []
    for layer in range(layer_count):
        refresh = selector != layer % 2
        outgoing = jnp.where(refresh, pieces[layer], jnp.zeros_like(pieces[layer]))
        arrived = exchange(jnp.concatenate([outgoing, asked[layer]], 1))
        arrived_update = arrived[:, : 2 * part_rows].reshape(devices, 2, part_rows, width)
        renewed = (
            stale_cache[layer, :, 0].astype(jnp.float32)
            + blend * arrived_update.transpose(1, 0, 2, 3).astype(jnp.float32)
        ).astype(jnp.bfloat16)
        key_rows = renewed[0].reshape(devices * part_rows, group_heads, head_dim)
        value_rows = renewed[1].reshape(devices * part_rows, group_heads, head_dim)
        block_span = 1
        while (
            block_span * token_count < 512 and devices % (2 * block_span) == 0
        ):
            block_span = block_span * 2
        blocks = arrived[:, 2 * part_rows :].reshape(
            devices // block_span, block_span * token_count, group_heads, head_dim
        )
        partial_out, log_total = answer_part(blocks, key_rows, value_rows)
        back_out = exchange(
            partial_out.astype(jnp.bfloat16).reshape(devices, token_count, width)
        ).astype(jnp.float32)
        back_log = exchange(
            log_total.astype(jnp.bfloat16).reshape(devices, token_count, group_heads)
        ).astype(jnp.float32)
        back_out = back_out.reshape(group_count, part_count, token_count, group_heads, head_dim)
        back_log = back_log.reshape(group_count, part_count, token_count, group_heads)
        factor = jnp.exp(back_log - jnp.max(back_log, 1, keepdims=True))
        merged = jnp.sum(factor[..., None] * back_out, 1) / jnp.sum(factor, 1)[..., None]
        attended_list.append(
            merged.transpose(1, 0, 2, 3)
            .reshape(token_count, channel_count)
            .astype(jnp.bfloat16)
        )
        renewed_list.append(renewed)
    return jnp.stack(attended_list), jnp.stack(renewed_list)[:, :, None]


def body(queries, current_pairs, earlier_pairs, stale_cache, block_exponents, step_index):
    layer_count = queries.shape[0]
    head_count = block_exponents.shape[-1]
    devices = lax.axis_size("patch")
    one_part = 1 < devices <= head_count and devices & (devices - 1) == 0 and layer_count == 2
    chosen = whole_key_body if one_part else split_key_body
    return chosen(
        queries, current_pairs, earlier_pairs, stale_cache, block_exponents, step_index
    )


def solution(mesh):
    in_specs = (
        P(None, ("groups", "patch"), None),
        P(None, None, ("groups", "patch"), None),
        P(None, None, ("groups", "patch"), None),
        P(None, None, ("groups", "patch"), None, None, None),
        P(None, None, ("groups", "patch"), None),
        P("groups"),
    )
    out_specs = (
        P(None, ("groups", "patch"), None),
        P(None, None, ("groups", "patch"), None, None, None),
    )
    return jax.shard_map(body, mesh=mesh, in_specs=in_specs, out_specs=out_specs, check_vma=False)
```

time: 52.8 us -> 45.3 us (0.86)
  blocking collectives: 43.5 us -> 0 us
  starting transfers between devices: 0 us -> 27.4 us
  waiting for transfers between devices: 0 us -> 10.2 us
  local copies, waits for them, and re-layouts: 5.2 us -> 0.01 us
  Pallas kernels: 2.49 us -> 6.18 us
    all_to_all x2 -> x0, blocking collectives: 43.5 us -> none  [exchange(): lax.all_to_all(rows, 'patch', split_axis=0, concat_axis=0, tiled=True)]
    ppermute x0 -> x23, starting transfers between devices: none -> 27.4 us  [pairwise(): return lax.ppermute(array, 'patch', pairs)]
    ppermute x0 -> x23, waiting for transfers between devices: none -> 10.2 us  [pairwise(): return lax.ppermute(array, 'patch', pairs)]
    unnamed x10 -> x6, local copies, waits for them, and re-layouts: 4.06 us -> 0.01 us
    pallas_call x2 -> x5, Pallas kernels: 2.49 us -> 6.18 us  [the longest x1 2.69 us: pack(): pl.pallas_call(partial(pack_kernel, chips), in_specs=[pl.BlockSpec(memory...]
    reshape x3 -> x0, local copies, waits for them, and re-layouts: 1.14 us -> none  [the longest x1 0.93 us: whole_key_body(): attended = back.reshape(devices, token_count, layer_count, width).transpo...]
  transfers between devices with their start and end apart: 0 -> 23, of which waited for: 0 -> 9; matrix products, arithmetic and copies ran while one was open for 0% -> 0% of each run, Pallas kernels for 0% -> 10%
where the time goes in v3:
time: 45.3 us; the launch traced here: 45.2 us
  starting transfers between devices  27.4 us (60%)
  waiting for transfers between devices  10.2 us (23%)
  Pallas kernels  6.18 us (14%)
  between operations  1.4 us (3%)
    ppermute x23, starting transfers between devices, pairwise(): return lax.ppermute(array, 'patch', pairs)  27.4 us
    ppermute x23, waiting for transfers between devices, pairwise(): return lax.ppermute(array, 'patch', pairs)  10.2 us
    pallas_call x1, Pallas kernels, pack(): pl.pallas_call(partial(pack_kernel, chips), in_specs=[pl.BlockSpec(memory...  2.69 us
    pallas_call x1, Pallas kernels, attend_refreshed(): pl.pallas_call(partial(refreshed_kernel, order, head_dim), in_specs=[pl.B...  0.99 us
  transfers between devices with their start and end apart: 23, of which 9 were waited for; matrix products, arithmetic and copies ran while one was open for 0% of the time, Pallas kernels for 10%

profile of v3, /device:TPU:0, one launch (start us, length us, event | category | flops | bytes accessed | tf_op | source)
XLA Modules:
  0.0 45.2 jit_solution(17887831670153980983)
XLA Ops:
  0.6 0.5 %collective-permute-start = (bf16[2,2,384,256]{3,2,1,0:T(8,128)(2,1)}, bf16[2,2,384,256]{3,2,1,0:T(8,128)(2,1)S(1)}, u32[]{:S(2)}, u32[]{:S(2)}) collective-permute-start(bf16[2,2,384,256]{3,2,1,0:T(8,128)(2,1)} %bitcast.4), channel_id=1, source_target_pairs={{0,1},{1,0},{2,3},{3,2},{4,5},{5,4},{6,7},{7,6},{8,9},{9,8},{10,11... | collective-permute-start | bytes 2359304 | tf_op jit(solution)/shard_map/ppermute | solution.py:32
  1.8 2.7 %shard_map.77 = (bf16[24,2048]{1,0:T(8,128)(2,1)}, bf16[24,2048]{1,0:T(8,128)(2,1)}, bf16[24,2048]{1,0:T(8,128)(2,1)}, bf16[24,2048]{1,0:T(8,128)(2,1)}, bf16[24...) custom-call(s32[1]{0:T(128)S(6)} %copy.9.step_ref, ...), custom_call_target="tpu_custom_call" | custom-call | tf_op jit(solution)/shard_map/pallas_call | solution.py:102
  4.5 4.6 %collective-permute-start.1 = (bf16[24,2048]{1,0:T(8,128)(2,1)}, bf16[24,2048]{1,0:T(8,128)(2,1)S(1)}, u32[]{:S(2)}, u32[]{:S(2)}) collective-permute-start(bf16[24,2048]{1,0:T(8,128)(2,1)} %get-tuple-element.37), channel_id=1, source_target_pairs={{0,10},{1,11},{2,8},{3,9},{4,14},{5,15},{6,12},{7,13},{8,2},{9,3},... | collective-permute-start | bytes 294920 | tf_op jit(solution)/shard_map/ppermute | solution.py:32
  9.1 0.5 %collective-permute-start.2 = (bf16[24,2048]{1,0:T(8,128)(2,1)}, bf16[24,2048]{1,0:T(8,128)(2,1)S(1)}, u32[]{:S(2)}, u32[]{:S(2)}) collective-permute-start(bf16[24,2048]{1,0:T(8,128)(2,1)} %get-tuple-element.38), channel_id=1, source_target_pairs={{0,2},{1,3},{2,0},{3,1},{4,6},{5,7},{6,4},{7,5},{8,10},{9,11},{10,... | collective-permute-start | bytes 294920 | tf_op jit(solution)/shard_map/ppermute | solution.py:32
  9.7 2.5 %collective-permute-start.3 = (bf16[24,2048]{1,0:T(8,128)(2,1)}, bf16[24,2048]{1,0:T(8,128)(2,1)S(1)}, u32[]{:S(2)}, u32[]{:S(2)}) collective-permute-start(bf16[24,2048]{1,0:T(8,128)(2,1)} %get-tuple-element.39), channel_id=1, source_target_pairs={{0,6},{1,7},{2,4},{3,5},{4,2},{5,3},{6,0},{7,1},{8,14},{9,15},{10,... | collective-permute-start | bytes 294920 | tf_op jit(solution)/shard_map/ppermute | solution.py:32
  12.4 1.7 %collective-permute-start.5 = (bf16[24,2048]{1,0:T(8,128)(2,1)}, bf16[24,2048]{1,0:T(8,128)(2,1)S(1)}, u32[]{:S(2)}, u32[]{:S(2)}) collective-permute-start(bf16[24,2048]{1,0:T(8,128)(2,1)} %get-tuple-element.41), channel_id=1, source_target_pairs={{0,8},{1,9},{2,10},{3,11},{4,12},{5,13},{6,14},{7,15},{8,0},{9,1},... | collective-permute-start | bytes 294920 | tf_op jit(solution)/shard_map/ppermute | solution.py:32
  14.1 1.1 %collective-permute-done.1.refs_0_ = bf16[24,2048]{1,0:T(8,128)(2,1)S(1)} collective-permute-done((bf16[24,2048]{1,0:T(8,128)(2,1)}, bf16[24,2048]{1,0:T(8,128)(2,1)S(1)}, u32[]{:S(2)}, u32[]{:S(2)}) %collective-permute-start.1) | collective-permute-done | bytes 98336 | tf_op jit(solution)/shard_map/ppermute | solution.py:32
  15.1 1.4 %collective-permute-start.6 = (bf16[24,2048]{1,0:T(8,128)(2,1)}, bf16[24,2048]{1,0:T(8,128)(2,1)S(1)}, u32[]{:S(2)}, u32[]{:S(2)}) collective-permute-start(bf16[24,2048]{1,0:T(8,128)(2,1)} %get-tuple-element.42), channel_id=1, source_target_pairs={{0,4},{1,5},{2,6},{3,7},{4,0},{5,1},{6,2},{7,3},{8,12},{9,13},{10,... | collective-permute-start | bytes 294920 | tf_op jit(solution)/shard_map/ppermute | solution.py:32
  16.6 0.8 %collective-permute-done.2.refs_1_ = bf16[24,2048]{1,0:T(8,128)(2,1)S(1)} collective-permute-done((bf16[24,2048]{1,0:T(8,128)(2,1)}, bf16[24,2048]{1,0:T(8,128)(2,1)S(1)}, u32[]{:S(2)}, u32[]{:S(2)}) %collective-permute-start.2) | collective-permute-done | bytes 98336 | tf_op jit(solution)/shard_map/ppermute | solution.py:32
  17.3 2.8 %collective-permute-start.7 = (bf16[24,2048]{1,0:T(8,128)(2,1)}, bf16[24,2048]{1,0:T(8,128)(2,1)S(1)}, u32[]{:S(2)}, u32[]{:S(2)}) collective-permute-start(bf16[24,2048]{1,0:T(8,128)(2,1)} %get-tuple-element.43), channel_id=1, source_target_pairs={{0,14},{1,15},{2,12},{3,13},{4,10},{5,11},{6,8},{7,9},{8,6},{9,7},... | collective-permute-start | bytes 294920 | tf_op jit(solution)/shard_map/ppermute | solution.py:32
  20.7 5.7 %collective-permute-done.5.refs_4_ = bf16[24,2048]{1,0:T(8,128)(2,1)S(1)} collective-permute-done((bf16[24,2048]{1,0:T(8,128)(2,1)}, bf16[24,2048]{1,0:T(8,128)(2,1)S(1)}, u32[]{:S(2)}, u32[]{:S(2)}) %collective-permute-start.5) | collective-permute-done | bytes 98336 | tf_op jit(solution)/shard_map/ppermute | solution.py:32
  26.4 0.5 %collective-permute-start.10 = (bf16[24,2048]{1,0:T(8,128)(2,1)S(1)}, bf16[24,2048]{1,0:T(8,128)(2,1)S(1)}, u32[]{:S(2)}, u32[]{:S(2)}) collective-permute-start(bf16[24,2048]{1,0:T(8,128)(2,1)S(1)} %collective-permute-done.3.refs_2_), channel_id=1, source_target_pairs={{0,1},{1,0},{2,3},{3,2},{4,5},{5,4},{6,7},{7,6},{8,9},{9,8},{10,11... | collective-permute-start | bytes 294920 | tf_op jit(solution)/shard_map/ppermute | solution.py:32
  28.0 0.8 %shard_map.78.refs_16_ = bf16[192,512]{1,0:T(8,128)(2,1)S(1)} custom-call(s32[1]{0:T(128)S(6)} %copy.9.step_ref, bf16[2,24,4096]{2,1,0:T(8,128)(2,1)S(1)} %copy-done.1, bf16[24,2048]{1,0:T(8,128)(2,1)S(1)} %collective-permute-done.1.refs_0_, bf16[24,2048]{1,0:T(8,128)(2,1)S(1)} %collective-permute-done.2.refs_1_, ...), custom_call_target="tpu_custom_call" | custom-call | tf_op jit(solution)/shard_map/pallas_call | solution.py:175
  29.0 1.0 %shard_map.79 = (bf16[24,1024]{1,0:T(8,128)(2,1)S(1)}, bf16[24,1024]{1,0:T(8,128)(2,1)S(1)}, bf16[24,1024]{1,0:T(8,128)(2,1)S(1)}, bf16[24,1024]{1,0:T(8,128)(2,...) custom-call(s32[1]{0:T(128)S(6)} %copy.9.step_ref, ...), custom_call_target="tpu_custom_call" | custom-call | tf_op jit(solution)/shard_map/pallas_call | solution.py:241
  30.0 2.7 %collective-permute-start.16 = (bf16[24,1024]{1,0:T(8,128)(2,1)S(1)}, bf16[24,1024]{1,0:T(8,128)(2,1)S(1)}, u32[]{:S(2)}, u32[]{:S(2)}) collective-permute-start(bf16[24,1024]{1,0:T(8,128)(2,1)S(1)} %get-tuple-element.46), channel_id=1, source_target_pairs={{0,14},{1,15},{2,12},{3,13},{4,10},{5,11},{6,8},{7,9},{8,6},{9,7},... | collective-permute-start | bytes 147464 | tf_op jit(solution)/shard_map/ppermute | solution.py:32
  32.7 1.2 %collective-permute-start.17 = (bf16[24,1024]{1,0:T(8,128)(2,1)S(1)}, bf16[24,1024]{1,0:T(8,128)(2,1)S(1)}, u32[]{:S(2)}, u32[]{:S(2)}) collective-permute-start(bf16[24,1024]{1,0:T(8,128)(2,1)S(1)} %get-tuple-element.47), channel_id=1, source_target_pairs={{0,12},{1,13},{2,14},{3,15},{4,8},{5,9},{6,10},{7,11},{8,4},{9,5},... | collective-permute-start | bytes 147464 | tf_op jit(solution)/shard_map/ppermute | solution.py:32
  33.9 2.3 %collective-permute-start.18 = (bf16[24,1024]{1,0:T(8,128)(2,1)S(1)}, bf16[24,1024]{1,0:T(8,128)(2,1)S(1)}, u32[]{:S(2)}, u32[]{:S(2)}) collective-permute-start(bf16[24,1024]{1,0:T(8,128)(2,1)S(1)} %get-tuple-element.48), channel_id=1, source_target_pairs={{0,10},{1,11},{2,8},{3,9},{4,14},{5,15},{6,12},{7,13},{8,2},{9,3},... | collective-permute-start | bytes 147464 | tf_op jit(solution)/shard_map/ppermute | solution.py:32
  36.2 1.8 %collective-permute-start.19 = (bf16[24,1024]{1,0:T(8,128)(2,1)S(1)}, bf16[24,1024]{1,0:T(8,128)(2,1)S(1)}, u32[]{:S(2)}, u32[]{:S(2)}) collective-permute-start(bf16[24,1024]{1,0:T(8,128)(2,1)S(1)} %get-tuple-element.49), channel_id=1, source_target_pairs={{0,4},{1,5},{2,6},{3,7},{4,0},{5,1},{6,2},{7,3},{8,12},{9,13},{10,... | collective-permute-start | bytes 147464 | tf_op jit(solution)/shard_map/ppermute | solution.py:32
  38.0 1.7 %collective-permute-start.21 = (bf16[24,1024]{1,0:T(8,128)(2,1)S(1)}, bf16[24,1024]{1,0:T(8,128)(2,1)S(1)}, u32[]{:S(2)}, u32[]{:S(2)}) collective-permute-start(bf16[24,1024]{1,0:T(8,128)(2,1)S(1)} %get-tuple-element.51), channel_id=1, source_target_pairs={{0,6},{1,7},{2,4},{3,5},{4,2},{5,3},{6,0},{7,1},{8,14},{9,15},{10,... | collective-permute-start | bytes 147464 | tf_op jit(solution)/shard_map/ppermute | solution.py:32
  39.7 1.5 %collective-permute-start.22 = (bf16[24,1024]{1,0:T(8,128)(2,1)S(1)}, bf16[24,1024]{1,0:T(8,128)(2,1)S(1)}, u32[]{:S(2)}, u32[]{:S(2)}) collective-permute-start(bf16[24,1024]{1,0:T(8,128)(2,1)S(1)} %get-tuple-element.52), channel_id=1, source_target_pairs={{0,2},{1,3},{2,0},{3,1},{4,6},{5,7},{6,4},{7,5},{8,10},{9,11},{10,... | collective-permute-start | bytes 147464 | tf_op jit(solution)/shard_map/ppermute | solution.py:32
  41.2 0.9 %shard_map.81 = bf16[2,2,384,256]{3,2,1,0:T(8,128)(2,1)} custom-call(s32[1]{0:T(128)S(6)} %copy.9.step_ref, bf16[2,2,384,256]{3,2,1,0:T(8,128)(2,1)S(1)} %bitcast.7, bf16[2,384,256]{2,1,0:T(8,128)(2,1)S(1)} %get-tuple-element.55.renewed_ref), custom_call_target="tpu_custom_call" | custom-call | tf_op jit(solution)/shard_map/pallas_call | solution.py:267
  42.6 0.6 %collective-permute-done.20.refs_4_ = bf16[24,1024]{1,0:T(8,128)(2,1)S(1)} collective-permute-done((bf16[24,1024]{1,0:T(8,128)(2,1)S(1)}, bf16[24,1024]{1,0:T(8,128)(2,1)S(1)}, u32[]{:S(2)}, u32[]{:S(2)}) %collective-permute-start.20) | collective-permute-done | bytes 49184 | tf_op jit(solution)/shard_map/ppermute | solution.py:32
  43.2 1.0 %collective-permute-done.21.refs_5_ = bf16[24,1024]{1,0:T(8,128)(2,1)S(1)} collective-permute-done((bf16[24,1024]{1,0:T(8,128)(2,1)S(1)}, bf16[24,1024]{1,0:T(8,128)(2,1)S(1)}, u32[]{:S(2)}, u32[]{:S(2)}) %collective-permute-start.21) | collective-permute-done | bytes 49184 | tf_op jit(solution)/shard_map/ppermute | solution.py:32
  44.4 0.8 %shard_map.80 = bf16[2,24,4096]{2,1,0:T(8,128)(2,1)} custom-call(s32[1]{0:T(128)S(6)} %copy.9.step_ref, bf16[24,1024]{1,0:T(8,128)(2,1)S(1)} %collective-permute-done.16.refs_0_, bf16[24,1024]{1,0:T(8,128)(2,1)S(1)} %collective-permute-done.17.refs_1_, bf16[24,1024]{1,0:T(8,128)(2,1)S(1)} %collective-permute-done.18.refs_2_, ...), custom_call_target="tpu_custom_call" | custom-call | tf_op jit(solution)/shard_map/pallas_call | solution.py:302
  (33 shorter events, 2.7 us)
Async XLA Ops:
  0.6 3.9 %collective-permute-start = (bf16[2,2,384,256]{3,2,1,0:T(8,128)(2,1)}, bf16[2,2,384,256]{3,2,1,0:T(8,128)(2,1)S(1)}, u32[]{:S(2)}, u32[]{:S(2)}) collective-permute-start(bf16[2,2,384,256]{3,2,1,0:T(8,128)(2,1)} %bitcast.4), channel_id=1, source_target_pairs={{0,1},{1,0},{2,3},{3,2},{4,5},{5,4},{6,7},{7,6},{8,9},{9,8},{10,11... | collective-permute-start | bytes 2359304 | tf_op jit(solution)/shard_map/ppermute | solution.py:32
  1.8 26.2 %copy-start = (bf16[2,2,1,16,24,256]{5,4,3,2,1,0:T(8,128)(2,1)S(1)}, bf16[2,2,1,16,24,256]{5,4,3,2,1,0:T(8,128)(2,1)}, u32[]{:S(2)}) copy-start(bf16[2,2,1,16,24,256]{5,4,3,2,1,0:T(8,128)(2,1)} %param.9) | copy-start | bytes 2359300
  4.5 10.6 %collective-permute-start.1 = (bf16[24,2048]{1,0:T(8,128)(2,1)}, bf16[24,2048]{1,0:T(8,128)(2,1)S(1)}, u32[]{:S(2)}, u32[]{:S(2)}) collective-permute-start(bf16[24,2048]{1,0:T(8,128)(2,1)} %get-tuple-element.37), channel_id=1, source_target_pairs={{0,10},{1,11},{2,8},{3,9},{4,14},{5,15},{6,12},{7,13},{8,2},{9,3},... | collective-permute-start | bytes 294920 | tf_op jit(solution)/shard_map/ppermute | solution.py:32
  9.1 8.2 %collective-permute-start.2 = (bf16[24,2048]{1,0:T(8,128)(2,1)}, bf16[24,2048]{1,0:T(8,128)(2,1)S(1)}, u32[]{:S(2)}, u32[]{:S(2)}) collective-permute-start(bf16[24,2048]{1,0:T(8,128)(2,1)} %get-tuple-element.38), channel_id=1, source_target_pairs={{0,2},{1,3},{2,0},{3,1},{4,6},{5,7},{6,4},{7,5},{8,10},{9,11},{10,... | collective-permute-start | bytes 294920 | tf_op jit(solution)/shard_map/ppermute | solution.py:32
  9.7 10.5 %collective-permute-start.3 = (bf16[24,2048]{1,0:T(8,128)(2,1)}, bf16[24,2048]{1,0:T(8,128)(2,1)S(1)}, u32[]{:S(2)}, u32[]{:S(2)}) collective-permute-start(bf16[24,2048]{1,0:T(8,128)(2,1)} %get-tuple-element.39), channel_id=1, source_target_pairs={{0,6},{1,7},{2,4},{3,5},{4,2},{5,3},{6,0},{7,1},{8,14},{9,15},{10,... | collective-permute-start | bytes 294920 | tf_op jit(solution)/shard_map/ppermute | solution.py:32
  12.2 8.0 %collective-permute-start.4 = (bf16[24,2048]{1,0:T(8,128)(2,1)}, bf16[24,2048]{1,0:T(8,128)(2,1)S(1)}, u32[]{:S(2)}, u32[]{:S(2)}) collective-permute-start(bf16[24,2048]{1,0:T(8,128)(2,1)} %get-tuple-element.40), channel_id=1, source_target_pairs={{0,12},{1,13},{2,14},{3,15},{4,8},{5,9},{6,10},{7,11},{8,4},{9,5},... | collective-permute-start | bytes 294920 | tf_op jit(solution)/shard_map/ppermute | solution.py:32
  12.4 14.0 %collective-permute-start.5 = (bf16[24,2048]{1,0:T(8,128)(2,1)}, bf16[24,2048]{1,0:T(8,128)(2,1)S(1)}, u32[]{:S(2)}, u32[]{:S(2)}) collective-permute-start(bf16[24,2048]{1,0:T(8,128)(2,1)} %get-tuple-element.41), channel_id=1, source_target_pairs={{0,8},{1,9},{2,10},{3,11},{4,12},{5,13},{6,14},{7,15},{8,0},{9,1},... | collective-permute-start | bytes 294920 | tf_op jit(solution)/shard_map/ppermute | solution.py:32
  15.1 11.3 %collective-permute-start.6 = (bf16[24,2048]{1,0:T(8,128)(2,1)}, bf16[24,2048]{1,0:T(8,128)(2,1)S(1)}, u32[]{:S(2)}, u32[]{:S(2)}) collective-permute-start(bf16[24,2048]{1,0:T(8,128)(2,1)} %get-tuple-element.42), channel_id=1, source_target_pairs={{0,4},{1,5},{2,6},{3,7},{4,0},{5,1},{6,2},{7,3},{8,12},{9,13},{10,... | collective-permute-start | bytes 294920 | tf_op jit(solution)/shard_map/ppermute | solution.py:32
  17.3 9.6 %collective-permute-start.7 = (bf16[24,2048]{1,0:T(8,128)(2,1)}, bf16[24,2048]{1,0:T(8,128)(2,1)S(1)}, u32[]{:S(2)}, u32[]{:S(2)}) collective-permute-start(bf16[24,2048]{1,0:T(8,128)(2,1)} %get-tuple-element.43), channel_id=1, source_target_pairs={{0,14},{1,15},{2,12},{3,13},{4,10},{5,11},{6,8},{7,9},{8,6},{9,7},... | collective-permute-start | bytes 294920 | tf_op jit(solution)/shard_map/ppermute | solution.py:32
  20.2 6.8 %collective-permute-start.15 = (bf16[24,2048]{1,0:T(8,128)(2,1)}, bf16[24,2048]{1,0:T(8,128)(2,1)S(1)}, u32[]{:S(2)}, u32[]{:S(2)}) collective-permute-start(bf16[24,2048]{1,0:T(8,128)(2,1)} %get-tuple-element.44.refs_7_), channel_id=1, source_target_pairs={{0,1},{1,0},{2,3},{3,2},{4,5},{5,4},{6,7},{7,6},{8,9},{9,8},{10,11... | collective-permute-start | bytes 294920 | tf_op jit(solution)/shard_map/ppermute | solution.py:32
  20.2 7.3 %collective-permute-start.8 = (bf16[24,2048]{1,0:T(8,128)(2,1)S(1)}, bf16[24,2048]{1,0:T(8,128)(2,1)S(1)}, u32[]{:S(2)}, u32[]{:S(2)}) collective-permute-start(bf16[24,2048]{1,0:T(8,128)(2,1)S(1)} %collective-permute-done.1.refs_0_), channel_id=1, source_target_pairs={{0,1},{1,0},{2,3},{3,2},{4,5},{5,4},{6,7},{7,6},{8,9},{9,8},{10,11... | collective-permute-start | bytes 294920 | tf_op jit(solution)/shard_map/ppermute | solution.py:32
  26.4 1.3 %collective-permute-start.9 = (bf16[24,2048]{1,0:T(8,128)(2,1)S(1)}, bf16[24,2048]{1,0:T(8,128)(2,1)S(1)}, u32[]{:S(2)}, u32[]{:S(2)}) collective-permute-start(bf16[24,2048]{1,0:T(8,128)(2,1)S(1)} %collective-permute-done.2.refs_1_), channel_id=1, source_target_pairs={{0,1},{1,0},{2,3},{3,2},{4,5},{5,4},{6,7},{7,6},{8,9},{9,8},{10,11... | collective-permute-start | bytes 294920 | tf_op jit(solution)/shard_map/ppermute | solution.py:32
  26.4 2.4 %collective-permute-start.10 = (bf16[24,2048]{1,0:T(8,128)(2,1)S(1)}, bf16[24,2048]{1,0:T(8,128)(2,1)S(1)}, u32[]{:S(2)}, u32[]{:S(2)}) collective-permute-start(bf16[24,2048]{1,0:T(8,128)(2,1)S(1)} %collective-permute-done.3.refs_2_), channel_id=1, source_target_pairs={{0,1},{1,0},{2,3},{3,2},{4,5},{5,4},{6,7},{7,6},{8,9},{9,8},{10,11... | collective-permute-start | bytes 294920 | tf_op jit(solution)/shard_map/ppermute | solution.py:32
  26.9 1.9 %collective-permute-start.11 = (bf16[24,2048]{1,0:T(8,128)(2,1)S(1)}, bf16[24,2048]{1,0:T(8,128)(2,1)S(1)}, u32[]{:S(2)}, u32[]{:S(2)}) collective-permute-start(bf16[24,2048]{1,0:T(8,128)(2,1)S(1)} %collective-permute-done.4.refs_3_), channel_id=1, source_target_pairs={{0,1},{1,0},{2,3},{3,2},{4,5},{5,4},{6,7},{7,6},{8,9},{9,8},{10,11... | collective-permute-start | bytes 294920 | tf_op jit(solution)/shard_map/ppermute | solution.py:32
  27.0 1.8 %collective-permute-start.12 = (bf16[24,2048]{1,0:T(8,128)(2,1)S(1)}, bf16[24,2048]{1,0:T(8,128)(2,1)S(1)}, u32[]{:S(2)}, u32[]{:S(2)}) collective-permute-start(bf16[24,2048]{1,0:T(8,128)(2,1)S(1)} %collective-permute-done.5.refs_4_), channel_id=1, source_target_pairs={{0,1},{1,0},{2,3},{3,2},{4,5},{5,4},{6,7},{7,6},{8,9},{9,8},{10,11... | collective-permute-start | bytes 294920 | tf_op jit(solution)/shard_map/ppermute | solution.py:32
  27.5 1.4 %collective-permute-start.13 = (bf16[24,2048]{1,0:T(8,128)(2,1)S(1)}, bf16[24,2048]{1,0:T(8,128)(2,1)S(1)}, u32[]{:S(2)}, u32[]{:S(2)}) collective-permute-start(bf16[24,2048]{1,0:T(8,128)(2,1)S(1)} %collective-permute-done.6.refs_5_), channel_id=1, source_target_pairs={{0,1},{1,0},{2,3},{3,2},{4,5},{5,4},{6,7},{7,6},{8,9},{9,8},{10,11... | collective-permute-start | bytes 294920 | tf_op jit(solution)/shard_map/ppermute | solution.py:32
  27.7 1.3 %collective-permute-start.14 = (bf16[24,2048]{1,0:T(8,128)(2,1)S(1)}, bf16[24,2048]{1,0:T(8,128)(2,1)S(1)}, u32[]{:S(2)}, u32[]{:S(2)}) collective-permute-start(bf16[24,2048]{1,0:T(8,128)(2,1)S(1)} %collective-permute-done.7.refs_6_), channel_id=1, source_target_pairs={{0,1},{1,0},{2,3},{3,2},{4,5},{5,4},{6,7},{7,6},{8,9},{9,8},{10,11... | collective-permute-start | bytes 294920 | tf_op jit(solution)/shard_map/ppermute | solution.py:32
  30.0 8.0 %collective-permute-start.16 = (bf16[24,1024]{1,0:T(8,128)(2,1)S(1)}, bf16[24,1024]{1,0:T(8,128)(2,1)S(1)}, u32[]{:S(2)}, u32[]{:S(2)}) collective-permute-start(bf16[24,1024]{1,0:T(8,128)(2,1)S(1)} %get-tuple-element.46), channel_id=1, source_target_pairs={{0,14},{1,15},{2,12},{3,13},{4,10},{5,11},{6,8},{7,9},{8,6},{9,7},... | collective-permute-start | bytes 147464 | tf_op jit(solution)/shard_map/ppermute | solution.py:32
  32.7 7.0 %collective-permute-start.17 = (bf16[24,1024]{1,0:T(8,128)(2,1)S(1)}, bf16[24,1024]{1,0:T(8,128)(2,1)S(1)}, u32[]{:S(2)}, u32[]{:S(2)}) collective-permute-start(bf16[24,1024]{1,0:T(8,128)(2,1)S(1)} %get-tuple-element.47), channel_id=1, source_target_pairs={{0,12},{1,13},{2,14},{3,15},{4,8},{5,9},{6,10},{7,11},{8,4},{9,5},... | collective-permute-start | bytes 147464 | tf_op jit(solution)/shard_map/ppermute | solution.py:32
  33.9 8.8 %collective-permute-start.18 = (bf16[24,1024]{1,0:T(8,128)(2,1)S(1)}, bf16[24,1024]{1,0:T(8,128)(2,1)S(1)}, u32[]{:S(2)}, u32[]{:S(2)}) collective-permute-start(bf16[24,1024]{1,0:T(8,128)(2,1)S(1)} %get-tuple-element.48), channel_id=1, source_target_pairs={{0,10},{1,11},{2,8},{3,9},{4,14},{5,15},{6,12},{7,13},{8,2},{9,3},... | collective-permute-start | bytes 147464 | tf_op jit(solution)/shard_map/ppermute | solution.py:32
  36.2 6.5 %collective-permute-start.19 = (bf16[24,1024]{1,0:T(8,128)(2,1)S(1)}, bf16[24,1024]{1,0:T(8,128)(2,1)S(1)}, u32[]{:S(2)}, u32[]{:S(2)}) collective-permute-start(bf16[24,1024]{1,0:T(8,128)(2,1)S(1)} %get-tuple-element.49), channel_id=1, source_target_pairs={{0,4},{1,5},{2,6},{3,7},{4,0},{5,1},{6,2},{7,3},{8,12},{9,13},{10,... | collective-permute-start | bytes 147464 | tf_op jit(solution)/shard_map/ppermute | solution.py:32
  38.0 5.2 %collective-permute-start.20 = (bf16[24,1024]{1,0:T(8,128)(2,1)S(1)}, bf16[24,1024]{1,0:T(8,128)(2,1)S(1)}, u32[]{:S(2)}, u32[]{:S(2)}) collective-permute-start(bf16[24,1024]{1,0:T(8,128)(2,1)S(1)} %get-tuple-element.50), channel_id=1, source_target_pairs={{0,8},{1,9},{2,10},{3,11},{4,12},{5,13},{6,14},{7,15},{8,0},{9,1},... | collective-permute-start | bytes 147464 | tf_op jit(solution)/shard_map/ppermute | solution.py:32
  38.0 6.2 %collective-permute-start.21 = (bf16[24,1024]{1,0:T(8,128)(2,1)S(1)}, bf16[24,1024]{1,0:T(8,128)(2,1)S(1)}, u32[]{:S(2)}, u32[]{:S(2)}) collective-permute-start(bf16[24,1024]{1,0:T(8,128)(2,1)S(1)} %get-tuple-element.51), channel_id=1, source_target_pairs={{0,6},{1,7},{2,4},{3,5},{4,2},{5,3},{6,0},{7,1},{8,14},{9,15},{10,... | collective-permute-start | bytes 147464 | tf_op jit(solution)/shard_map/ppermute | solution.py:32
  39.7 4.7 %collective-permute-start.22 = (bf16[24,1024]{1,0:T(8,128)(2,1)S(1)}, bf16[24,1024]{1,0:T(8,128)(2,1)S(1)}, u32[]{:S(2)}, u32[]{:S(2)}) collective-permute-start(bf16[24,1024]{1,0:T(8,128)(2,1)S(1)} %get-tuple-element.52), channel_id=1, source_target_pairs={{0,2},{1,3},{2,0},{3,1},{4,6},{5,7},{6,4},{7,5},{8,10},{9,11},{10,... | collective-permute-start | bytes 147464 | tf_op jit(solution)/shard_map/ppermute | solution.py:32
  (2 other events, 50.7 us)

commit v4 on v3

--- a/solution.py
+++ b/solution.py
@@ -43,72 +43,86 @@
         copy.wait()
 
 
-def pack_kernel(chips, step_ref, query_ref, current_ref, earlier_ref, exponent_ref, *refs):
+def pack_kernel(order, step_ref, query_ref, current_ref, earlier_ref, exponent_ref, *refs):
+    chips = len(order)
     messages = refs[:chips]
-    queries, current, earlier, exponents, packed, sems, out_sems = refs[chips:]
+    queries, current, earlier, exponents, limits, packed, sems, side_sems, out_sems = refs[chips:]
     _, _, channel_count = query_ref.shape
     head_count = exponent_ref.shape[-1]
     head_dim = channel_count // head_count
     width = channel_count // chips
     kept, refreshed = layers_of(step_ref[0])
     here = lax.div(lax.axis_index("patch"), 2)
-    pairs = (
-        (query_ref, queries),
-        (current_ref.at[refreshed], current),
-        (earlier_ref.at[refreshed], earlier),
-        (exponent_ref.at[refreshed], exponents),
-    )
     copies = start_all(
         [
-            pltpu.make_async_copy(source, target, sems.at[index])
-            for index, (source, target) in enumerate(pairs)
+            pltpu.make_async_copy(exponent_ref.at[refreshed], exponents, sems.at[0]),
+            pltpu.make_async_copy(query_ref, queries, sems.at[1]),
         ]
     )
-    places = [lax.bitwise_xor(here, chip) for chip in range(chips)]
+    side_copies = [
+        start_all(
+            [
+                pltpu.make_async_copy(
+                    source.at[refreshed, side], target.at[side], side_sems.at[side, index]
+                )
+                for index, (source, target) in enumerate(
+                    ((current_ref, current), (earlier_ref, earlier))
+                )
+            ]
+        )
+        for side in range(2)
+    ]
     copies[0].wait()
-    for slot, layer in enumerate((kept, refreshed)):
-        for chip in range(chips):
-            packed[places[chip], :, slot * width : (slot + 1) * width] = queries[
-                layer, :, chip * width : (chip + 1) * width
-            ]
-    wait_all(copies[1:])
     for side in range(2):
-        limits = block_limits(exponents[side])
-        first = (2 + side) * width
+        values = block_limits(exponents[side])
         for head in range(head_count):
-            span = slice(head * head_dim, (head + 1) * head_dim)
+            limits[side, :, head * head_dim : (head + 1) * head_dim] = jnp.broadcast_to(
+                values[:, head : head + 1], (values.shape[0], head_dim)
+            )
+    copies[1].wait()
+    spans = [
+        pl.ds(pl.multiple_of(lax.bitwise_xor(here, chip) * width, width), width)
+        for chip in order
+    ]
+    for chip, span in zip(order, spans):
+        for slot, layer in enumerate((kept, refreshed)):
+            packed[chip, :, slot * width : (slot + 1) * width] = queries[layer, :, span]
+    out_copies = []
+    for side in range(2):
+        wait_all(side_copies[side])
+        for chip, span in zip(order, spans):
             residual = current[side, :, span].astype(jnp.float32) - earlier[
                 side, :, span
             ].astype(jnp.float32)
-            limit = limits[:, head : head + 1]
+            limit = limits[side, :, span]
             update = jnp.minimum(jnp.maximum(residual, -limit), limit).astype(jnp.bfloat16)
-            chip, inner = divmod(head * head_dim, width)
-            packed[places[chip], :, first + inner : first + inner + head_dim] = update
-    wait_all(
-        start_all(
-            [
-                pltpu.make_async_copy(packed.at[chip], messages[chip], out_sems.at[chip])
-                for chip in range(chips)
-            ]
-        )
-    )
-
-
-def pack(step_index, queries, current_pairs, earlier_pairs, block_exponents, chips):
+            packed[chip, :, (2 + side) * width : (3 + side) * width] = update
+            if side == 1:
+                out_copies.append(
+                    pltpu.make_async_copy(packed.at[chip], messages[chip], out_sems.at[chip])
+                )
+                out_copies[-1].start()
+    wait_all(out_copies)
+
+
+def pack(step_index, queries, current_pairs, earlier_pairs, block_exponents, order):
     _, token_count, channel_count = queries.shape
+    chips = len(order)
     columns = 4 * (channel_count // chips)
     far = pl.BlockSpec(memory_space=pl.ANY)
     layers = [current_pairs, earlier_pairs, block_exponents]
     return pl.pallas_call(
-        partial(pack_kernel, chips),
+        partial(pack_kernel, order),
         in_specs=[pl.BlockSpec(memory_space=pltpu.SMEM)] + [far] * 4,
         out_specs=[far] * chips,
         out_shape=[jax.ShapeDtypeStruct((token_count, columns), jnp.bfloat16)] * chips,
         scratch_shapes=[pltpu.VMEM(queries.shape, queries.dtype)]
         + [pltpu.VMEM(array.shape[1:], array.dtype) for array in layers]
         + [
+            pltpu.VMEM(current_pairs.shape[1:], jnp.float32),
             pltpu.VMEM((chips, token_count, columns), jnp.bfloat16),
-            pltpu.SemaphoreType.DMA((4,)),
+            pltpu.SemaphoreType.DMA((2,)),
+            pltpu.SemaphoreType.DMA((2, 2)),
             pltpu.SemaphoreType.DMA((chips,)),
         ],
         compiler_params=pltpu.CompilerParams(vmem_limit_bytes=PACK_BYTES),
@@ -315,7 +329,7 @@
 
 def distances(chips):
     if chips == 8:
-        return [5, 1, 3, 6, 4, 2, 7, 0], [7, 6, 5, 2, 4, 3, 1, 0]
+        return [5, 1, 3, 4, 6, 2, 7, 0], [7, 6, 5, 2, 4, 3, 1, 0]
     order = list(range(chips - 1, -1, -1))
     return order, order
 
@@ -328,12 +342,12 @@
     layer_count, token_count, channel_count = queries.shape
     head_dim = channel_count // block_exponents.shape[-1]
     stale = stale_cache.reshape(layer_count, 2, devices * token_count, -1)
+    order, back_order = distances(chips)
     other_stale = pairwise(stale, 1, devices)
     messages = pack(
-        step_index, queries, current_pairs, earlier_pairs, block_exponents, chips
+        step_index, queries, current_pairs, earlier_pairs, block_exponents, order
     )
     *messages, other_stale = lax.optimization_barrier((*messages, other_stale))
-    order, back_order = distances(chips)
     arrived = {
         chip: pairwise(messages[chip], 2 * chip, devices) for chip in order if chip
     }

time: 45.3 us -> 44.6 us (0.985)
  waiting for transfers between devices: 10.2 us -> 7.66 us
  starting transfers between devices: 27.4 us -> 29.4 us
    ppermute x23, waiting for transfers between devices: 10.2 us -> 7.66 us  [pairwise(): return lax.ppermute(array, 'patch', pairs)]
    ppermute x23, starting transfers between devices: 27.4 us -> 29.4 us  [pairwise(): return lax.ppermute(array, 'patch', pairs)]
where the time goes in v4:
time: 44.6 us; the launch traced here: 44.5 us
  starting transfers between devices  29.4 us (66%)
  waiting for transfers between devices  7.66 us (17%)
  Pallas kernels  6 us (13%)
  between operations  1.4 us (3%)
    ppermute x23, starting transfers between devices, pairwise(): return lax.ppermute(array, 'patch', pairs)  29.4 us
    ppermute x23, waiting for transfers between devices, pairwise(): return lax.ppermute(array, 'patch', pairs)  7.66 us
    pallas_call x1, Pallas kernels, pack(): pl.pallas_call(partial(pack_kernel, order), in_specs=[pl.BlockSpec(memory...  2.53 us
    pallas_call x1, Pallas kernels, attend_refreshed(): pl.pallas_call(partial(refreshed_kernel, order, head_dim), in_specs=[pl.B...  0.98 us
  transfers between devices with their start and end apart: 23, of which 9 were waited for; matrix products, arithmetic and copies ran while one was open for 0% of the time, Pallas kernels for 10%

profile of v4, /device:TPU:0, one launch (start us, length us, event | category | flops | bytes accessed | tf_op | source)
XLA Modules:
  0.0 44.5 jit_solution(6010589943572534387)
XLA Ops:
  0.6 0.5 %collective-permute-start = (bf16[2,2,384,256]{3,2,1,0:T(8,128)(2,1)}, bf16[2,2,384,256]{3,2,1,0:T(8,128)(2,1)S(1)}, u32[]{:S(2)}, u32[]{:S(2)}) collective-permute-start(bf16[2,2,384,256]{3,2,1,0:T(8,128)(2,1)} %bitcast.4), channel_id=1, source_target_pairs={{0,1},{1,0},{2,3},{3,2},{4,5},{5,4},{6,7},{7,6},{8,9},{9,8},{10,11... | collective-permute-start | bytes 2359304 | tf_op jit(solution)/shard_map/ppermute | solution.py:32
  1.8 2.5 %shard_map.77 = (bf16[24,2048]{1,0:T(8,128)(2,1)}, bf16[24,2048]{1,0:T(8,128)(2,1)}, bf16[24,2048]{1,0:T(8,128)(2,1)}, bf16[24,2048]{1,0:T(8,128)(2,1)}, bf16[24...) custom-call(s32[1]{0:T(128)S(6)} %copy.9.step_ref, ...), custom_call_target="tpu_custom_call" | custom-call | tf_op jit(solution)/shard_map/pallas_call | solution.py:114
  4.4 4.6 %collective-permute-start.1 = (bf16[24,2048]{1,0:T(8,128)(2,1)}, bf16[24,2048]{1,0:T(8,128)(2,1)S(1)}, u32[]{:S(2)}, u32[]{:S(2)}) collective-permute-start(bf16[24,2048]{1,0:T(8,128)(2,1)} %get-tuple-element.37), channel_id=1, source_target_pairs={{0,10},{1,11},{2,8},{3,9},{4,14},{5,15},{6,12},{7,13},{8,2},{9,3},... | collective-permute-start | bytes 294920 | tf_op jit(solution)/shard_map/ppermute | solution.py:32
  9.0 0.5 %collective-permute-start.2 = (bf16[24,2048]{1,0:T(8,128)(2,1)}, bf16[24,2048]{1,0:T(8,128)(2,1)S(1)}, u32[]{:S(2)}, u32[]{:S(2)}) collective-permute-start(bf16[24,2048]{1,0:T(8,128)(2,1)} %get-tuple-element.38), channel_id=1, source_target_pairs={{0,2},{1,3},{2,0},{3,1},{4,6},{5,7},{6,4},{7,5},{8,10},{9,11},{10,... | collective-permute-start | bytes 294920 | tf_op jit(solution)/shard_map/ppermute | solution.py:32
  9.5 2.5 %collective-permute-start.3 = (bf16[24,2048]{1,0:T(8,128)(2,1)}, bf16[24,2048]{1,0:T(8,128)(2,1)S(1)}, u32[]{:S(2)}, u32[]{:S(2)}) collective-permute-start(bf16[24,2048]{1,0:T(8,128)(2,1)} %get-tuple-element.39), channel_id=1, source_target_pairs={{0,6},{1,7},{2,4},{3,5},{4,2},{5,3},{6,0},{7,1},{8,14},{9,15},{10,... | collective-permute-start | bytes 294920 | tf_op jit(solution)/shard_map/ppermute | solution.py:32
  12.3 2.5 %collective-permute-start.5 = (bf16[24,2048]{1,0:T(8,128)(2,1)}, bf16[24,2048]{1,0:T(8,128)(2,1)S(1)}, u32[]{:S(2)}, u32[]{:S(2)}) collective-permute-start(bf16[24,2048]{1,0:T(8,128)(2,1)} %get-tuple-element.41), channel_id=1, source_target_pairs={{0,12},{1,13},{2,14},{3,15},{4,8},{5,9},{6,10},{7,11},{8,4},{9,5},... | collective-permute-start | bytes 294920 | tf_op jit(solution)/shard_map/ppermute | solution.py:32
  15.0 1.2 %collective-permute-start.6 = (bf16[24,2048]{1,0:T(8,128)(2,1)}, bf16[24,2048]{1,0:T(8,128)(2,1)S(1)}, u32[]{:S(2)}, u32[]{:S(2)}) collective-permute-start(bf16[24,2048]{1,0:T(8,128)(2,1)} %get-tuple-element.42), channel_id=1, source_target_pairs={{0,4},{1,5},{2,6},{3,7},{4,0},{5,1},{6,2},{7,3},{8,12},{9,13},{10,... | collective-permute-start | bytes 294920 | tf_op jit(solution)/shard_map/ppermute | solution.py:32
  16.3 3.7 %collective-permute-start.7 = (bf16[24,2048]{1,0:T(8,128)(2,1)}, bf16[24,2048]{1,0:T(8,128)(2,1)S(1)}, u32[]{:S(2)}, u32[]{:S(2)}) collective-permute-start(bf16[24,2048]{1,0:T(8,128)(2,1)} %get-tuple-element.43), channel_id=1, source_target_pairs={{0,14},{1,15},{2,12},{3,13},{4,10},{5,11},{6,8},{7,9},{8,6},{9,7},... | collective-permute-start | bytes 294920 | tf_op jit(solution)/shard_map/ppermute | solution.py:32
  20.0 3.1 %collective-permute-done.4.refs_3_ = bf16[24,2048]{1,0:T(8,128)(2,1)S(1)} collective-permute-done((bf16[24,2048]{1,0:T(8,128)(2,1)}, bf16[24,2048]{1,0:T(8,128)(2,1)S(1)}, u32[]{:S(2)}, u32[]{:S(2)}) %collective-permute-start.4) | collective-permute-done | bytes 98336 | tf_op jit(solution)/shard_map/ppermute | solution.py:32
  23.1 0.5 %collective-permute-start.9 = (bf16[24,2048]{1,0:T(8,128)(2,1)S(1)}, bf16[24,2048]{1,0:T(8,128)(2,1)S(1)}, u32[]{:S(2)}, u32[]{:S(2)}) collective-permute-start(bf16[24,2048]{1,0:T(8,128)(2,1)S(1)} %collective-permute-done.2.refs_1_), channel_id=1, source_target_pairs={{0,1},{1,0},{2,3},{3,2},{4,5},{5,4},{6,7},{7,6},{8,9},{9,8},{10,11... | collective-permute-start | bytes 294920 | tf_op jit(solution)/shard_map/ppermute | solution.py:32
  23.7 1.7 %collective-permute-done.7.refs_6_ = bf16[24,2048]{1,0:T(8,128)(2,1)S(1)} collective-permute-done((bf16[24,2048]{1,0:T(8,128)(2,1)}, bf16[24,2048]{1,0:T(8,128)(2,1)S(1)}, u32[]{:S(2)}, u32[]{:S(2)}) %collective-permute-start.7) | collective-permute-done | bytes 98336 | tf_op jit(solution)/shard_map/ppermute | solution.py:32
  25.4 0.5 %collective-permute-start.12 = (bf16[24,2048]{1,0:T(8,128)(2,1)S(1)}, bf16[24,2048]{1,0:T(8,128)(2,1)S(1)}, u32[]{:S(2)}, u32[]{:S(2)}) collective-permute-start(bf16[24,2048]{1,0:T(8,128)(2,1)S(1)} %collective-permute-done.5.refs_4_), channel_id=1, source_target_pairs={{0,1},{1,0},{2,3},{3,2},{4,5},{5,4},{6,7},{7,6},{8,9},{9,8},{10,11... | collective-permute-start | bytes 294920 | tf_op jit(solution)/shard_map/ppermute | solution.py:32
  26.4 0.8 %shard_map.78.refs_16_ = bf16[192,512]{1,0:T(8,128)(2,1)S(1)} custom-call(s32[1]{0:T(128)S(6)} %copy.9.step_ref, bf16[2,24,4096]{2,1,0:T(8,128)(2,1)S(1)} %copy-done.1, bf16[24,2048]{1,0:T(8,128)(2,1)S(1)} %collective-permute-done.1.refs_0_, bf16[24,2048]{1,0:T(8,128)(2,1)S(1)} %collective-permute-done.2.refs_1_, ...), custom_call_target="tpu_custom_call" | custom-call | tf_op jit(solution)/shard_map/pallas_call | solution.py:189
  27.4 1.0 %shard_map.79 = (bf16[24,1024]{1,0:T(8,128)(2,1)S(1)}, bf16[24,1024]{1,0:T(8,128)(2,1)S(1)}, bf16[24,1024]{1,0:T(8,128)(2,1)S(1)}, bf16[24,1024]{1,0:T(8,128)(2,...) custom-call(s32[1]{0:T(128)S(6)} %copy.9.step_ref, ...), custom_call_target="tpu_custom_call" | custom-call | tf_op jit(solution)/shard_map/pallas_call | solution.py:255
  28.4 3.9 %collective-permute-start.16 = (bf16[24,1024]{1,0:T(8,128)(2,1)S(1)}, bf16[24,1024]{1,0:T(8,128)(2,1)S(1)}, u32[]{:S(2)}, u32[]{:S(2)}) collective-permute-start(bf16[24,1024]{1,0:T(8,128)(2,1)S(1)} %get-tuple-element.46), channel_id=1, source_target_pairs={{0,14},{1,15},{2,12},{3,13},{4,10},{5,11},{6,8},{7,9},{8,6},{9,7},... | collective-permute-start | bytes 147464 | tf_op jit(solution)/shard_map/ppermute | solution.py:32
  32.2 0.7 %collective-permute-start.17 = (bf16[24,1024]{1,0:T(8,128)(2,1)S(1)}, bf16[24,1024]{1,0:T(8,128)(2,1)S(1)}, u32[]{:S(2)}, u32[]{:S(2)}) collective-permute-start(bf16[24,1024]{1,0:T(8,128)(2,1)S(1)} %get-tuple-element.47), channel_id=1, source_target_pairs={{0,12},{1,13},{2,14},{3,15},{4,8},{5,9},{6,10},{7,11},{8,4},{9,5},... | collective-permute-start | bytes 147464 | tf_op jit(solution)/shard_map/ppermute | solution.py:32
  32.9 3.1 %collective-permute-start.18 = (bf16[24,1024]{1,0:T(8,128)(2,1)S(1)}, bf16[24,1024]{1,0:T(8,128)(2,1)S(1)}, u32[]{:S(2)}, u32[]{:S(2)}) collective-permute-start(bf16[24,1024]{1,0:T(8,128)(2,1)S(1)} %get-tuple-element.48), channel_id=1, source_target_pairs={{0,10},{1,11},{2,8},{3,9},{4,14},{5,15},{6,12},{7,13},{8,2},{9,3},... | collective-permute-start | bytes 147464 | tf_op jit(solution)/shard_map/ppermute | solution.py:32
  36.0 1.5 %collective-permute-start.19 = (bf16[24,1024]{1,0:T(8,128)(2,1)S(1)}, bf16[24,1024]{1,0:T(8,128)(2,1)S(1)}, u32[]{:S(2)}, u32[]{:S(2)}) collective-permute-start(bf16[24,1024]{1,0:T(8,128)(2,1)S(1)} %get-tuple-element.49), channel_id=1, source_target_pairs={{0,4},{1,5},{2,6},{3,7},{4,0},{5,1},{6,2},{7,3},{8,12},{9,13},{10,... | collective-permute-start | bytes 147464 | tf_op jit(solution)/shard_map/ppermute | solution.py:32
  37.6 1.4 %collective-permute-start.21 = (bf16[24,1024]{1,0:T(8,128)(2,1)S(1)}, bf16[24,1024]{1,0:T(8,128)(2,1)S(1)}, u32[]{:S(2)}, u32[]{:S(2)}) collective-permute-start(bf16[24,1024]{1,0:T(8,128)(2,1)S(1)} %get-tuple-element.51), channel_id=1, source_target_pairs={{0,6},{1,7},{2,4},{3,5},{4,2},{5,3},{6,0},{7,1},{8,14},{9,15},{10,... | collective-permute-start | bytes 147464 | tf_op jit(solution)/shard_map/ppermute | solution.py:32
  39.0 1.3 %collective-permute-start.22 = (bf16[24,1024]{1,0:T(8,128)(2,1)S(1)}, bf16[24,1024]{1,0:T(8,128)(2,1)S(1)}, u32[]{:S(2)}, u32[]{:S(2)}) collective-permute-start(bf16[24,1024]{1,0:T(8,128)(2,1)S(1)} %get-tuple-element.52), channel_id=1, source_target_pairs={{0,2},{1,3},{2,0},{3,1},{4,6},{5,7},{6,4},{7,5},{8,10},{9,11},{10,... | collective-permute-start | bytes 147464 | tf_op jit(solution)/shard_map/ppermute | solution.py:32
  40.3 0.9 %shard_map.81 = bf16[2,2,384,256]{3,2,1,0:T(8,128)(2,1)} custom-call(s32[1]{0:T(128)S(6)} %copy.9.step_ref, bf16[2,2,384,256]{3,2,1,0:T(8,128)(2,1)S(1)} %bitcast.7, bf16[2,384,256]{2,1,0:T(8,128)(2,1)S(1)} %get-tuple-element.55.renewed_ref), custom_call_target="tpu_custom_call" | custom-call | tf_op jit(solution)/shard_map/pallas_call | solution.py:281
  41.2 0.7 %collective-permute-done.18.refs_2_ = bf16[24,1024]{1,0:T(8,128)(2,1)S(1)} collective-permute-done((bf16[24,1024]{1,0:T(8,128)(2,1)S(1)}, bf16[24,1024]{1,0:T(8,128)(2,1)S(1)}, u32[]{:S(2)}, u32[]{:S(2)}) %collective-permute-start.18) | collective-permute-done | bytes 49184 | tf_op jit(solution)/shard_map/ppermute | solution.py:32
  41.9 1.1 %collective-permute-done.20.refs_4_ = bf16[24,1024]{1,0:T(8,128)(2,1)S(1)} collective-permute-done((bf16[24,1024]{1,0:T(8,128)(2,1)S(1)}, bf16[24,1024]{1,0:T(8,128)(2,1)S(1)}, u32[]{:S(2)}, u32[]{:S(2)}) %collective-permute-start.20) | collective-permute-done | bytes 49184 | tf_op jit(solution)/shard_map/ppermute | solution.py:32
  43.7 0.8 %shard_map.80 = bf16[2,24,4096]{2,1,0:T(8,128)(2,1)} custom-call(s32[1]{0:T(128)S(6)} %copy.9.step_ref, bf16[24,1024]{1,0:T(8,128)(2,1)S(1)} %collective-permute-done.16.refs_0_, bf16[24,1024]{1,0:T(8,128)(2,1)S(1)} %collective-permute-done.17.refs_1_, bf16[24,1024]{1,0:T(8,128)(2,1)S(1)} %collective-permute-done.18.refs_2_, ...), custom_call_target="tpu_custom_call" | custom-call | tf_op jit(solution)/shard_map/pallas_call | solution.py:316
  (33 shorter events, 2.1 us)
Async XLA Ops:
  0.6 3.7 %collective-permute-start = (bf16[2,2,384,256]{3,2,1,0:T(8,128)(2,1)}, bf16[2,2,384,256]{3,2,1,0:T(8,128)(2,1)S(1)}, u32[]{:S(2)}, u32[]{:S(2)}) collective-permute-start(bf16[2,2,384,256]{3,2,1,0:T(8,128)(2,1)} %bitcast.4), channel_id=1, source_target_pairs={{0,1},{1,0},{2,3},{3,2},{4,5},{5,4},{6,7},{7,6},{8,9},{9,8},{10,11... | collective-permute-start | bytes 2359304 | tf_op jit(solution)/shard_map/ppermute | solution.py:32
  1.8 24.6 %copy-start = (bf16[2,2,1,16,24,256]{5,4,3,2,1,0:T(8,128)(2,1)S(1)}, bf16[2,2,1,16,24,256]{5,4,3,2,1,0:T(8,128)(2,1)}, u32[]{:S(2)}) copy-start(bf16[2,2,1,16,24,256]{5,4,3,2,1,0:T(8,128)(2,1)} %param.9) | copy-start | bytes 2359300
  4.4 10.6 %collective-permute-start.1 = (bf16[24,2048]{1,0:T(8,128)(2,1)}, bf16[24,2048]{1,0:T(8,128)(2,1)S(1)}, u32[]{:S(2)}, u32[]{:S(2)}) collective-permute-start(bf16[24,2048]{1,0:T(8,128)(2,1)} %get-tuple-element.37), channel_id=1, source_target_pairs={{0,10},{1,11},{2,8},{3,9},{4,14},{5,15},{6,12},{7,13},{8,2},{9,3},... | collective-permute-start | bytes 294920 | tf_op jit(solution)/shard_map/ppermute | solution.py:32
  9.0 7.4 %collective-permute-start.2 = (bf16[24,2048]{1,0:T(8,128)(2,1)}, bf16[24,2048]{1,0:T(8,128)(2,1)S(1)}, u32[]{:S(2)}, u32[]{:S(2)}) collective-permute-start(bf16[24,2048]{1,0:T(8,128)(2,1)} %get-tuple-element.38), channel_id=1, source_target_pairs={{0,2},{1,3},{2,0},{3,1},{4,6},{5,7},{6,4},{7,5},{8,10},{9,11},{10,... | collective-permute-start | bytes 294920 | tf_op jit(solution)/shard_map/ppermute | solution.py:32
  9.5 10.5 %collective-permute-start.3 = (bf16[24,2048]{1,0:T(8,128)(2,1)}, bf16[24,2048]{1,0:T(8,128)(2,1)S(1)}, u32[]{:S(2)}, u32[]{:S(2)}) collective-permute-start(bf16[24,2048]{1,0:T(8,128)(2,1)} %get-tuple-element.39), channel_id=1, source_target_pairs={{0,6},{1,7},{2,4},{3,5},{4,2},{5,3},{6,0},{7,1},{8,14},{9,15},{10,... | collective-permute-start | bytes 294920 | tf_op jit(solution)/shard_map/ppermute | solution.py:32
  12.0 11.1 %collective-permute-start.4 = (bf16[24,2048]{1,0:T(8,128)(2,1)}, bf16[24,2048]{1,0:T(8,128)(2,1)S(1)}, u32[]{:S(2)}, u32[]{:S(2)}) collective-permute-start(bf16[24,2048]{1,0:T(8,128)(2,1)} %get-tuple-element.40), channel_id=1, source_target_pairs={{0,8},{1,9},{2,10},{3,11},{4,12},{5,13},{6,14},{7,15},{8,0},{9,1},... | collective-permute-start | bytes 294920 | tf_op jit(solution)/shard_map/ppermute | solution.py:32
  12.3 10.8 %collective-permute-start.5 = (bf16[24,2048]{1,0:T(8,128)(2,1)}, bf16[24,2048]{1,0:T(8,128)(2,1)S(1)}, u32[]{:S(2)}, u32[]{:S(2)}) collective-permute-start(bf16[24,2048]{1,0:T(8,128)(2,1)} %get-tuple-element.41), channel_id=1, source_target_pairs={{0,12},{1,13},{2,14},{3,15},{4,8},{5,9},{6,10},{7,11},{8,4},{9,5},... | collective-permute-start | bytes 294920 | tf_op jit(solution)/shard_map/ppermute | solution.py:32
  15.0 8.7 %collective-permute-start.6 = (bf16[24,2048]{1,0:T(8,128)(2,1)}, bf16[24,2048]{1,0:T(8,128)(2,1)S(1)}, u32[]{:S(2)}, u32[]{:S(2)}) collective-permute-start(bf16[24,2048]{1,0:T(8,128)(2,1)} %get-tuple-element.42), channel_id=1, source_target_pairs={{0,4},{1,5},{2,6},{3,7},{4,0},{5,1},{6,2},{7,3},{8,12},{9,13},{10,... | collective-permute-start | bytes 294920 | tf_op jit(solution)/shard_map/ppermute | solution.py:32
  16.3 9.1 %collective-permute-start.7 = (bf16[24,2048]{1,0:T(8,128)(2,1)}, bf16[24,2048]{1,0:T(8,128)(2,1)S(1)}, u32[]{:S(2)}, u32[]{:S(2)}) collective-permute-start(bf16[24,2048]{1,0:T(8,128)(2,1)} %get-tuple-element.43), channel_id=1, source_target_pairs={{0,14},{1,15},{2,12},{3,13},{4,10},{5,11},{6,8},{7,9},{8,6},{9,7},... | collective-permute-start | bytes 294920 | tf_op jit(solution)/shard_map/ppermute | solution.py:32
  20.0 5.4 %collective-permute-start.15 = (bf16[24,2048]{1,0:T(8,128)(2,1)}, bf16[24,2048]{1,0:T(8,128)(2,1)S(1)}, u32[]{:S(2)}, u32[]{:S(2)}) collective-permute-start(bf16[24,2048]{1,0:T(8,128)(2,1)} %get-tuple-element.44.refs_7_), channel_id=1, source_target_pairs={{0,1},{1,0},{2,3},{3,2},{4,5},{5,4},{6,7},{7,6},{8,9},{9,8},{10,11... | collective-permute-start | bytes 294920 | tf_op jit(solution)/shard_map/ppermute | solution.py:32
  23.1 2.8 %collective-permute-start.8 = (bf16[24,2048]{1,0:T(8,128)(2,1)S(1)}, bf16[24,2048]{1,0:T(8,128)(2,1)S(1)}, u32[]{:S(2)}, u32[]{:S(2)}) collective-permute-start(bf16[24,2048]{1,0:T(8,128)(2,1)S(1)} %collective-permute-done.1.refs_0_), channel_id=1, source_target_pairs={{0,1},{1,0},{2,3},{3,2},{4,5},{5,4},{6,7},{7,6},{8,9},{9,8},{10,11... | collective-permute-start | bytes 294920 | tf_op jit(solution)/shard_map/ppermute | solution.py:32
  23.1 2.9 %collective-permute-start.9 = (bf16[24,2048]{1,0:T(8,128)(2,1)S(1)}, bf16[24,2048]{1,0:T(8,128)(2,1)S(1)}, u32[]{:S(2)}, u32[]{:S(2)}) collective-permute-start(bf16[24,2048]{1,0:T(8,128)(2,1)S(1)} %collective-permute-done.2.refs_1_), channel_id=1, source_target_pairs={{0,1},{1,0},{2,3},{3,2},{4,5},{5,4},{6,7},{7,6},{8,9},{9,8},{10,11... | collective-permute-start | bytes 294920 | tf_op jit(solution)/shard_map/ppermute | solution.py:32
  23.6 3.6 %collective-permute-start.10 = (bf16[24,2048]{1,0:T(8,128)(2,1)S(1)}, bf16[24,2048]{1,0:T(8,128)(2,1)S(1)}, u32[]{:S(2)}, u32[]{:S(2)}) collective-permute-start(bf16[24,2048]{1,0:T(8,128)(2,1)S(1)} %collective-permute-done.3.refs_2_), channel_id=1, source_target_pairs={{0,1},{1,0},{2,3},{3,2},{4,5},{5,4},{6,7},{7,6},{8,9},{9,8},{10,11... | collective-permute-start | bytes 294920 | tf_op jit(solution)/shard_map/ppermute | solution.py:32
  25.4 1.9 %collective-permute-start.11 = (bf16[24,2048]{1,0:T(8,128)(2,1)S(1)}, bf16[24,2048]{1,0:T(8,128)(2,1)S(1)}, u32[]{:S(2)}, u32[]{:S(2)}) collective-permute-start(bf16[24,2048]{1,0:T(8,128)(2,1)S(1)} %collective-permute-done.4.refs_3_), channel_id=1, source_target_pairs={{0,1},{1,0},{2,3},{3,2},{4,5},{5,4},{6,7},{7,6},{8,9},{9,8},{10,11... | collective-permute-start | bytes 294920 | tf_op jit(solution)/shard_map/ppermute | solution.py:32
  25.4 1.9 %collective-permute-start.12 = (bf16[24,2048]{1,0:T(8,128)(2,1)S(1)}, bf16[24,2048]{1,0:T(8,128)(2,1)S(1)}, u32[]{:S(2)}, u32[]{:S(2)}) collective-permute-start(bf16[24,2048]{1,0:T(8,128)(2,1)S(1)} %collective-permute-done.5.refs_4_), channel_id=1, source_target_pairs={{0,1},{1,0},{2,3},{3,2},{4,5},{5,4},{6,7},{7,6},{8,9},{9,8},{10,11... | collective-permute-start | bytes 294920 | tf_op jit(solution)/shard_map/ppermute | solution.py:32
  25.9 1.4 %collective-permute-start.13 = (bf16[24,2048]{1,0:T(8,128)(2,1)S(1)}, bf16[24,2048]{1,0:T(8,128)(2,1)S(1)}, u32[]{:S(2)}, u32[]{:S(2)}) collective-permute-start(bf16[24,2048]{1,0:T(8,128)(2,1)S(1)} %collective-permute-done.6.refs_5_), channel_id=1, source_target_pairs={{0,1},{1,0},{2,3},{3,2},{4,5},{5,4},{6,7},{7,6},{8,9},{9,8},{10,11... | collective-permute-start | bytes 294920 | tf_op jit(solution)/shard_map/ppermute | solution.py:32
  26.0 1.4 %collective-permute-start.14 = (bf16[24,2048]{1,0:T(8,128)(2,1)S(1)}, bf16[24,2048]{1,0:T(8,128)(2,1)S(1)}, u32[]{:S(2)}, u32[]{:S(2)}) collective-permute-start(bf16[24,2048]{1,0:T(8,128)(2,1)S(1)} %collective-permute-done.7.refs_6_), channel_id=1, source_target_pairs={{0,1},{1,0},{2,3},{3,2},{4,5},{5,4},{6,7},{7,6},{8,9},{9,8},{10,11... | collective-permute-start | bytes 294920 | tf_op jit(solution)/shard_map/ppermute | solution.py:32
  28.4 9.2 %collective-permute-start.16 = (bf16[24,1024]{1,0:T(8,128)(2,1)S(1)}, bf16[24,1024]{1,0:T(8,128)(2,1)S(1)}, u32[]{:S(2)}, u32[]{:S(2)}) collective-permute-start(bf16[24,1024]{1,0:T(8,128)(2,1)S(1)} %get-tuple-element.46), channel_id=1, source_target_pairs={{0,14},{1,15},{2,12},{3,13},{4,10},{5,11},{6,8},{7,9},{8,6},{9,7},... | collective-permute-start | bytes 147464 | tf_op jit(solution)/shard_map/ppermute | solution.py:32
  32.2 6.7 %collective-permute-start.17 = (bf16[24,1024]{1,0:T(8,128)(2,1)S(1)}, bf16[24,1024]{1,0:T(8,128)(2,1)S(1)}, u32[]{:S(2)}, u32[]{:S(2)}) collective-permute-start(bf16[24,1024]{1,0:T(8,128)(2,1)S(1)} %get-tuple-element.47), channel_id=1, source_target_pairs={{0,12},{1,13},{2,14},{3,15},{4,8},{5,9},{6,10},{7,11},{8,4},{9,5},... | collective-permute-start | bytes 147464 | tf_op jit(solution)/shard_map/ppermute | solution.py:32
  32.9 9.0 %collective-permute-start.18 = (bf16[24,1024]{1,0:T(8,128)(2,1)S(1)}, bf16[24,1024]{1,0:T(8,128)(2,1)S(1)}, u32[]{:S(2)}, u32[]{:S(2)}) collective-permute-start(bf16[24,1024]{1,0:T(8,128)(2,1)S(1)} %get-tuple-element.48), channel_id=1, source_target_pairs={{0,10},{1,11},{2,8},{3,9},{4,14},{5,15},{6,12},{7,13},{8,2},{9,3},... | collective-permute-start | bytes 147464 | tf_op jit(solution)/shard_map/ppermute | solution.py:32
  36.0 5.9 %collective-permute-start.19 = (bf16[24,1024]{1,0:T(8,128)(2,1)S(1)}, bf16[24,1024]{1,0:T(8,128)(2,1)S(1)}, u32[]{:S(2)}, u32[]{:S(2)}) collective-permute-start(bf16[24,1024]{1,0:T(8,128)(2,1)S(1)} %get-tuple-element.49), channel_id=1, source_target_pairs={{0,4},{1,5},{2,6},{3,7},{4,0},{5,1},{6,2},{7,3},{8,12},{9,13},{10,... | collective-permute-start | bytes 147464 | tf_op jit(solution)/shard_map/ppermute | solution.py:32
  37.5 5.5 %collective-permute-start.20 = (bf16[24,1024]{1,0:T(8,128)(2,1)S(1)}, bf16[24,1024]{1,0:T(8,128)(2,1)S(1)}, u32[]{:S(2)}, u32[]{:S(2)}) collective-permute-start(bf16[24,1024]{1,0:T(8,128)(2,1)S(1)} %get-tuple-element.50), channel_id=1, source_target_pairs={{0,8},{1,9},{2,10},{3,11},{4,12},{5,13},{6,14},{7,15},{8,0},{9,1},... | collective-permute-start | bytes 147464 | tf_op jit(solution)/shard_map/ppermute | solution.py:32
  37.6 5.8 %collective-permute-start.21 = (bf16[24,1024]{1,0:T(8,128)(2,1)S(1)}, bf16[24,1024]{1,0:T(8,128)(2,1)S(1)}, u32[]{:S(2)}, u32[]{:S(2)}) collective-permute-start(bf16[24,1024]{1,0:T(8,128)(2,1)S(1)} %get-tuple-element.51), channel_id=1, source_target_pairs={{0,6},{1,7},{2,4},{3,5},{4,2},{5,3},{6,0},{7,1},{8,14},{9,15},{10,... | collective-permute-start | bytes 147464 | tf_op jit(solution)/shard_map/ppermute | solution.py:32
  39.0 4.7 %collective-permute-start.22 = (bf16[24,1024]{1,0:T(8,128)(2,1)S(1)}, bf16[24,1024]{1,0:T(8,128)(2,1)S(1)}, u32[]{:S(2)}, u32[]{:S(2)}) collective-permute-start(bf16[24,1024]{1,0:T(8,128)(2,1)S(1)} %get-tuple-element.52), channel_id=1, source_target_pairs={{0,2},{1,3},{2,0},{3,1},{4,6},{5,7},{6,4},{7,5},{8,10},{9,11},{10,... | collective-permute-start | bytes 147464 | tf_op jit(solution)/shard_map/ppermute | solution.py:32
  (2 other events, 47.6 us)

commit v5 on v4

--- a/solution.py
+++ b/solution.py
@@ -162,6 +162,7 @@
 def kept_kernel(order, head_dim, step_ref, query_ref, *refs):
     messages = dict(zip([chip for chip in order if chip], refs))
     own_ref, other_ref, out_ref = refs[len(messages) :]
+    token_count = query_ref.shape[1]
     width = own_ref.shape[-1]
     kept, _ = layers_of(step_ref[0])
     here, core = lax.div(lax.axis_index("patch"), 2), lax.rem(lax.axis_index("patch"), 2)
@@ -178,7 +179,10 @@
         keys, values = cache_ref[kept, 0], cache_ref[kept, 1]
         for head, result in enumerate(answer(queries, keys, values, head_dim)):
             place = pl.ds(pl.multiple_of(first + head * head_dim, head_dim), head_dim)
-            out_ref[:, place] = result.astype(jnp.bfloat16)
+            for slot in range(len(order)):
+                out_ref[slot, :, place] = result[
+                    slot * token_count : (slot + 1) * token_count
+                ].astype(jnp.bfloat16)
 
 
 def attend_kept(step_index, queries, arrived, order, stale, other_stale, head_dim):
@@ -191,7 +195,7 @@
         in_specs=[pl.BlockSpec(memory_space=pltpu.SMEM)] + [whole] * (chips + 2),
         out_specs=whole,
         out_shape=jax.ShapeDtypeStruct(
-            (chips * token_count, channel_count // chips), jnp.bfloat16
+            (chips, token_count, channel_count // chips), jnp.bfloat16
         ),
         compiler_params=pltpu.CompilerParams(vmem_limit_bytes=VMEM_BYTES),
     )(step_index, queries, *messages, stale, other_stale)
@@ -239,11 +243,8 @@
                 answers[slot][:, place] = result[
                     slot * token_count : (slot + 1) * token_count
                 ].astype(jnp.bfloat16)
-    earlier = kept_out[...].astype(jnp.float32)
     for slot in range(chips):
-        answers[slot][:, : 2 * width] = earlier[
-            slot * token_count : (slot + 1) * token_count
-        ].astype(jnp.bfloat16)
+        answers[slot][:, : 2 * width] = kept_out[slot]
 
 
 def attend_refreshed(
@@ -296,18 +297,21 @@
 def place_kernel(order, step_ref, *refs):
     chips = len(order)
     answers = refs[:chips]
-    out_ref, placed, sem = refs[chips:]
+    out_ref, placed, sems = refs[chips:]
     width = answers[0].shape[-1] // 2
     here = lax.div(lax.axis_index("patch"), 2)
-    for slot, chip in enumerate(order):
-        first = pl.multiple_of(lax.bitwise_xor(here, chip) * width, width)
-        for half, layer in enumerate(layers_of(step_ref[0])):
+    copies = []
+    for half, layer in enumerate(layers_of(step_ref[0])):
+        for slot, chip in enumerate(order):
+            first = pl.multiple_of(lax.bitwise_xor(here, chip) * width, width)
             placed[layer, :, pl.ds(first, width)] = answers[slot][
                 :, half * width : (half + 1) * width
             ]
-    copy = pltpu.make_async_copy(placed, out_ref, sem)
-    copy.start()
-    copy.wait()
+        copies.append(
+            pltpu.make_async_copy(placed.at[layer], out_ref.at[layer], sems.at[half])
+        )
+        copies[-1].start()
+    wait_all(copies)
 
 
 def place(step_index, answers, order):
@@ -321,7 +325,7 @@
         out_shape=attended,
         scratch_shapes=[
             pltpu.VMEM(attended.shape, attended.dtype),
-            pltpu.SemaphoreType.DMA(()),
+            pltpu.SemaphoreType.DMA((2,)),
         ],
         compiler_params=pltpu.CompilerParams(vmem_limit_bytes=VMEM_BYTES),
     )(step_index, *answers)
@@ -329,7 +333,7 @@
 
 def distances(chips):
     if chips == 8:
-        return [5, 1, 3, 4, 6, 2, 7, 0], [7, 6, 5, 2, 4, 3, 1, 0]
+        return [5, 1, 3, 4, 6, 2, 7, 0], [7, 6, 5, 4, 3, 2, 1, 0]
     order = list(range(chips - 1, -1, -1))
     return order, order
 

time: 44.6 us -> 44.5 us (level)
  transfers between devices with their start and end apart: 23 -> 23, of which waited for: 9 -> 8; matrix products, arithmetic and copies ran while one was open for 0% -> 0% of each run, Pallas kernels for 10% -> 10%
where the time goes in v5:
time: 44.5 us; the launch traced here: 44.3 us
  starting transfers between devices  29.4 us (66%)
  waiting for transfers between devices  7.53 us (17%)
  Pallas kernels  6 us (13%)
  between operations  1.4 us (3%)
    ppermute x23, starting transfers between devices, pairwise(): return lax.ppermute(array, 'patch', pairs)  29.4 us
    ppermute x23, waiting for transfers between devices, pairwise(): return lax.ppermute(array, 'patch', pairs)  7.53 us
    pallas_call x1, Pallas kernels, pack(): pl.pallas_call(partial(pack_kernel, order), in_specs=[pl.BlockSpec(memory...  2.53 us
    pallas_call x1, Pallas kernels, attend_refreshed(): pl.pallas_call(partial(refreshed_kernel, order, head_dim), in_specs=[pl.B...  0.98 us
    pallas_call x1, Pallas kernels, store(): pl.pallas_call(store_kernel, in_specs=[pl.BlockSpec(memory_space=pltpu.SM...  0.89 us
  transfers between devices with their start and end apart: 23, of which 8 were waited for; matrix products, arithmetic and copies ran while one was open for 0% of the time, Pallas kernels for 10%

profile of v5, /device:TPU:0, one launch (start us, length us, event | category | flops | bytes accessed | tf_op | source)
XLA Modules:
  0.0 44.3 jit_solution(340520480161883296)
XLA Ops:
  0.6 0.5 %collective-permute-start = (bf16[2,2,384,256]{3,2,1,0:T(8,128)(2,1)}, bf16[2,2,384,256]{3,2,1,0:T(8,128)(2,1)S(1)}, u32[]{:S(2)}, u32[]{:S(2)}) collective-permute-start(bf16[2,2,384,256]{3,2,1,0:T(8,128)(2,1)} %bitcast.4), channel_id=1, source_target_pairs={{0,1},{1,0},{2,3},{3,2},{4,5},{5,4},{6,7},{7,6},{8,9},{9,8},{10,11... | collective-permute-start | bytes 2359304 | tf_op jit(solution)/shard_map/ppermute | solution.py:32
  1.8 2.5 %shard_map.77 = (bf16[24,2048]{1,0:T(8,128)(2,1)}, bf16[24,2048]{1,0:T(8,128)(2,1)}, bf16[24,2048]{1,0:T(8,128)(2,1)}, bf16[24,2048]{1,0:T(8,128)(2,1)}, bf16[24...) custom-call(s32[1]{0:T(128)S(6)} %copy.9.step_ref, ...), custom_call_target="tpu_custom_call" | custom-call | tf_op jit(solution)/shard_map/pallas_call | solution.py:114
  4.4 4.6 %collective-permute-start.1 = (bf16[24,2048]{1,0:T(8,128)(2,1)}, bf16[24,2048]{1,0:T(8,128)(2,1)S(1)}, u32[]{:S(2)}, u32[]{:S(2)}) collective-permute-start(bf16[24,2048]{1,0:T(8,128)(2,1)} %get-tuple-element.37), channel_id=1, source_target_pairs={{0,10},{1,11},{2,8},{3,9},{4,14},{5,15},{6,12},{7,13},{8,2},{9,3},... | collective-permute-start | bytes 294920 | tf_op jit(solution)/shard_map/ppermute | solution.py:32
  9.0 0.5 %collective-permute-start.2 = (bf16[24,2048]{1,0:T(8,128)(2,1)}, bf16[24,2048]{1,0:T(8,128)(2,1)S(1)}, u32[]{:S(2)}, u32[]{:S(2)}) collective-permute-start(bf16[24,2048]{1,0:T(8,128)(2,1)} %get-tuple-element.38), channel_id=1, source_target_pairs={{0,2},{1,3},{2,0},{3,1},{4,6},{5,7},{6,4},{7,5},{8,10},{9,11},{10,... | collective-permute-start | bytes 294920 | tf_op jit(solution)/shard_map/ppermute | solution.py:32
  9.5 2.5 %collective-permute-start.3 = (bf16[24,2048]{1,0:T(8,128)(2,1)}, bf16[24,2048]{1,0:T(8,128)(2,1)S(1)}, u32[]{:S(2)}, u32[]{:S(2)}) collective-permute-start(bf16[24,2048]{1,0:T(8,128)(2,1)} %get-tuple-element.39), channel_id=1, source_target_pairs={{0,6},{1,7},{2,4},{3,5},{4,2},{5,3},{6,0},{7,1},{8,14},{9,15},{10,... | collective-permute-start | bytes 294920 | tf_op jit(solution)/shard_map/ppermute | solution.py:32
  12.3 2.5 %collective-permute-start.5 = (bf16[24,2048]{1,0:T(8,128)(2,1)}, bf16[24,2048]{1,0:T(8,128)(2,1)S(1)}, u32[]{:S(2)}, u32[]{:S(2)}) collective-permute-start(bf16[24,2048]{1,0:T(8,128)(2,1)} %get-tuple-element.41), channel_id=1, source_target_pairs={{0,12},{1,13},{2,14},{3,15},{4,8},{5,9},{6,10},{7,11},{8,4},{9,5},... | collective-permute-start | bytes 294920 | tf_op jit(solution)/shard_map/ppermute | solution.py:32
  15.0 1.2 %collective-permute-start.6 = (bf16[24,2048]{1,0:T(8,128)(2,1)}, bf16[24,2048]{1,0:T(8,128)(2,1)S(1)}, u32[]{:S(2)}, u32[]{:S(2)}) collective-permute-start(bf16[24,2048]{1,0:T(8,128)(2,1)} %get-tuple-element.42), channel_id=1, source_target_pairs={{0,4},{1,5},{2,6},{3,7},{4,0},{5,1},{6,2},{7,3},{8,12},{9,13},{10,... | collective-permute-start | bytes 294920 | tf_op jit(solution)/shard_map/ppermute | solution.py:32
  16.3 3.7 %collective-permute-start.7 = (bf16[24,2048]{1,0:T(8,128)(2,1)}, bf16[24,2048]{1,0:T(8,128)(2,1)S(1)}, u32[]{:S(2)}, u32[]{:S(2)}) collective-permute-start(bf16[24,2048]{1,0:T(8,128)(2,1)} %get-tuple-element.43), channel_id=1, source_target_pairs={{0,14},{1,15},{2,12},{3,13},{4,10},{5,11},{6,8},{7,9},{8,6},{9,7},... | collective-permute-start | bytes 294920 | tf_op jit(solution)/shard_map/ppermute | solution.py:32
  20.0 3.1 %collective-permute-done.4.refs_3_ = bf16[24,2048]{1,0:T(8,128)(2,1)S(1)} collective-permute-done((bf16[24,2048]{1,0:T(8,128)(2,1)}, bf16[24,2048]{1,0:T(8,128)(2,1)S(1)}, u32[]{:S(2)}, u32[]{:S(2)}) %collective-permute-start.4) | collective-permute-done | bytes 98336 | tf_op jit(solution)/shard_map/ppermute | solution.py:32
  23.1 0.5 %collective-permute-start.9 = (bf16[24,2048]{1,0:T(8,128)(2,1)S(1)}, bf16[24,2048]{1,0:T(8,128)(2,1)S(1)}, u32[]{:S(2)}, u32[]{:S(2)}) collective-permute-start(bf16[24,2048]{1,0:T(8,128)(2,1)S(1)} %collective-permute-done.2.refs_1_), channel_id=1, source_target_pairs={{0,1},{1,0},{2,3},{3,2},{4,5},{5,4},{6,7},{7,6},{8,9},{9,8},{10,11... | collective-permute-start | bytes 294920 | tf_op jit(solution)/shard_map/ppermute | solution.py:32
  23.7 1.7 %collective-permute-done.7.refs_6_ = bf16[24,2048]{1,0:T(8,128)(2,1)S(1)} collective-permute-done((bf16[24,2048]{1,0:T(8,128)(2,1)}, bf16[24,2048]{1,0:T(8,128)(2,1)S(1)}, u32[]{:S(2)}, u32[]{:S(2)}) %collective-permute-start.7) | collective-permute-done | bytes 98336 | tf_op jit(solution)/shard_map/ppermute | solution.py:32
  25.4 0.5 %collective-permute-start.12 = (bf16[24,2048]{1,0:T(8,128)(2,1)S(1)}, bf16[24,2048]{1,0:T(8,128)(2,1)S(1)}, u32[]{:S(2)}, u32[]{:S(2)}) collective-permute-start(bf16[24,2048]{1,0:T(8,128)(2,1)S(1)} %collective-permute-done.5.refs_4_), channel_id=1, source_target_pairs={{0,1},{1,0},{2,3},{3,2},{4,5},{5,4},{6,7},{7,6},{8,9},{9,8},{10,11... | collective-permute-start | bytes 294920 | tf_op jit(solution)/shard_map/ppermute | solution.py:32
  26.4 0.8 %shard_map.78.refs_16_ = bf16[8,24,512]{2,1,0:T(8,128)(2,1)S(1)} custom-call(s32[1]{0:T(128)S(6)} %copy.9.step_ref, bf16[2,24,4096]{2,1,0:T(8,128)(2,1)S(1)} %copy-done.1, bf16[24,2048]{1,0:T(8,128)(2,1)S(1)} %collective-permute-done.1.refs_0_, bf16[24,2048]{1,0:T(8,128)(2,1)S(1)} %collective-permute-done.2.refs_1_, ...), custom_call_target="tpu_custom_call" | custom-call | tf_op jit(solution)/shard_map/pallas_call | solution.py:193
  27.4 1.0 %shard_map.79 = (bf16[24,1024]{1,0:T(8,128)(2,1)S(1)}, bf16[24,1024]{1,0:T(8,128)(2,1)S(1)}, bf16[24,1024]{1,0:T(8,128)(2,1)S(1)}, bf16[24,1024]{1,0:T(8,128)(2,...) custom-call(s32[1]{0:T(128)S(6)} %copy.9.step_ref, ...), custom_call_target="tpu_custom_call" | custom-call | tf_op jit(solution)/shard_map/pallas_call | solution.py:256
  28.4 3.9 %collective-permute-start.16 = (bf16[24,1024]{1,0:T(8,128)(2,1)S(1)}, bf16[24,1024]{1,0:T(8,128)(2,1)S(1)}, u32[]{:S(2)}, u32[]{:S(2)}) collective-permute-start(bf16[24,1024]{1,0:T(8,128)(2,1)S(1)} %get-tuple-element.46), channel_id=1, source_target_pairs={{0,14},{1,15},{2,12},{3,13},{4,10},{5,11},{6,8},{7,9},{8,6},{9,7},... | collective-permute-start | bytes 147464 | tf_op jit(solution)/shard_map/ppermute | solution.py:32
  32.2 0.7 %collective-permute-start.17 = (bf16[24,1024]{1,0:T(8,128)(2,1)S(1)}, bf16[24,1024]{1,0:T(8,128)(2,1)S(1)}, u32[]{:S(2)}, u32[]{:S(2)}) collective-permute-start(bf16[24,1024]{1,0:T(8,128)(2,1)S(1)} %get-tuple-element.47), channel_id=1, source_target_pairs={{0,12},{1,13},{2,14},{3,15},{4,8},{5,9},{6,10},{7,11},{8,4},{9,5},... | collective-permute-start | bytes 147464 | tf_op jit(solution)/shard_map/ppermute | solution.py:32
  32.9 3.1 %collective-permute-start.18 = (bf16[24,1024]{1,0:T(8,128)(2,1)S(1)}, bf16[24,1024]{1,0:T(8,128)(2,1)S(1)}, u32[]{:S(2)}, u32[]{:S(2)}) collective-permute-start(bf16[24,1024]{1,0:T(8,128)(2,1)S(1)} %get-tuple-element.48), channel_id=1, source_target_pairs={{0,10},{1,11},{2,8},{3,9},{4,14},{5,15},{6,12},{7,13},{8,2},{9,3},... | collective-permute-start | bytes 147464 | tf_op jit(solution)/shard_map/ppermute | solution.py:32
  36.1 2.3 %collective-permute-start.20 = (bf16[24,1024]{1,0:T(8,128)(2,1)S(1)}, bf16[24,1024]{1,0:T(8,128)(2,1)S(1)}, u32[]{:S(2)}, u32[]{:S(2)}) collective-permute-start(bf16[24,1024]{1,0:T(8,128)(2,1)S(1)} %get-tuple-element.50), channel_id=1, source_target_pairs={{0,6},{1,7},{2,4},{3,5},{4,2},{5,3},{6,0},{7,1},{8,14},{9,15},{10,... | collective-permute-start | bytes 147464 | tf_op jit(solution)/shard_map/ppermute | solution.py:32
  38.4 0.6 %collective-permute-start.21 = (bf16[24,1024]{1,0:T(8,128)(2,1)S(1)}, bf16[24,1024]{1,0:T(8,128)(2,1)S(1)}, u32[]{:S(2)}, u32[]{:S(2)}) collective-permute-start(bf16[24,1024]{1,0:T(8,128)(2,1)S(1)} %get-tuple-element.51), channel_id=1, source_target_pairs={{0,4},{1,5},{2,6},{3,7},{4,0},{5,1},{6,2},{7,3},{8,12},{9,13},{10,... | collective-permute-start | bytes 147464 | tf_op jit(solution)/shard_map/ppermute | solution.py:32
  39.0 1.3 %collective-permute-start.22 = (bf16[24,1024]{1,0:T(8,128)(2,1)S(1)}, bf16[24,1024]{1,0:T(8,128)(2,1)S(1)}, u32[]{:S(2)}, u32[]{:S(2)}) collective-permute-start(bf16[24,1024]{1,0:T(8,128)(2,1)S(1)} %get-tuple-element.52), channel_id=1, source_target_pairs={{0,2},{1,3},{2,0},{3,1},{4,6},{5,7},{6,4},{7,5},{8,10},{9,11},{10,... | collective-permute-start | bytes 147464 | tf_op jit(solution)/shard_map/ppermute | solution.py:32
  40.3 0.9 %shard_map.81 = bf16[2,2,384,256]{3,2,1,0:T(8,128)(2,1)} custom-call(s32[1]{0:T(128)S(6)} %copy.9.step_ref, bf16[2,2,384,256]{3,2,1,0:T(8,128)(2,1)S(1)} %bitcast.7, bf16[2,384,256]{2,1,0:T(8,128)(2,1)S(1)} %get-tuple-element.55.renewed_ref), custom_call_target="tpu_custom_call" | custom-call | tf_op jit(solution)/shard_map/pallas_call | solution.py:282
  41.2 1.3 %collective-permute-done.18.refs_2_ = bf16[24,1024]{1,0:T(8,128)(2,1)S(1)} collective-permute-done((bf16[24,1024]{1,0:T(8,128)(2,1)S(1)}, bf16[24,1024]{1,0:T(8,128)(2,1)S(1)}, u32[]{:S(2)}, u32[]{:S(2)}) %collective-permute-start.18) | collective-permute-done | bytes 49184 | tf_op jit(solution)/shard_map/ppermute | solution.py:32
  42.8 0.7 %collective-permute-done.21.refs_5_ = bf16[24,1024]{1,0:T(8,128)(2,1)S(1)} collective-permute-done((bf16[24,1024]{1,0:T(8,128)(2,1)S(1)}, bf16[24,1024]{1,0:T(8,128)(2,1)S(1)}, u32[]{:S(2)}, u32[]{:S(2)}) %collective-permute-start.21) | collective-permute-done | bytes 49184 | tf_op jit(solution)/shard_map/ppermute | solution.py:32
  43.5 0.8 %shard_map.80 = bf16[2,24,4096]{2,1,0:T(8,128)(2,1)} custom-call(s32[1]{0:T(128)S(6)} %copy.9.step_ref, bf16[24,1024]{1,0:T(8,128)(2,1)S(1)} %collective-permute-done.16.refs_0_, bf16[24,1024]{1,0:T(8,128)(2,1)S(1)} %collective-permute-done.17.refs_1_, bf16[24,1024]{1,0:T(8,128)(2,1)S(1)} %collective-permute-done.18.refs_2_, ...), custom_call_target="tpu_custom_call" | custom-call | tf_op jit(solution)/shard_map/pallas_call | solution.py:320
  (33 shorter events, 1.8 us)
Async XLA Ops:
  0.6 3.7 %collective-permute-start = (bf16[2,2,384,256]{3,2,1,0:T(8,128)(2,1)}, bf16[2,2,384,256]{3,2,1,0:T(8,128)(2,1)S(1)}, u32[]{:S(2)}, u32[]{:S(2)}) collective-permute-start(bf16[2,2,384,256]{3,2,1,0:T(8,128)(2,1)} %bitcast.4), channel_id=1, source_target_pairs={{0,1},{1,0},{2,3},{3,2},{4,5},{5,4},{6,7},{7,6},{8,9},{9,8},{10,11... | collective-permute-start | bytes 2359304 | tf_op jit(solution)/shard_map/ppermute | solution.py:32
  1.8 24.6 %copy-start = (bf16[2,2,1,16,24,256]{5,4,3,2,1,0:T(8,128)(2,1)S(1)}, bf16[2,2,1,16,24,256]{5,4,3,2,1,0:T(8,128)(2,1)}, u32[]{:S(2)}) copy-start(bf16[2,2,1,16,24,256]{5,4,3,2,1,0:T(8,128)(2,1)} %param.9) | copy-start | bytes 2359300
  4.4 10.6 %collective-permute-start.1 = (bf16[24,2048]{1,0:T(8,128)(2,1)}, bf16[24,2048]{1,0:T(8,128)(2,1)S(1)}, u32[]{:S(2)}, u32[]{:S(2)}) collective-permute-start(bf16[24,2048]{1,0:T(8,128)(2,1)} %get-tuple-element.37), channel_id=1, source_target_pairs={{0,10},{1,11},{2,8},{3,9},{4,14},{5,15},{6,12},{7,13},{8,2},{9,3},... | collective-permute-start | bytes 294920 | tf_op jit(solution)/shard_map/ppermute | solution.py:32
  9.0 7.4 %collective-permute-start.2 = (bf16[24,2048]{1,0:T(8,128)(2,1)}, bf16[24,2048]{1,0:T(8,128)(2,1)S(1)}, u32[]{:S(2)}, u32[]{:S(2)}) collective-permute-start(bf16[24,2048]{1,0:T(8,128)(2,1)} %get-tuple-element.38), channel_id=1, source_target_pairs={{0,2},{1,3},{2,0},{3,1},{4,6},{5,7},{6,4},{7,5},{8,10},{9,11},{10,... | collective-permute-start | bytes 294920 | tf_op jit(solution)/shard_map/ppermute | solution.py:32
  9.5 10.5 %collective-permute-start.3 = (bf16[24,2048]{1,0:T(8,128)(2,1)}, bf16[24,2048]{1,0:T(8,128)(2,1)S(1)}, u32[]{:S(2)}, u32[]{:S(2)}) collective-permute-start(bf16[24,2048]{1,0:T(8,128)(2,1)} %get-tuple-element.39), channel_id=1, source_target_pairs={{0,6},{1,7},{2,4},{3,5},{4,2},{5,3},{6,0},{7,1},{8,14},{9,15},{10,... | collective-permute-start | bytes 294920 | tf_op jit(solution)/shard_map/ppermute | solution.py:32
  12.0 11.1 %collective-permute-start.4 = (bf16[24,2048]{1,0:T(8,128)(2,1)}, bf16[24,2048]{1,0:T(8,128)(2,1)S(1)}, u32[]{:S(2)}, u32[]{:S(2)}) collective-permute-start(bf16[24,2048]{1,0:T(8,128)(2,1)} %get-tuple-element.40), channel_id=1, source_target_pairs={{0,8},{1,9},{2,10},{3,11},{4,12},{5,13},{6,14},{7,15},{8,0},{9,1},... | collective-permute-start | bytes 294920 | tf_op jit(solution)/shard_map/ppermute | solution.py:32
  12.3 10.8 %collective-permute-start.5 = (bf16[24,2048]{1,0:T(8,128)(2,1)}, bf16[24,2048]{1,0:T(8,128)(2,1)S(1)}, u32[]{:S(2)}, u32[]{:S(2)}) collective-permute-start(bf16[24,2048]{1,0:T(8,128)(2,1)} %get-tuple-element.41), channel_id=1, source_target_pairs={{0,12},{1,13},{2,14},{3,15},{4,8},{5,9},{6,10},{7,11},{8,4},{9,5},... | collective-permute-start | bytes 294920 | tf_op jit(solution)/shard_map/ppermute | solution.py:32
  15.0 8.7 %collective-permute-start.6 = (bf16[24,2048]{1,0:T(8,128)(2,1)}, bf16[24,2048]{1,0:T(8,128)(2,1)S(1)}, u32[]{:S(2)}, u32[]{:S(2)}) collective-permute-start(bf16[24,2048]{1,0:T(8,128)(2,1)} %get-tuple-element.42), channel_id=1, source_target_pairs={{0,4},{1,5},{2,6},{3,7},{4,0},{5,1},{6,2},{7,3},{8,12},{9,13},{10,... | collective-permute-start | bytes 294920 | tf_op jit(solution)/shard_map/ppermute | solution.py:32
  16.3 9.1 %collective-permute-start.7 = (bf16[24,2048]{1,0:T(8,128)(2,1)}, bf16[24,2048]{1,0:T(8,128)(2,1)S(1)}, u32[]{:S(2)}, u32[]{:S(2)}) collective-permute-start(bf16[24,2048]{1,0:T(8,128)(2,1)} %get-tuple-element.43), channel_id=1, source_target_pairs={{0,14},{1,15},{2,12},{3,13},{4,10},{5,11},{6,8},{7,9},{8,6},{9,7},... | collective-permute-start | bytes 294920 | tf_op jit(solution)/shard_map/ppermute | solution.py:32
  20.0 5.4 %collective-permute-start.15 = (bf16[24,2048]{1,0:T(8,128)(2,1)}, bf16[24,2048]{1,0:T(8,128)(2,1)S(1)}, u32[]{:S(2)}, u32[]{:S(2)}) collective-permute-start(bf16[24,2048]{1,0:T(8,128)(2,1)} %get-tuple-element.44.refs_7_), channel_id=1, source_target_pairs={{0,1},{1,0},{2,3},{3,2},{4,5},{5,4},{6,7},{7,6},{8,9},{9,8},{10,11... | collective-permute-start | bytes 294920 | tf_op jit(solution)/shard_map/ppermute | solution.py:32
  23.1 2.8 %collective-permute-start.8 = (bf16[24,2048]{1,0:T(8,128)(2,1)S(1)}, bf16[24,2048]{1,0:T(8,128)(2,1)S(1)}, u32[]{:S(2)}, u32[]{:S(2)}) collective-permute-start(bf16[24,2048]{1,0:T(8,128)(2,1)S(1)} %collective-permute-done.1.refs_0_), channel_id=1, source_target_pairs={{0,1},{1,0},{2,3},{3,2},{4,5},{5,4},{6,7},{7,6},{8,9},{9,8},{10,11... | collective-permute-start | bytes 294920 | tf_op jit(solution)/shard_map/ppermute | solution.py:32
  23.1 2.9 %collective-permute-start.9 = (bf16[24,2048]{1,0:T(8,128)(2,1)S(1)}, bf16[24,2048]{1,0:T(8,128)(2,1)S(1)}, u32[]{:S(2)}, u32[]{:S(2)}) collective-permute-start(bf16[24,2048]{1,0:T(8,128)(2,1)S(1)} %collective-permute-done.2.refs_1_), channel_id=1, source_target_pairs={{0,1},{1,0},{2,3},{3,2},{4,5},{5,4},{6,7},{7,6},{8,9},{9,8},{10,11... | collective-permute-start | bytes 294920 | tf_op jit(solution)/shard_map/ppermute | solution.py:32
  23.6 3.6 %collective-permute-start.10 = (bf16[24,2048]{1,0:T(8,128)(2,1)S(1)}, bf16[24,2048]{1,0:T(8,128)(2,1)S(1)}, u32[]{:S(2)}, u32[]{:S(2)}) collective-permute-start(bf16[24,2048]{1,0:T(8,128)(2,1)S(1)} %collective-permute-done.3.refs_2_), channel_id=1, source_target_pairs={{0,1},{1,0},{2,3},{3,2},{4,5},{5,4},{6,7},{7,6},{8,9},{9,8},{10,11... | collective-permute-start | bytes 294920 | tf_op jit(solution)/shard_map/ppermute | solution.py:32
  25.4 1.9 %collective-permute-start.11 = (bf16[24,2048]{1,0:T(8,128)(2,1)S(1)}, bf16[24,2048]{1,0:T(8,128)(2,1)S(1)}, u32[]{:S(2)}, u32[]{:S(2)}) collective-permute-start(bf16[24,2048]{1,0:T(8,128)(2,1)S(1)} %collective-permute-done.4.refs_3_), channel_id=1, source_target_pairs={{0,1},{1,0},{2,3},{3,2},{4,5},{5,4},{6,7},{7,6},{8,9},{9,8},{10,11... | collective-permute-start | bytes 294920 | tf_op jit(solution)/shard_map/ppermute | solution.py:32
  25.4 1.9 %collective-permute-start.12 = (bf16[24,2048]{1,0:T(8,128)(2,1)S(1)}, bf16[24,2048]{1,0:T(8,128)(2,1)S(1)}, u32[]{:S(2)}, u32[]{:S(2)}) collective-permute-start(bf16[24,2048]{1,0:T(8,128)(2,1)S(1)} %collective-permute-done.5.refs_4_), channel_id=1, source_target_pairs={{0,1},{1,0},{2,3},{3,2},{4,5},{5,4},{6,7},{7,6},{8,9},{9,8},{10,11... | collective-permute-start | bytes 294920 | tf_op jit(solution)/shard_map/ppermute | solution.py:32
  25.9 1.4 %collective-permute-start.13 = (bf16[24,2048]{1,0:T(8,128)(2,1)S(1)}, bf16[24,2048]{1,0:T(8,128)(2,1)S(1)}, u32[]{:S(2)}, u32[]{:S(2)}) collective-permute-start(bf16[24,2048]{1,0:T(8,128)(2,1)S(1)} %collective-permute-done.6.refs_5_), channel_id=1, source_target_pairs={{0,1},{1,0},{2,3},{3,2},{4,5},{5,4},{6,7},{7,6},{8,9},{9,8},{10,11... | collective-permute-start | bytes 294920 | tf_op jit(solution)/shard_map/ppermute | solution.py:32
  26.0 1.4 %collective-permute-start.14 = (bf16[24,2048]{1,0:T(8,128)(2,1)S(1)}, bf16[24,2048]{1,0:T(8,128)(2,1)S(1)}, u32[]{:S(2)}, u32[]{:S(2)}) collective-permute-start(bf16[24,2048]{1,0:T(8,128)(2,1)S(1)} %collective-permute-done.7.refs_6_), channel_id=1, source_target_pairs={{0,1},{1,0},{2,3},{3,2},{4,5},{5,4},{6,7},{7,6},{8,9},{9,8},{10,11... | collective-permute-start | bytes 294920 | tf_op jit(solution)/shard_map/ppermute | solution.py:32
  28.4 10.1 %collective-permute-start.16 = (bf16[24,1024]{1,0:T(8,128)(2,1)S(1)}, bf16[24,1024]{1,0:T(8,128)(2,1)S(1)}, u32[]{:S(2)}, u32[]{:S(2)}) collective-permute-start(bf16[24,1024]{1,0:T(8,128)(2,1)S(1)} %get-tuple-element.46), channel_id=1, source_target_pairs={{0,14},{1,15},{2,12},{3,13},{4,10},{5,11},{6,8},{7,9},{8,6},{9,7},... | collective-permute-start | bytes 147464 | tf_op jit(solution)/shard_map/ppermute | solution.py:32
  32.2 6.7 %collective-permute-start.17 = (bf16[24,1024]{1,0:T(8,128)(2,1)S(1)}, bf16[24,1024]{1,0:T(8,128)(2,1)S(1)}, u32[]{:S(2)}, u32[]{:S(2)}) collective-permute-start(bf16[24,1024]{1,0:T(8,128)(2,1)S(1)} %get-tuple-element.47), channel_id=1, source_target_pairs={{0,12},{1,13},{2,14},{3,15},{4,8},{5,9},{6,10},{7,11},{8,4},{9,5},... | collective-permute-start | bytes 147464 | tf_op jit(solution)/shard_map/ppermute | solution.py:32
  32.9 9.5 %collective-permute-start.18 = (bf16[24,1024]{1,0:T(8,128)(2,1)S(1)}, bf16[24,1024]{1,0:T(8,128)(2,1)S(1)}, u32[]{:S(2)}, u32[]{:S(2)}) collective-permute-start(bf16[24,1024]{1,0:T(8,128)(2,1)S(1)} %get-tuple-element.48), channel_id=1, source_target_pairs={{0,10},{1,11},{2,8},{3,9},{4,14},{5,15},{6,12},{7,13},{8,2},{9,3},... | collective-permute-start | bytes 147464 | tf_op jit(solution)/shard_map/ppermute | solution.py:32
  36.0 6.8 %collective-permute-start.19 = (bf16[24,1024]{1,0:T(8,128)(2,1)S(1)}, bf16[24,1024]{1,0:T(8,128)(2,1)S(1)}, u32[]{:S(2)}, u32[]{:S(2)}) collective-permute-start(bf16[24,1024]{1,0:T(8,128)(2,1)S(1)} %get-tuple-element.49), channel_id=1, source_target_pairs={{0,8},{1,9},{2,10},{3,11},{4,12},{5,13},{6,14},{7,15},{8,0},{9,1},... | collective-permute-start | bytes 147464 | tf_op jit(solution)/shard_map/ppermute | solution.py:32
  36.1 6.7 %collective-permute-start.20 = (bf16[24,1024]{1,0:T(8,128)(2,1)S(1)}, bf16[24,1024]{1,0:T(8,128)(2,1)S(1)}, u32[]{:S(2)}, u32[]{:S(2)}) collective-permute-start(bf16[24,1024]{1,0:T(8,128)(2,1)S(1)} %get-tuple-element.50), channel_id=1, source_target_pairs={{0,6},{1,7},{2,4},{3,5},{4,2},{5,3},{6,0},{7,1},{8,14},{9,15},{10,... | collective-permute-start | bytes 147464 | tf_op jit(solution)/shard_map/ppermute | solution.py:32
  38.4 5.1 %collective-permute-start.21 = (bf16[24,1024]{1,0:T(8,128)(2,1)S(1)}, bf16[24,1024]{1,0:T(8,128)(2,1)S(1)}, u32[]{:S(2)}, u32[]{:S(2)}) collective-permute-start(bf16[24,1024]{1,0:T(8,128)(2,1)S(1)} %get-tuple-element.51), channel_id=1, source_target_pairs={{0,4},{1,5},{2,6},{3,7},{4,0},{5,1},{6,2},{7,3},{8,12},{9,13},{10,... | collective-permute-start | bytes 147464 | tf_op jit(solution)/shard_map/ppermute | solution.py:32
  39.0 4.5 %collective-permute-start.22 = (bf16[24,1024]{1,0:T(8,128)(2,1)S(1)}, bf16[24,1024]{1,0:T(8,128)(2,1)S(1)}, u32[]{:S(2)}, u32[]{:S(2)}) collective-permute-start(bf16[24,1024]{1,0:T(8,128)(2,1)S(1)} %get-tuple-element.52), channel_id=1, source_target_pairs={{0,2},{1,3},{2,0},{3,1},{4,6},{5,7},{6,4},{7,5},{8,10},{9,11},{10,... | collective-permute-start | bytes 147464 | tf_op jit(solution)/shard_map/ppermute | solution.py:32
  (2 other events, 47.6 us)

commit v6 on v5

--- a/solution.py
+++ b/solution.py
@@ -46,7 +46,7 @@
 def pack_kernel(order, step_ref, query_ref, current_ref, earlier_ref, exponent_ref, *refs):
     chips = len(order)
     messages = refs[:chips]
-    queries, current, earlier, exponents, limits, packed, sems, side_sems, out_sems = refs[chips:]
+    queries, current, earlier, exponents, limits, sems, side_sems = refs[chips:]
     _, _, channel_count = query_ref.shape
     head_count = exponent_ref.shape[-1]
     head_dim = channel_count // head_count
@@ -59,19 +59,14 @@
             pltpu.make_async_copy(query_ref, queries, sems.at[1]),
         ]
     )
-    side_copies = [
-        start_all(
-            [
-                pltpu.make_async_copy(
-                    source.at[refreshed, side], target.at[side], side_sems.at[side, index]
-                )
-                for index, (source, target) in enumerate(
-                    ((current_ref, current), (earlier_ref, earlier))
-                )
-            ]
-        )
-        for side in range(2)
-    ]
+    pair_copies = start_all(
+        [
+            pltpu.make_async_copy(source.at[refreshed], target, side_sems.at[index])
+            for index, (source, target) in enumerate(
+                ((current_ref, current), (earlier_ref, earlier))
+            )
+        ]
+    )
     copies[0].wait()
     for side in range(2):
         values = block_limits(exponents[side])
@@ -86,23 +81,17 @@
     ]
     for chip, span in zip(order, spans):
         for slot, layer in enumerate((kept, refreshed)):
-            packed[chip, :, slot * width : (slot + 1) * width] = queries[layer, :, span]
-    out_copies = []
+            messages[chip][:, slot * width : (slot + 1) * width] = queries[layer, :, span]
     for side in range(2):
-        wait_all(side_copies[side])
+        if side == 0:
+            wait_all(pair_copies)
         for chip, span in zip(order, spans):
             residual = current[side, :, span].astype(jnp.float32) - earlier[
                 side, :, span
             ].astype(jnp.float32)
             limit = limits[side, :, span]
             update = jnp.minimum(jnp.maximum(residual, -limit), limit).astype(jnp.bfloat16)
-            packed[chip, :, (2 + side) * width : (3 + side) * width] = update
-            if side == 1:
-                out_copies.append(
-                    pltpu.make_async_copy(packed.at[chip], messages[chip], out_sems.at[chip])
-                )
-                out_copies[-1].start()
-    wait_all(out_copies)
+            messages[chip][:, (2 + side) * width : (3 + side) * width] = update
 
 
 def pack(step_index, queries, current_pairs, earlier_pairs, block_exponents, order):
@@ -114,16 +103,14 @@
     return pl.pallas_call(
         partial(pack_kernel, order),
         in_specs=[pl.BlockSpec(memory_space=pltpu.SMEM)] + [far] * 4,
-        out_specs=[far] * chips,
+        out_specs=[pl.BlockSpec(memory_space=pltpu.VMEM)] * chips,
         out_shape=[jax.ShapeDtypeStruct((token_count, columns), jnp.bfloat16)] * chips,
         scratch_shapes=[pltpu.VMEM(queries.shape, queries.dtype)]
         + [pltpu.VMEM(array.shape[1:], array.dtype) for array in layers]
         + [
             pltpu.VMEM(current_pairs.shape[1:], jnp.float32),
-            pltpu.VMEM((chips, token_count, columns), jnp.bfloat16),
             pltpu.SemaphoreType.DMA((2,)),
-            pltpu.SemaphoreType.DMA((2, 2)),
-            pltpu.SemaphoreType.DMA((chips,)),
+            pltpu.SemaphoreType.DMA((2,)),
         ],
         compiler_params=pltpu.CompilerParams(vmem_limit_bytes=PACK_BYTES),
     )(step_index, queries, current_pairs, earlier_pairs, block_exponents)

time: 44.5 us -> 44.3 us (level)
  transfers between devices with their start and end apart: 23 -> 23, of which waited for: 8 -> 8; matrix products, arithmetic and copies ran while one was open for 0% -> 0% of each run, Pallas kernels for 10% -> 9%
where the time goes in v6:
time: 44.3 us; the launch traced here: 44.1 us
  starting transfers between devices  29.4 us (66%)
  waiting for transfers between devices  7.54 us (17%)
  Pallas kernels  5.8 us (13%)
  between operations  1.4 us (3%)
    ppermute x23, starting transfers between devices, pairwise(): return lax.ppermute(array, 'patch', pairs)  29.4 us
    ppermute x23, waiting for transfers between devices, pairwise(): return lax.ppermute(array, 'patch', pairs)  7.54 us
    pallas_call x1, Pallas kernels, pack(): pl.pallas_call(partial(pack_kernel, order), in_specs=[pl.BlockSpec(memory...  2.32 us
    pallas_call x1, Pallas kernels, attend_refreshed(): pl.pallas_call(partial(refreshed_kernel, order, head_dim), in_specs=[pl.B...  0.99 us
    pallas_call x1, Pallas kernels, store(): pl.pallas_call(store_kernel, in_specs=[pl.BlockSpec(memory_space=pltpu.SM...  0.89 us
  transfers between devices with their start and end apart: 23, of which 8 were waited for; matrix products, arithmetic and copies ran while one was open for 0% of the time, Pallas kernels for 9%

profile of v6, /device:TPU:0, one launch (start us, length us, event | category | flops | bytes accessed | tf_op | source)
XLA Modules:
  0.0 44.1 jit_solution(11511052311645135606)
XLA Ops:
  0.6 0.5 %collective-permute-start = (bf16[2,2,384,256]{3,2,1,0:T(8,128)(2,1)}, bf16[2,2,384,256]{3,2,1,0:T(8,128)(2,1)S(1)}, u32[]{:S(2)}, u32[]{:S(2)}) collective-permute-start(bf16[2,2,384,256]{3,2,1,0:T(8,128)(2,1)} %bitcast.4), channel_id=1, source_target_pairs={{0,1},{1,0},{2,3},{3,2},{4,5},{5,4},{6,7},{7,6},{8,9},{9,8},{10,11... | collective-permute-start | bytes 2359304 | tf_op jit(solution)/shard_map/ppermute | solution.py:32
  1.8 2.3 %shard_map.77 = (bf16[24,2048]{1,0:T(8,128)(2,1)}, bf16[24,2048]{1,0:T(8,128)(2,1)}, bf16[24,2048]{1,0:T(8,128)(2,1)}, bf16[24,2048]{1,0:T(8,128)(2,1)}, bf16[24...) custom-call(s32[1]{0:T(128)S(6)} %copy.9.step_ref, ...), custom_call_target="tpu_custom_call" | custom-call | tf_op jit(solution)/shard_map/pallas_call | solution.py:103
  4.2 4.6 %collective-permute-start.1 = (bf16[24,2048]{1,0:T(8,128)(2,1)}, bf16[24,2048]{1,0:T(8,128)(2,1)S(1)}, u32[]{:S(2)}, u32[]{:S(2)}) collective-permute-start(bf16[24,2048]{1,0:T(8,128)(2,1)} %get-tuple-element.37), channel_id=1, source_target_pairs={{0,10},{1,11},{2,8},{3,9},{4,14},{5,15},{6,12},{7,13},{8,2},{9,3},... | collective-permute-start | bytes 294920 | tf_op jit(solution)/shard_map/ppermute | solution.py:32
  8.8 0.5 %collective-permute-start.2 = (bf16[24,2048]{1,0:T(8,128)(2,1)}, bf16[24,2048]{1,0:T(8,128)(2,1)S(1)}, u32[]{:S(2)}, u32[]{:S(2)}) collective-permute-start(bf16[24,2048]{1,0:T(8,128)(2,1)} %get-tuple-element.38), channel_id=1, source_target_pairs={{0,2},{1,3},{2,0},{3,1},{4,6},{5,7},{6,4},{7,5},{8,10},{9,11},{10,... | collective-permute-start | bytes 294920 | tf_op jit(solution)/shard_map/ppermute | solution.py:32
  9.3 2.5 %collective-permute-start.3 = (bf16[24,2048]{1,0:T(8,128)(2,1)}, bf16[24,2048]{1,0:T(8,128)(2,1)S(1)}, u32[]{:S(2)}, u32[]{:S(2)}) collective-permute-start(bf16[24,2048]{1,0:T(8,128)(2,1)} %get-tuple-element.39), channel_id=1, source_target_pairs={{0,6},{1,7},{2,4},{3,5},{4,2},{5,3},{6,0},{7,1},{8,14},{9,15},{10,... | collective-permute-start | bytes 294920 | tf_op jit(solution)/shard_map/ppermute | solution.py:32
  12.1 2.5 %collective-permute-start.5 = (bf16[24,2048]{1,0:T(8,128)(2,1)}, bf16[24,2048]{1,0:T(8,128)(2,1)S(1)}, u32[]{:S(2)}, u32[]{:S(2)}) collective-permute-start(bf16[24,2048]{1,0:T(8,128)(2,1)} %get-tuple-element.41), channel_id=1, source_target_pairs={{0,12},{1,13},{2,14},{3,15},{4,8},{5,9},{6,10},{7,11},{8,4},{9,5},... | collective-permute-start | bytes 294920 | tf_op jit(solution)/shard_map/ppermute | solution.py:32
  14.7 1.2 %collective-permute-start.6 = (bf16[24,2048]{1,0:T(8,128)(2,1)}, bf16[24,2048]{1,0:T(8,128)(2,1)S(1)}, u32[]{:S(2)}, u32[]{:S(2)}) collective-permute-start(bf16[24,2048]{1,0:T(8,128)(2,1)} %get-tuple-element.42), channel_id=1, source_target_pairs={{0,4},{1,5},{2,6},{3,7},{4,0},{5,1},{6,2},{7,3},{8,12},{9,13},{10,... | collective-permute-start | bytes 294920 | tf_op jit(solution)/shard_map/ppermute | solution.py:32
  16.1 3.7 %collective-permute-start.7 = (bf16[24,2048]{1,0:T(8,128)(2,1)}, bf16[24,2048]{1,0:T(8,128)(2,1)S(1)}, u32[]{:S(2)}, u32[]{:S(2)}) collective-permute-start(bf16[24,2048]{1,0:T(8,128)(2,1)} %get-tuple-element.43), channel_id=1, source_target_pairs={{0,14},{1,15},{2,12},{3,13},{4,10},{5,11},{6,8},{7,9},{8,6},{9,7},... | collective-permute-start | bytes 294920 | tf_op jit(solution)/shard_map/ppermute | solution.py:32
  19.8 3.1 %collective-permute-done.4.refs_3_ = bf16[24,2048]{1,0:T(8,128)(2,1)S(1)} collective-permute-done((bf16[24,2048]{1,0:T(8,128)(2,1)}, bf16[24,2048]{1,0:T(8,128)(2,1)S(1)}, u32[]{:S(2)}, u32[]{:S(2)}) %collective-permute-start.4) | collective-permute-done | bytes 98336 | tf_op jit(solution)/shard_map/ppermute | solution.py:32
  22.9 0.5 %collective-permute-start.9 = (bf16[24,2048]{1,0:T(8,128)(2,1)S(1)}, bf16[24,2048]{1,0:T(8,128)(2,1)S(1)}, u32[]{:S(2)}, u32[]{:S(2)}) collective-permute-start(bf16[24,2048]{1,0:T(8,128)(2,1)S(1)} %collective-permute-done.2.refs_1_), channel_id=1, source_target_pairs={{0,1},{1,0},{2,3},{3,2},{4,5},{5,4},{6,7},{7,6},{8,9},{9,8},{10,11... | collective-permute-start | bytes 294920 | tf_op jit(solution)/shard_map/ppermute | solution.py:32
  23.5 1.7 %collective-permute-done.7.refs_6_ = bf16[24,2048]{1,0:T(8,128)(2,1)S(1)} collective-permute-done((bf16[24,2048]{1,0:T(8,128)(2,1)}, bf16[24,2048]{1,0:T(8,128)(2,1)S(1)}, u32[]{:S(2)}, u32[]{:S(2)}) %collective-permute-start.7) | collective-permute-done | bytes 98336 | tf_op jit(solution)/shard_map/ppermute | solution.py:32
  25.2 0.5 %collective-permute-start.12 = (bf16[24,2048]{1,0:T(8,128)(2,1)S(1)}, bf16[24,2048]{1,0:T(8,128)(2,1)S(1)}, u32[]{:S(2)}, u32[]{:S(2)}) collective-permute-start(bf16[24,2048]{1,0:T(8,128)(2,1)S(1)} %collective-permute-done.5.refs_4_), channel_id=1, source_target_pairs={{0,1},{1,0},{2,3},{3,2},{4,5},{5,4},{6,7},{7,6},{8,9},{9,8},{10,11... | collective-permute-start | bytes 294920 | tf_op jit(solution)/shard_map/ppermute | solution.py:32
  26.2 0.8 %shard_map.78.refs_16_ = bf16[8,24,512]{2,1,0:T(8,128)(2,1)S(1)} custom-call(s32[1]{0:T(128)S(6)} %copy.9.step_ref, bf16[2,24,4096]{2,1,0:T(8,128)(2,1)S(1)} %copy-done.1, bf16[24,2048]{1,0:T(8,128)(2,1)S(1)} %collective-permute-done.1.refs_0_, bf16[24,2048]{1,0:T(8,128)(2,1)S(1)} %collective-permute-done.2.refs_1_, ...), custom_call_target="tpu_custom_call" | custom-call | tf_op jit(solution)/shard_map/pallas_call | solution.py:180
  27.2 1.0 %shard_map.79 = (bf16[24,1024]{1,0:T(8,128)(2,1)S(1)}, bf16[24,1024]{1,0:T(8,128)(2,1)S(1)}, bf16[24,1024]{1,0:T(8,128)(2,1)S(1)}, bf16[24,1024]{1,0:T(8,128)(2,...) custom-call(s32[1]{0:T(128)S(6)} %copy.9.step_ref, ...), custom_call_target="tpu_custom_call" | custom-call | tf_op jit(solution)/shard_map/pallas_call | solution.py:243
  28.2 3.9 %collective-permute-start.16 = (bf16[24,1024]{1,0:T(8,128)(2,1)S(1)}, bf16[24,1024]{1,0:T(8,128)(2,1)S(1)}, u32[]{:S(2)}, u32[]{:S(2)}) collective-permute-start(bf16[24,1024]{1,0:T(8,128)(2,1)S(1)} %get-tuple-element.46), channel_id=1, source_target_pairs={{0,14},{1,15},{2,12},{3,13},{4,10},{5,11},{6,8},{7,9},{8,6},{9,7},... | collective-permute-start | bytes 147464 | tf_op jit(solution)/shard_map/ppermute | solution.py:32
  32.0 0.7 %collective-permute-start.17 = (bf16[24,1024]{1,0:T(8,128)(2,1)S(1)}, bf16[24,1024]{1,0:T(8,128)(2,1)S(1)}, u32[]{:S(2)}, u32[]{:S(2)}) collective-permute-start(bf16[24,1024]{1,0:T(8,128)(2,1)S(1)} %get-tuple-element.47), channel_id=1, source_target_pairs={{0,12},{1,13},{2,14},{3,15},{4,8},{5,9},{6,10},{7,11},{8,4},{9,5},... | collective-permute-start | bytes 147464 | tf_op jit(solution)/shard_map/ppermute | solution.py:32
  32.7 3.1 %collective-permute-start.18 = (bf16[24,1024]{1,0:T(8,128)(2,1)S(1)}, bf16[24,1024]{1,0:T(8,128)(2,1)S(1)}, u32[]{:S(2)}, u32[]{:S(2)}) collective-permute-start(bf16[24,1024]{1,0:T(8,128)(2,1)S(1)} %get-tuple-element.48), channel_id=1, source_target_pairs={{0,10},{1,11},{2,8},{3,9},{4,14},{5,15},{6,12},{7,13},{8,2},{9,3},... | collective-permute-start | bytes 147464 | tf_op jit(solution)/shard_map/ppermute | solution.py:32
  35.9 2.3 %collective-permute-start.20 = (bf16[24,1024]{1,0:T(8,128)(2,1)S(1)}, bf16[24,1024]{1,0:T(8,128)(2,1)S(1)}, u32[]{:S(2)}, u32[]{:S(2)}) collective-permute-start(bf16[24,1024]{1,0:T(8,128)(2,1)S(1)} %get-tuple-element.50), channel_id=1, source_target_pairs={{0,6},{1,7},{2,4},{3,5},{4,2},{5,3},{6,0},{7,1},{8,14},{9,15},{10,... | collective-permute-start | bytes 147464 | tf_op jit(solution)/shard_map/ppermute | solution.py:32
  38.2 0.5 %collective-permute-start.21 = (bf16[24,1024]{1,0:T(8,128)(2,1)S(1)}, bf16[24,1024]{1,0:T(8,128)(2,1)S(1)}, u32[]{:S(2)}, u32[]{:S(2)}) collective-permute-start(bf16[24,1024]{1,0:T(8,128)(2,1)S(1)} %get-tuple-element.51), channel_id=1, source_target_pairs={{0,4},{1,5},{2,6},{3,7},{4,0},{5,1},{6,2},{7,3},{8,12},{9,13},{10,... | collective-permute-start | bytes 147464 | tf_op jit(solution)/shard_map/ppermute | solution.py:32
  38.8 1.3 %collective-permute-start.22 = (bf16[24,1024]{1,0:T(8,128)(2,1)S(1)}, bf16[24,1024]{1,0:T(8,128)(2,1)S(1)}, u32[]{:S(2)}, u32[]{:S(2)}) collective-permute-start(bf16[24,1024]{1,0:T(8,128)(2,1)S(1)} %get-tuple-element.52), channel_id=1, source_target_pairs={{0,2},{1,3},{2,0},{3,1},{4,6},{5,7},{6,4},{7,5},{8,10},{9,11},{10,... | collective-permute-start | bytes 147464 | tf_op jit(solution)/shard_map/ppermute | solution.py:32
  40.1 0.9 %shard_map.81 = bf16[2,2,384,256]{3,2,1,0:T(8,128)(2,1)} custom-call(s32[1]{0:T(128)S(6)} %copy.9.step_ref, bf16[2,2,384,256]{3,2,1,0:T(8,128)(2,1)S(1)} %bitcast.7, bf16[2,384,256]{2,1,0:T(8,128)(2,1)S(1)} %get-tuple-element.55.renewed_ref), custom_call_target="tpu_custom_call" | custom-call | tf_op jit(solution)/shard_map/pallas_call | solution.py:269
  41.0 1.3 %collective-permute-done.18.refs_2_ = bf16[24,1024]{1,0:T(8,128)(2,1)S(1)} collective-permute-done((bf16[24,1024]{1,0:T(8,128)(2,1)S(1)}, bf16[24,1024]{1,0:T(8,128)(2,1)S(1)}, u32[]{:S(2)}, u32[]{:S(2)}) %collective-permute-start.18) | collective-permute-done | bytes 49184 | tf_op jit(solution)/shard_map/ppermute | solution.py:32
  42.6 0.7 %collective-permute-done.21.refs_5_ = bf16[24,1024]{1,0:T(8,128)(2,1)S(1)} collective-permute-done((bf16[24,1024]{1,0:T(8,128)(2,1)S(1)}, bf16[24,1024]{1,0:T(8,128)(2,1)S(1)}, u32[]{:S(2)}, u32[]{:S(2)}) %collective-permute-start.21) | collective-permute-done | bytes 49184 | tf_op jit(solution)/shard_map/ppermute | solution.py:32
  43.3 0.8 %shard_map.80 = bf16[2,24,4096]{2,1,0:T(8,128)(2,1)} custom-call(s32[1]{0:T(128)S(6)} %copy.9.step_ref, bf16[24,1024]{1,0:T(8,128)(2,1)S(1)} %collective-permute-done.16.refs_0_, bf16[24,1024]{1,0:T(8,128)(2,1)S(1)} %collective-permute-done.17.refs_1_, bf16[24,1024]{1,0:T(8,128)(2,1)S(1)} %collective-permute-done.18.refs_2_, ...), custom_call_target="tpu_custom_call" | custom-call | tf_op jit(solution)/shard_map/pallas_call | solution.py:307
  (33 shorter events, 1.8 us)
Async XLA Ops:
  0.6 3.5 %collective-permute-start = (bf16[2,2,384,256]{3,2,1,0:T(8,128)(2,1)}, bf16[2,2,384,256]{3,2,1,0:T(8,128)(2,1)S(1)}, u32[]{:S(2)}, u32[]{:S(2)}) collective-permute-start(bf16[2,2,384,256]{3,2,1,0:T(8,128)(2,1)} %bitcast.4), channel_id=1, source_target_pairs={{0,1},{1,0},{2,3},{3,2},{4,5},{5,4},{6,7},{7,6},{8,9},{9,8},{10,11... | collective-permute-start | bytes 2359304 | tf_op jit(solution)/shard_map/ppermute | solution.py:32
  1.8 24.4 %copy-start = (bf16[2,2,1,16,24,256]{5,4,3,2,1,0:T(8,128)(2,1)S(1)}, bf16[2,2,1,16,24,256]{5,4,3,2,1,0:T(8,128)(2,1)}, u32[]{:S(2)}) copy-start(bf16[2,2,1,16,24,256]{5,4,3,2,1,0:T(8,128)(2,1)} %param.9) | copy-start | bytes 2359300
  4.2 10.6 %collective-permute-start.1 = (bf16[24,2048]{1,0:T(8,128)(2,1)}, bf16[24,2048]{1,0:T(8,128)(2,1)S(1)}, u32[]{:S(2)}, u32[]{:S(2)}) collective-permute-start(bf16[24,2048]{1,0:T(8,128)(2,1)} %get-tuple-element.37), channel_id=1, source_target_pairs={{0,10},{1,11},{2,8},{3,9},{4,14},{5,15},{6,12},{7,13},{8,2},{9,3},... | collective-permute-start | bytes 294920 | tf_op jit(solution)/shard_map/ppermute | solution.py:32
  8.8 7.4 %collective-permute-start.2 = (bf16[24,2048]{1,0:T(8,128)(2,1)}, bf16[24,2048]{1,0:T(8,128)(2,1)S(1)}, u32[]{:S(2)}, u32[]{:S(2)}) collective-permute-start(bf16[24,2048]{1,0:T(8,128)(2,1)} %get-tuple-element.38), channel_id=1, source_target_pairs={{0,2},{1,3},{2,0},{3,1},{4,6},{5,7},{6,4},{7,5},{8,10},{9,11},{10,... | collective-permute-start | bytes 294920 | tf_op jit(solution)/shard_map/ppermute | solution.py:32
  9.3 10.5 %collective-permute-start.3 = (bf16[24,2048]{1,0:T(8,128)(2,1)}, bf16[24,2048]{1,0:T(8,128)(2,1)S(1)}, u32[]{:S(2)}, u32[]{:S(2)}) collective-permute-start(bf16[24,2048]{1,0:T(8,128)(2,1)} %get-tuple-element.39), channel_id=1, source_target_pairs={{0,6},{1,7},{2,4},{3,5},{4,2},{5,3},{6,0},{7,1},{8,14},{9,15},{10,... | collective-permute-start | bytes 294920 | tf_op jit(solution)/shard_map/ppermute | solution.py:32
  11.8 11.1 %collective-permute-start.4 = (bf16[24,2048]{1,0:T(8,128)(2,1)}, bf16[24,2048]{1,0:T(8,128)(2,1)S(1)}, u32[]{:S(2)}, u32[]{:S(2)}) collective-permute-start(bf16[24,2048]{1,0:T(8,128)(2,1)} %get-tuple-element.40), channel_id=1, source_target_pairs={{0,8},{1,9},{2,10},{3,11},{4,12},{5,13},{6,14},{7,15},{8,0},{9,1},... | collective-permute-start | bytes 294920 | tf_op jit(solution)/shard_map/ppermute | solution.py:32
  12.1 10.8 %collective-permute-start.5 = (bf16[24,2048]{1,0:T(8,128)(2,1)}, bf16[24,2048]{1,0:T(8,128)(2,1)S(1)}, u32[]{:S(2)}, u32[]{:S(2)}) collective-permute-start(bf16[24,2048]{1,0:T(8,128)(2,1)} %get-tuple-element.41), channel_id=1, source_target_pairs={{0,12},{1,13},{2,14},{3,15},{4,8},{5,9},{6,10},{7,11},{8,4},{9,5},... | collective-permute-start | bytes 294920 | tf_op jit(solution)/shard_map/ppermute | solution.py:32
  14.7 8.7 %collective-permute-start.6 = (bf16[24,2048]{1,0:T(8,128)(2,1)}, bf16[24,2048]{1,0:T(8,128)(2,1)S(1)}, u32[]{:S(2)}, u32[]{:S(2)}) collective-permute-start(bf16[24,2048]{1,0:T(8,128)(2,1)} %get-tuple-element.42), channel_id=1, source_target_pairs={{0,4},{1,5},{2,6},{3,7},{4,0},{5,1},{6,2},{7,3},{8,12},{9,13},{10,... | collective-permute-start | bytes 294920 | tf_op jit(solution)/shard_map/ppermute | solution.py:32
  16.1 9.0 %collective-permute-start.7 = (bf16[24,2048]{1,0:T(8,128)(2,1)}, bf16[24,2048]{1,0:T(8,128)(2,1)S(1)}, u32[]{:S(2)}, u32[]{:S(2)}) collective-permute-start(bf16[24,2048]{1,0:T(8,128)(2,1)} %get-tuple-element.43), channel_id=1, source_target_pairs={{0,14},{1,15},{2,12},{3,13},{4,10},{5,11},{6,8},{7,9},{8,6},{9,7},... | collective-permute-start | bytes 294920 | tf_op jit(solution)/shard_map/ppermute | solution.py:32
  19.8 5.4 %collective-permute-start.15 = (bf16[24,2048]{1,0:T(8,128)(2,1)}, bf16[24,2048]{1,0:T(8,128)(2,1)S(1)}, u32[]{:S(2)}, u32[]{:S(2)}) collective-permute-start(bf16[24,2048]{1,0:T(8,128)(2,1)} %get-tuple-element.44.refs_7_), channel_id=1, source_target_pairs={{0,1},{1,0},{2,3},{3,2},{4,5},{5,4},{6,7},{7,6},{8,9},{9,8},{10,11... | collective-permute-start | bytes 294920 | tf_op jit(solution)/shard_map/ppermute | solution.py:32
  22.9 2.8 %collective-permute-start.8 = (bf16[24,2048]{1,0:T(8,128)(2,1)S(1)}, bf16[24,2048]{1,0:T(8,128)(2,1)S(1)}, u32[]{:S(2)}, u32[]{:S(2)}) collective-permute-start(bf16[24,2048]{1,0:T(8,128)(2,1)S(1)} %collective-permute-done.1.refs_0_), channel_id=1, source_target_pairs={{0,1},{1,0},{2,3},{3,2},{4,5},{5,4},{6,7},{7,6},{8,9},{9,8},{10,11... | collective-permute-start | bytes 294920 | tf_op jit(solution)/shard_map/ppermute | solution.py:32
  22.9 2.9 %collective-permute-start.9 = (bf16[24,2048]{1,0:T(8,128)(2,1)S(1)}, bf16[24,2048]{1,0:T(8,128)(2,1)S(1)}, u32[]{:S(2)}, u32[]{:S(2)}) collective-permute-start(bf16[24,2048]{1,0:T(8,128)(2,1)S(1)} %collective-permute-done.2.refs_1_), channel_id=1, source_target_pairs={{0,1},{1,0},{2,3},{3,2},{4,5},{5,4},{6,7},{7,6},{8,9},{9,8},{10,11... | collective-permute-start | bytes 294920 | tf_op jit(solution)/shard_map/ppermute | solution.py:32
  23.4 3.6 %collective-permute-start.10 = (bf16[24,2048]{1,0:T(8,128)(2,1)S(1)}, bf16[24,2048]{1,0:T(8,128)(2,1)S(1)}, u32[]{:S(2)}, u32[]{:S(2)}) collective-permute-start(bf16[24,2048]{1,0:T(8,128)(2,1)S(1)} %collective-permute-done.3.refs_2_), channel_id=1, source_target_pairs={{0,1},{1,0},{2,3},{3,2},{4,5},{5,4},{6,7},{7,6},{8,9},{9,8},{10,11... | collective-permute-start | bytes 294920 | tf_op jit(solution)/shard_map/ppermute | solution.py:32
  25.2 1.9 %collective-permute-start.11 = (bf16[24,2048]{1,0:T(8,128)(2,1)S(1)}, bf16[24,2048]{1,0:T(8,128)(2,1)S(1)}, u32[]{:S(2)}, u32[]{:S(2)}) collective-permute-start(bf16[24,2048]{1,0:T(8,128)(2,1)S(1)} %collective-permute-done.4.refs_3_), channel_id=1, source_target_pairs={{0,1},{1,0},{2,3},{3,2},{4,5},{5,4},{6,7},{7,6},{8,9},{9,8},{10,11... | collective-permute-start | bytes 294920 | tf_op jit(solution)/shard_map/ppermute | solution.py:32
  25.2 1.9 %collective-permute-start.12 = (bf16[24,2048]{1,0:T(8,128)(2,1)S(1)}, bf16[24,2048]{1,0:T(8,128)(2,1)S(1)}, u32[]{:S(2)}, u32[]{:S(2)}) collective-permute-start(bf16[24,2048]{1,0:T(8,128)(2,1)S(1)} %collective-permute-done.5.refs_4_), channel_id=1, source_target_pairs={{0,1},{1,0},{2,3},{3,2},{4,5},{5,4},{6,7},{7,6},{8,9},{9,8},{10,11... | collective-permute-start | bytes 294920 | tf_op jit(solution)/shard_map/ppermute | solution.py:32
  25.7 1.4 %collective-permute-start.13 = (bf16[24,2048]{1,0:T(8,128)(2,1)S(1)}, bf16[24,2048]{1,0:T(8,128)(2,1)S(1)}, u32[]{:S(2)}, u32[]{:S(2)}) collective-permute-start(bf16[24,2048]{1,0:T(8,128)(2,1)S(1)} %collective-permute-done.6.refs_5_), channel_id=1, source_target_pairs={{0,1},{1,0},{2,3},{3,2},{4,5},{5,4},{6,7},{7,6},{8,9},{9,8},{10,11... | collective-permute-start | bytes 294920 | tf_op jit(solution)/shard_map/ppermute | solution.py:32
  25.8 1.4 %collective-permute-start.14 = (bf16[24,2048]{1,0:T(8,128)(2,1)S(1)}, bf16[24,2048]{1,0:T(8,128)(2,1)S(1)}, u32[]{:S(2)}, u32[]{:S(2)}) collective-permute-start(bf16[24,2048]{1,0:T(8,128)(2,1)S(1)} %collective-permute-done.7.refs_6_), channel_id=1, source_target_pairs={{0,1},{1,0},{2,3},{3,2},{4,5},{5,4},{6,7},{7,6},{8,9},{9,8},{10,11... | collective-permute-start | bytes 294920 | tf_op jit(solution)/shard_map/ppermute | solution.py:32
  28.2 10.0 %collective-permute-start.16 = (bf16[24,1024]{1,0:T(8,128)(2,1)S(1)}, bf16[24,1024]{1,0:T(8,128)(2,1)S(1)}, u32[]{:S(2)}, u32[]{:S(2)}) collective-permute-start(bf16[24,1024]{1,0:T(8,128)(2,1)S(1)} %get-tuple-element.46), channel_id=1, source_target_pairs={{0,14},{1,15},{2,12},{3,13},{4,10},{5,11},{6,8},{7,9},{8,6},{9,7},... | collective-permute-start | bytes 147464 | tf_op jit(solution)/shard_map/ppermute | solution.py:32
  32.0 6.7 %collective-permute-start.17 = (bf16[24,1024]{1,0:T(8,128)(2,1)S(1)}, bf16[24,1024]{1,0:T(8,128)(2,1)S(1)}, u32[]{:S(2)}, u32[]{:S(2)}) collective-permute-start(bf16[24,1024]{1,0:T(8,128)(2,1)S(1)} %get-tuple-element.47), channel_id=1, source_target_pairs={{0,12},{1,13},{2,14},{3,15},{4,8},{5,9},{6,10},{7,11},{8,4},{9,5},... | collective-permute-start | bytes 147464 | tf_op jit(solution)/shard_map/ppermute | solution.py:32
  32.7 9.5 %collective-permute-start.18 = (bf16[24,1024]{1,0:T(8,128)(2,1)S(1)}, bf16[24,1024]{1,0:T(8,128)(2,1)S(1)}, u32[]{:S(2)}, u32[]{:S(2)}) collective-permute-start(bf16[24,1024]{1,0:T(8,128)(2,1)S(1)} %get-tuple-element.48), channel_id=1, source_target_pairs={{0,10},{1,11},{2,8},{3,9},{4,14},{5,15},{6,12},{7,13},{8,2},{9,3},... | collective-permute-start | bytes 147464 | tf_op jit(solution)/shard_map/ppermute | solution.py:32
  35.8 6.8 %collective-permute-start.19 = (bf16[24,1024]{1,0:T(8,128)(2,1)S(1)}, bf16[24,1024]{1,0:T(8,128)(2,1)S(1)}, u32[]{:S(2)}, u32[]{:S(2)}) collective-permute-start(bf16[24,1024]{1,0:T(8,128)(2,1)S(1)} %get-tuple-element.49), channel_id=1, source_target_pairs={{0,8},{1,9},{2,10},{3,11},{4,12},{5,13},{6,14},{7,15},{8,0},{9,1},... | collective-permute-start | bytes 147464 | tf_op jit(solution)/shard_map/ppermute | solution.py:32
  35.9 6.7 %collective-permute-start.20 = (bf16[24,1024]{1,0:T(8,128)(2,1)S(1)}, bf16[24,1024]{1,0:T(8,128)(2,1)S(1)}, u32[]{:S(2)}, u32[]{:S(2)}) collective-permute-start(bf16[24,1024]{1,0:T(8,128)(2,1)S(1)} %get-tuple-element.50), channel_id=1, source_target_pairs={{0,6},{1,7},{2,4},{3,5},{4,2},{5,3},{6,0},{7,1},{8,14},{9,15},{10,... | collective-permute-start | bytes 147464 | tf_op jit(solution)/shard_map/ppermute | solution.py:32
  38.2 5.1 %collective-permute-start.21 = (bf16[24,1024]{1,0:T(8,128)(2,1)S(1)}, bf16[24,1024]{1,0:T(8,128)(2,1)S(1)}, u32[]{:S(2)}, u32[]{:S(2)}) collective-permute-start(bf16[24,1024]{1,0:T(8,128)(2,1)S(1)} %get-tuple-element.51), channel_id=1, source_target_pairs={{0,4},{1,5},{2,6},{3,7},{4,0},{5,1},{6,2},{7,3},{8,12},{9,13},{10,... | collective-permute-start | bytes 147464 | tf_op jit(solution)/shard_map/ppermute | solution.py:32
  38.8 4.6 %collective-permute-start.22 = (bf16[24,1024]{1,0:T(8,128)(2,1)S(1)}, bf16[24,1024]{1,0:T(8,128)(2,1)S(1)}, u32[]{:S(2)}, u32[]{:S(2)}) collective-permute-start(bf16[24,1024]{1,0:T(8,128)(2,1)S(1)} %get-tuple-element.52), channel_id=1, source_target_pairs={{0,2},{1,3},{2,0},{3,1},{4,6},{5,7},{6,4},{7,5},{8,10},{9,11},{10,... | collective-permute-start | bytes 147464 | tf_op jit(solution)/shard_map/ppermute | solution.py:32
  (2 other events, 47.4 us)

commit v7 on v6

--- a/solution.py
+++ b/solution.py
@@ -282,23 +282,15 @@
 
 
 def place_kernel(order, step_ref, *refs):
-    chips = len(order)
-    answers = refs[:chips]
-    out_ref, placed, sems = refs[chips:]
+    *answers, out_ref = refs
     width = answers[0].shape[-1] // 2
     here = lax.div(lax.axis_index("patch"), 2)
-    copies = []
     for half, layer in enumerate(layers_of(step_ref[0])):
         for slot, chip in enumerate(order):
             first = pl.multiple_of(lax.bitwise_xor(here, chip) * width, width)
-            placed[layer, :, pl.ds(first, width)] = answers[slot][
+            out_ref[layer, :, pl.ds(first, width)] = answers[slot][
                 :, half * width : (half + 1) * width
             ]
-        copies.append(
-            pltpu.make_async_copy(placed.at[layer], out_ref.at[layer], sems.at[half])
-        )
-        copies[-1].start()
-    wait_all(copies)
 
 
 def place(step_index, answers, order):
@@ -308,19 +300,15 @@
         partial(place_kernel, order),
         in_specs=[pl.BlockSpec(memory_space=pltpu.SMEM)]
         + [pl.BlockSpec(memory_space=pltpu.VMEM)] * len(order),
-        out_specs=pl.BlockSpec(memory_space=pl.ANY),
+        out_specs=pl.BlockSpec(memory_space=pltpu.VMEM),
         out_shape=attended,
-        scratch_shapes=[
-            pltpu.VMEM(attended.shape, attended.dtype),
-            pltpu.SemaphoreType.DMA((2,)),
-        ],
         compiler_params=pltpu.CompilerParams(vmem_limit_bytes=VMEM_BYTES),
     )(step_index, *answers)
 
 
 def distances(chips):
     if chips == 8:
-        return [5, 1, 3, 4, 6, 2, 7, 0], [7, 6, 5, 4, 3, 2, 1, 0]
+        return [5, 3, 4, 6, 2, 1, 7, 0], [7, 6, 5, 4, 3, 2, 1, 0]
     order = list(range(chips - 1, -1, -1))
     return order, order
 

time: 44.3 us -> 44.2 us (level)
  starting transfers between devices: 29.4 us -> 27.8 us
  waiting for transfers between devices: 7.54 us -> 9.01 us
    ppermute x23, starting transfers between devices: 29.4 us -> 27.8 us  [pairwise(): return lax.ppermute(array, 'patch', pairs)]
    ppermute x23, waiting for transfers between devices: 7.54 us -> 9.01 us  [pairwise(): return lax.ppermute(array, 'patch', pairs)]
  transfers between devices with their start and end apart: 23 -> 23, of which waited for: 8 -> 9; matrix products, arithmetic and copies ran while one was open for 0% -> 0% of each run, Pallas kernels for 9% -> 9%
where the time goes in v7:
time: 44.2 us; the launch traced here: 44 us
  starting transfers between devices  27.8 us (63%)
  waiting for transfers between devices  9.01 us (20%)
  Pallas kernels  5.8 us (13%)
  between operations  1.4 us (3%)
    ppermute x23, starting transfers between devices, pairwise(): return lax.ppermute(array, 'patch', pairs)  27.8 us
    ppermute x23, waiting for transfers between devices, pairwise(): return lax.ppermute(array, 'patch', pairs)  9.01 us
    pallas_call x1, Pallas kernels, pack(): pl.pallas_call(partial(pack_kernel, order), in_specs=[pl.BlockSpec(memory...  2.32 us
    pallas_call x1, Pallas kernels, attend_refreshed(): pl.pallas_call(partial(refreshed_kernel, order, head_dim), in_specs=[pl.B...  0.98 us
    pallas_call x1, Pallas kernels, store(): pl.pallas_call(store_kernel, in_specs=[pl.BlockSpec(memory_space=pltpu.SM...  0.89 us
  transfers between devices with their start and end apart: 23, of which 9 were waited for; matrix products, arithmetic and copies ran while one was open for 0% of the time, Pallas kernels for 9%

profile of v7, /device:TPU:0, one launch (start us, length us, event | category | flops | bytes accessed | tf_op | source)
XLA Modules:
  0.0 44.0 jit_solution(8963465077061846137)
XLA Ops:
  0.6 0.5 %collective-permute-start = (bf16[2,2,384,256]{3,2,1,0:T(8,128)(2,1)}, bf16[2,2,384,256]{3,2,1,0:T(8,128)(2,1)S(1)}, u32[]{:S(2)}, u32[]{:S(2)}) collective-permute-start(bf16[2,2,384,256]{3,2,1,0:T(8,128)(2,1)} %bitcast.4), channel_id=1, source_target_pairs={{0,1},{1,0},{2,3},{3,2},{4,5},{5,4},{6,7},{7,6},{8,9},{9,8},{10,11... | collective-permute-start | bytes 2359304 | tf_op jit(solution)/shard_map/ppermute | solution.py:32
  1.8 2.3 %shard_map.77 = (bf16[24,2048]{1,0:T(8,128)(2,1)}, bf16[24,2048]{1,0:T(8,128)(2,1)}, bf16[24,2048]{1,0:T(8,128)(2,1)}, bf16[24,2048]{1,0:T(8,128)(2,1)}, bf16[24...) custom-call(s32[1]{0:T(128)S(6)} %copy.9.step_ref, ...), custom_call_target="tpu_custom_call" | custom-call | tf_op jit(solution)/shard_map/pallas_call | solution.py:103
  4.2 4.6 %collective-permute-start.1 = (bf16[24,2048]{1,0:T(8,128)(2,1)}, bf16[24,2048]{1,0:T(8,128)(2,1)S(1)}, u32[]{:S(2)}, u32[]{:S(2)}) collective-permute-start(bf16[24,2048]{1,0:T(8,128)(2,1)} %get-tuple-element.37), channel_id=1, source_target_pairs={{0,10},{1,11},{2,8},{3,9},{4,14},{5,15},{6,12},{7,13},{8,2},{9,3},... | collective-permute-start | bytes 294920 | tf_op jit(solution)/shard_map/ppermute | solution.py:32
  8.8 1.5 %collective-permute-start.2 = (bf16[24,2048]{1,0:T(8,128)(2,1)}, bf16[24,2048]{1,0:T(8,128)(2,1)S(1)}, u32[]{:S(2)}, u32[]{:S(2)}) collective-permute-start(bf16[24,2048]{1,0:T(8,128)(2,1)} %get-tuple-element.38), channel_id=1, source_target_pairs={{0,6},{1,7},{2,4},{3,5},{4,2},{5,3},{6,0},{7,1},{8,14},{9,15},{10,... | collective-permute-start | bytes 294920 | tf_op jit(solution)/shard_map/ppermute | solution.py:32
  10.6 2.5 %collective-permute-start.4 = (bf16[24,2048]{1,0:T(8,128)(2,1)}, bf16[24,2048]{1,0:T(8,128)(2,1)S(1)}, u32[]{:S(2)}, u32[]{:S(2)}) collective-permute-start(bf16[24,2048]{1,0:T(8,128)(2,1)} %get-tuple-element.40), channel_id=1, source_target_pairs={{0,12},{1,13},{2,14},{3,15},{4,8},{5,9},{6,10},{7,11},{8,4},{9,5},... | collective-permute-start | bytes 294920 | tf_op jit(solution)/shard_map/ppermute | solution.py:32
  13.1 0.7 %collective-permute-start.5 = (bf16[24,2048]{1,0:T(8,128)(2,1)}, bf16[24,2048]{1,0:T(8,128)(2,1)S(1)}, u32[]{:S(2)}, u32[]{:S(2)}) collective-permute-start(bf16[24,2048]{1,0:T(8,128)(2,1)} %get-tuple-element.41), channel_id=1, source_target_pairs={{0,4},{1,5},{2,6},{3,7},{4,0},{5,1},{6,2},{7,3},{8,12},{9,13},{10,... | collective-permute-start | bytes 294920 | tf_op jit(solution)/shard_map/ppermute | solution.py:32
  13.8 0.9 %collective-permute-done.1.refs_0_ = bf16[24,2048]{1,0:T(8,128)(2,1)S(1)} collective-permute-done((bf16[24,2048]{1,0:T(8,128)(2,1)}, bf16[24,2048]{1,0:T(8,128)(2,1)S(1)}, u32[]{:S(2)}, u32[]{:S(2)}) %collective-permute-start.1) | collective-permute-done | bytes 98336 | tf_op jit(solution)/shard_map/ppermute | solution.py:32
  14.6 1.9 %collective-permute-start.6 = (bf16[24,2048]{1,0:T(8,128)(2,1)}, bf16[24,2048]{1,0:T(8,128)(2,1)S(1)}, u32[]{:S(2)}, u32[]{:S(2)}) collective-permute-start(bf16[24,2048]{1,0:T(8,128)(2,1)} %get-tuple-element.42), channel_id=1, source_target_pairs={{0,2},{1,3},{2,0},{3,1},{4,6},{5,7},{6,4},{7,5},{8,10},{9,11},{10,... | collective-permute-start | bytes 294920 | tf_op jit(solution)/shard_map/ppermute | solution.py:32
  16.6 1.1 %collective-permute-done.2.refs_1_ = bf16[24,2048]{1,0:T(8,128)(2,1)S(1)} collective-permute-done((bf16[24,2048]{1,0:T(8,128)(2,1)}, bf16[24,2048]{1,0:T(8,128)(2,1)S(1)}, u32[]{:S(2)}, u32[]{:S(2)}) %collective-permute-start.2) | collective-permute-done | bytes 98336 | tf_op jit(solution)/shard_map/ppermute | solution.py:32
  17.7 2.5 %collective-permute-start.7 = (bf16[24,2048]{1,0:T(8,128)(2,1)}, bf16[24,2048]{1,0:T(8,128)(2,1)S(1)}, u32[]{:S(2)}, u32[]{:S(2)}) collective-permute-start(bf16[24,2048]{1,0:T(8,128)(2,1)} %get-tuple-element.43), channel_id=1, source_target_pairs={{0,14},{1,15},{2,12},{3,13},{4,10},{5,11},{6,8},{7,9},{8,6},{9,7},... | collective-permute-start | bytes 294920 | tf_op jit(solution)/shard_map/ppermute | solution.py:32
  20.2 1.2 %collective-permute-done.3.refs_2_ = bf16[24,2048]{1,0:T(8,128)(2,1)S(1)} collective-permute-done((bf16[24,2048]{1,0:T(8,128)(2,1)}, bf16[24,2048]{1,0:T(8,128)(2,1)S(1)}, u32[]{:S(2)}, u32[]{:S(2)}) %collective-permute-start.3) | collective-permute-done | bytes 98336 | tf_op jit(solution)/shard_map/ppermute | solution.py:32
  22.4 2.8 %collective-permute-done.7.refs_6_ = bf16[24,2048]{1,0:T(8,128)(2,1)S(1)} collective-permute-done((bf16[24,2048]{1,0:T(8,128)(2,1)}, bf16[24,2048]{1,0:T(8,128)(2,1)S(1)}, u32[]{:S(2)}, u32[]{:S(2)}) %collective-permute-start.7) | collective-permute-done | bytes 98336 | tf_op jit(solution)/shard_map/ppermute | solution.py:32
  26.3 0.8 %shard_map.78.refs_16_ = bf16[8,24,512]{2,1,0:T(8,128)(2,1)S(1)} custom-call(s32[1]{0:T(128)S(6)} %copy.9.step_ref, bf16[2,24,4096]{2,1,0:T(8,128)(2,1)S(1)} %copy-done.1, bf16[24,2048]{1,0:T(8,128)(2,1)S(1)} %collective-permute-done.1.refs_0_, bf16[24,2048]{1,0:T(8,128)(2,1)S(1)} %collective-permute-done.2.refs_1_, ...), custom_call_target="tpu_custom_call" | custom-call | tf_op jit(solution)/shard_map/pallas_call | solution.py:180
  27.2 1.0 %shard_map.79 = (bf16[24,1024]{1,0:T(8,128)(2,1)S(1)}, bf16[24,1024]{1,0:T(8,128)(2,1)S(1)}, bf16[24,1024]{1,0:T(8,128)(2,1)S(1)}, bf16[24,1024]{1,0:T(8,128)(2,...) custom-call(s32[1]{0:T(128)S(6)} %copy.9.step_ref, ...), custom_call_target="tpu_custom_call" | custom-call | tf_op jit(solution)/shard_map/pallas_call | solution.py:243
  28.2 2.6 %collective-permute-start.16 = (bf16[24,1024]{1,0:T(8,128)(2,1)S(1)}, bf16[24,1024]{1,0:T(8,128)(2,1)S(1)}, u32[]{:S(2)}, u32[]{:S(2)}) collective-permute-start(bf16[24,1024]{1,0:T(8,128)(2,1)S(1)} %get-tuple-element.46), channel_id=1, source_target_pairs={{0,14},{1,15},{2,12},{3,13},{4,10},{5,11},{6,8},{7,9},{8,6},{9,7},... | collective-permute-start | bytes 147464 | tf_op jit(solution)/shard_map/ppermute | solution.py:32
  30.8 1.8 %collective-permute-start.17 = (bf16[24,1024]{1,0:T(8,128)(2,1)S(1)}, bf16[24,1024]{1,0:T(8,128)(2,1)S(1)}, u32[]{:S(2)}, u32[]{:S(2)}) collective-permute-start(bf16[24,1024]{1,0:T(8,128)(2,1)S(1)} %get-tuple-element.47), channel_id=1, source_target_pairs={{0,12},{1,13},{2,14},{3,15},{4,8},{5,9},{6,10},{7,11},{8,4},{9,5},... | collective-permute-start | bytes 147464 | tf_op jit(solution)/shard_map/ppermute | solution.py:32
  32.6 3.2 %collective-permute-start.18 = (bf16[24,1024]{1,0:T(8,128)(2,1)S(1)}, bf16[24,1024]{1,0:T(8,128)(2,1)S(1)}, u32[]{:S(2)}, u32[]{:S(2)}) collective-permute-start(bf16[24,1024]{1,0:T(8,128)(2,1)S(1)} %get-tuple-element.48), channel_id=1, source_target_pairs={{0,10},{1,11},{2,8},{3,9},{4,14},{5,15},{6,12},{7,13},{8,2},{9,3},... | collective-permute-start | bytes 147464 | tf_op jit(solution)/shard_map/ppermute | solution.py:32
  35.9 2.3 %collective-permute-start.20 = (bf16[24,1024]{1,0:T(8,128)(2,1)S(1)}, bf16[24,1024]{1,0:T(8,128)(2,1)S(1)}, u32[]{:S(2)}, u32[]{:S(2)}) collective-permute-start(bf16[24,1024]{1,0:T(8,128)(2,1)S(1)} %get-tuple-element.50), channel_id=1, source_target_pairs={{0,6},{1,7},{2,4},{3,5},{4,2},{5,3},{6,0},{7,1},{8,14},{9,15},{10,... | collective-permute-start | bytes 147464 | tf_op jit(solution)/shard_map/ppermute | solution.py:32
  38.2 0.6 %collective-permute-start.21 = (bf16[24,1024]{1,0:T(8,128)(2,1)S(1)}, bf16[24,1024]{1,0:T(8,128)(2,1)S(1)}, u32[]{:S(2)}, u32[]{:S(2)}) collective-permute-start(bf16[24,1024]{1,0:T(8,128)(2,1)S(1)} %get-tuple-element.51), channel_id=1, source_target_pairs={{0,4},{1,5},{2,6},{3,7},{4,0},{5,1},{6,2},{7,3},{8,12},{9,13},{10,... | collective-permute-start | bytes 147464 | tf_op jit(solution)/shard_map/ppermute | solution.py:32
  38.7 0.7 %collective-permute-start.22 = (bf16[24,1024]{1,0:T(8,128)(2,1)S(1)}, bf16[24,1024]{1,0:T(8,128)(2,1)S(1)}, u32[]{:S(2)}, u32[]{:S(2)}) collective-permute-start(bf16[24,1024]{1,0:T(8,128)(2,1)S(1)} %get-tuple-element.52), channel_id=1, source_target_pairs={{0,2},{1,3},{2,0},{3,1},{4,6},{5,7},{6,4},{7,5},{8,10},{9,11},{10,... | collective-permute-start | bytes 147464 | tf_op jit(solution)/shard_map/ppermute | solution.py:32
  39.4 0.9 %shard_map.81 = bf16[2,2,384,256]{3,2,1,0:T(8,128)(2,1)} custom-call(s32[1]{0:T(128)S(6)} %copy.9.step_ref, bf16[2,2,384,256]{3,2,1,0:T(8,128)(2,1)S(1)} %bitcast.7, bf16[2,384,256]{2,1,0:T(8,128)(2,1)S(1)} %get-tuple-element.55.renewed_ref), custom_call_target="tpu_custom_call" | custom-call | tf_op jit(solution)/shard_map/pallas_call | solution.py:269
  40.3 1.5 %collective-permute-done.18.refs_2_ = bf16[24,1024]{1,0:T(8,128)(2,1)S(1)} collective-permute-done((bf16[24,1024]{1,0:T(8,128)(2,1)S(1)}, bf16[24,1024]{1,0:T(8,128)(2,1)S(1)}, u32[]{:S(2)}, u32[]{:S(2)}) %collective-permute-start.18) | collective-permute-done | bytes 49184 | tf_op jit(solution)/shard_map/ppermute | solution.py:32
  42.2 0.8 %collective-permute-done.20.refs_4_ = bf16[24,1024]{1,0:T(8,128)(2,1)S(1)} collective-permute-done((bf16[24,1024]{1,0:T(8,128)(2,1)S(1)}, bf16[24,1024]{1,0:T(8,128)(2,1)S(1)}, u32[]{:S(2)}, u32[]{:S(2)}) %collective-permute-start.20) | collective-permute-done | bytes 49184 | tf_op jit(solution)/shard_map/ppermute | solution.py:32
  43.2 0.8 %shard_map.80 = bf16[2,24,4096]{2,1,0:T(8,128)(2,1)} custom-call(s32[1]{0:T(128)S(6)} %copy.9.step_ref, bf16[24,1024]{1,0:T(8,128)(2,1)S(1)} %collective-permute-done.16.refs_0_, bf16[24,1024]{1,0:T(8,128)(2,1)S(1)} %collective-permute-done.17.refs_1_, bf16[24,1024]{1,0:T(8,128)(2,1)S(1)} %collective-permute-done.18.refs_2_, ...), custom_call_target="tpu_custom_call" | custom-call | tf_op jit(solution)/shard_map/pallas_call | solution.py:299
  (33 shorter events, 3.2 us)
Async XLA Ops:
  0.6 3.5 %collective-permute-start = (bf16[2,2,384,256]{3,2,1,0:T(8,128)(2,1)}, bf16[2,2,384,256]{3,2,1,0:T(8,128)(2,1)S(1)}, u32[]{:S(2)}, u32[]{:S(2)}) collective-permute-start(bf16[2,2,384,256]{3,2,1,0:T(8,128)(2,1)} %bitcast.4), channel_id=1, source_target_pairs={{0,1},{1,0},{2,3},{3,2},{4,5},{5,4},{6,7},{7,6},{8,9},{9,8},{10,11... | collective-permute-start | bytes 2359304 | tf_op jit(solution)/shard_map/ppermute | solution.py:32
  1.8 24.4 %copy-start = (bf16[2,2,1,16,24,256]{5,4,3,2,1,0:T(8,128)(2,1)S(1)}, bf16[2,2,1,16,24,256]{5,4,3,2,1,0:T(8,128)(2,1)}, u32[]{:S(2)}) copy-start(bf16[2,2,1,16,24,256]{5,4,3,2,1,0:T(8,128)(2,1)} %param.9) | copy-start | bytes 2359300
  4.2 10.5 %collective-permute-start.1 = (bf16[24,2048]{1,0:T(8,128)(2,1)}, bf16[24,2048]{1,0:T(8,128)(2,1)S(1)}, u32[]{:S(2)}, u32[]{:S(2)}) collective-permute-start(bf16[24,2048]{1,0:T(8,128)(2,1)} %get-tuple-element.37), channel_id=1, source_target_pairs={{0,10},{1,11},{2,8},{3,9},{4,14},{5,15},{6,12},{7,13},{8,2},{9,3},... | collective-permute-start | bytes 294920 | tf_op jit(solution)/shard_map/ppermute | solution.py:32
  8.8 8.9 %collective-permute-start.2 = (bf16[24,2048]{1,0:T(8,128)(2,1)}, bf16[24,2048]{1,0:T(8,128)(2,1)S(1)}, u32[]{:S(2)}, u32[]{:S(2)}) collective-permute-start(bf16[24,2048]{1,0:T(8,128)(2,1)} %get-tuple-element.38), channel_id=1, source_target_pairs={{0,6},{1,7},{2,4},{3,5},{4,2},{5,3},{6,0},{7,1},{8,14},{9,15},{10,... | collective-permute-start | bytes 294920 | tf_op jit(solution)/shard_map/ppermute | solution.py:32
  10.3 11.1 %collective-permute-start.3 = (bf16[24,2048]{1,0:T(8,128)(2,1)}, bf16[24,2048]{1,0:T(8,128)(2,1)S(1)}, u32[]{:S(2)}, u32[]{:S(2)}) collective-permute-start(bf16[24,2048]{1,0:T(8,128)(2,1)} %get-tuple-element.39), channel_id=1, source_target_pairs={{0,8},{1,9},{2,10},{3,11},{4,12},{5,13},{6,14},{7,15},{8,0},{9,1},... | collective-permute-start | bytes 294920 | tf_op jit(solution)/shard_map/ppermute | solution.py:32
  10.6 10.8 %collective-permute-start.4 = (bf16[24,2048]{1,0:T(8,128)(2,1)}, bf16[24,2048]{1,0:T(8,128)(2,1)S(1)}, u32[]{:S(2)}, u32[]{:S(2)}) collective-permute-start(bf16[24,2048]{1,0:T(8,128)(2,1)} %get-tuple-element.40), channel_id=1, source_target_pairs={{0,12},{1,13},{2,14},{3,15},{4,8},{5,9},{6,10},{7,11},{8,4},{9,5},... | collective-permute-start | bytes 294920 | tf_op jit(solution)/shard_map/ppermute | solution.py:32
  13.1 8.8 %collective-permute-start.5 = (bf16[24,2048]{1,0:T(8,128)(2,1)}, bf16[24,2048]{1,0:T(8,128)(2,1)S(1)}, u32[]{:S(2)}, u32[]{:S(2)}) collective-permute-start(bf16[24,2048]{1,0:T(8,128)(2,1)} %get-tuple-element.41), channel_id=1, source_target_pairs={{0,4},{1,5},{2,6},{3,7},{4,0},{5,1},{6,2},{7,3},{8,12},{9,13},{10,... | collective-permute-start | bytes 294920 | tf_op jit(solution)/shard_map/ppermute | solution.py:32
  14.6 7.3 %collective-permute-start.6 = (bf16[24,2048]{1,0:T(8,128)(2,1)}, bf16[24,2048]{1,0:T(8,128)(2,1)S(1)}, u32[]{:S(2)}, u32[]{:S(2)}) collective-permute-start(bf16[24,2048]{1,0:T(8,128)(2,1)} %get-tuple-element.42), channel_id=1, source_target_pairs={{0,2},{1,3},{2,0},{3,1},{4,6},{5,7},{6,4},{7,5},{8,10},{9,11},{10,... | collective-permute-start | bytes 294920 | tf_op jit(solution)/shard_map/ppermute | solution.py:32
  17.7 7.5 %collective-permute-start.7 = (bf16[24,2048]{1,0:T(8,128)(2,1)}, bf16[24,2048]{1,0:T(8,128)(2,1)S(1)}, u32[]{:S(2)}, u32[]{:S(2)}) collective-permute-start(bf16[24,2048]{1,0:T(8,128)(2,1)} %get-tuple-element.43), channel_id=1, source_target_pairs={{0,14},{1,15},{2,12},{3,13},{4,10},{5,11},{6,8},{7,9},{8,6},{9,7},... | collective-permute-start | bytes 294920 | tf_op jit(solution)/shard_map/ppermute | solution.py:32
  21.4 3.8 %collective-permute-start.15 = (bf16[24,2048]{1,0:T(8,128)(2,1)}, bf16[24,2048]{1,0:T(8,128)(2,1)S(1)}, u32[]{:S(2)}, u32[]{:S(2)}) collective-permute-start(bf16[24,2048]{1,0:T(8,128)(2,1)} %get-tuple-element.44.refs_7_), channel_id=1, source_target_pairs={{0,1},{1,0},{2,3},{3,2},{4,5},{5,4},{6,7},{7,6},{8,9},{9,8},{10,11... | collective-permute-start | bytes 294920 | tf_op jit(solution)/shard_map/ppermute | solution.py:32
  21.4 4.3 %collective-permute-start.8 = (bf16[24,2048]{1,0:T(8,128)(2,1)S(1)}, bf16[24,2048]{1,0:T(8,128)(2,1)S(1)}, u32[]{:S(2)}, u32[]{:S(2)}) collective-permute-start(bf16[24,2048]{1,0:T(8,128)(2,1)S(1)} %collective-permute-done.1.refs_0_), channel_id=1, source_target_pairs={{0,1},{1,0},{2,3},{3,2},{4,5},{5,4},{6,7},{7,6},{8,9},{9,8},{10,11... | collective-permute-start | bytes 294920 | tf_op jit(solution)/shard_map/ppermute | solution.py:32
  21.9 3.9 %collective-permute-start.9 = (bf16[24,2048]{1,0:T(8,128)(2,1)S(1)}, bf16[24,2048]{1,0:T(8,128)(2,1)S(1)}, u32[]{:S(2)}, u32[]{:S(2)}) collective-permute-start(bf16[24,2048]{1,0:T(8,128)(2,1)S(1)} %collective-permute-done.2.refs_1_), channel_id=1, source_target_pairs={{0,1},{1,0},{2,3},{3,2},{4,5},{5,4},{6,7},{7,6},{8,9},{9,8},{10,11... | collective-permute-start | bytes 294920 | tf_op jit(solution)/shard_map/ppermute | solution.py:32
  22.0 5.1 %collective-permute-start.10 = (bf16[24,2048]{1,0:T(8,128)(2,1)S(1)}, bf16[24,2048]{1,0:T(8,128)(2,1)S(1)}, u32[]{:S(2)}, u32[]{:S(2)}) collective-permute-start(bf16[24,2048]{1,0:T(8,128)(2,1)S(1)} %collective-permute-done.3.refs_2_), channel_id=1, source_target_pairs={{0,1},{1,0},{2,3},{3,2},{4,5},{5,4},{6,7},{7,6},{8,9},{9,8},{10,11... | collective-permute-start | bytes 294920 | tf_op jit(solution)/shard_map/ppermute | solution.py:32
  25.2 1.9 %collective-permute-start.11 = (bf16[24,2048]{1,0:T(8,128)(2,1)S(1)}, bf16[24,2048]{1,0:T(8,128)(2,1)S(1)}, u32[]{:S(2)}, u32[]{:S(2)}) collective-permute-start(bf16[24,2048]{1,0:T(8,128)(2,1)S(1)} %collective-permute-done.4.refs_3_), channel_id=1, source_target_pairs={{0,1},{1,0},{2,3},{3,2},{4,5},{5,4},{6,7},{7,6},{8,9},{9,8},{10,11... | collective-permute-start | bytes 294920 | tf_op jit(solution)/shard_map/ppermute | solution.py:32
  25.2 1.9 %collective-permute-start.12 = (bf16[24,2048]{1,0:T(8,128)(2,1)S(1)}, bf16[24,2048]{1,0:T(8,128)(2,1)S(1)}, u32[]{:S(2)}, u32[]{:S(2)}) collective-permute-start(bf16[24,2048]{1,0:T(8,128)(2,1)S(1)} %collective-permute-done.5.refs_4_), channel_id=1, source_target_pairs={{0,1},{1,0},{2,3},{3,2},{4,5},{5,4},{6,7},{7,6},{8,9},{9,8},{10,11... | collective-permute-start | bytes 294920 | tf_op jit(solution)/shard_map/ppermute | solution.py:32
  25.7 1.4 %collective-permute-start.13 = (bf16[24,2048]{1,0:T(8,128)(2,1)S(1)}, bf16[24,2048]{1,0:T(8,128)(2,1)S(1)}, u32[]{:S(2)}, u32[]{:S(2)}) collective-permute-start(bf16[24,2048]{1,0:T(8,128)(2,1)S(1)} %collective-permute-done.6.refs_5_), channel_id=1, source_target_pairs={{0,1},{1,0},{2,3},{3,2},{4,5},{5,4},{6,7},{7,6},{8,9},{9,8},{10,11... | collective-permute-start | bytes 294920 | tf_op jit(solution)/shard_map/ppermute | solution.py:32
  25.8 1.4 %collective-permute-start.14 = (bf16[24,2048]{1,0:T(8,128)(2,1)S(1)}, bf16[24,2048]{1,0:T(8,128)(2,1)S(1)}, u32[]{:S(2)}, u32[]{:S(2)}) collective-permute-start(bf16[24,2048]{1,0:T(8,128)(2,1)S(1)} %collective-permute-done.7.refs_6_), channel_id=1, source_target_pairs={{0,1},{1,0},{2,3},{3,2},{4,5},{5,4},{6,7},{7,6},{8,9},{9,8},{10,11... | collective-permute-start | bytes 294920 | tf_op jit(solution)/shard_map/ppermute | solution.py:32
  28.2 10.0 %collective-permute-start.16 = (bf16[24,1024]{1,0:T(8,128)(2,1)S(1)}, bf16[24,1024]{1,0:T(8,128)(2,1)S(1)}, u32[]{:S(2)}, u32[]{:S(2)}) collective-permute-start(bf16[24,1024]{1,0:T(8,128)(2,1)S(1)} %get-tuple-element.46), channel_id=1, source_target_pairs={{0,14},{1,15},{2,12},{3,13},{4,10},{5,11},{6,8},{7,9},{8,6},{9,7},... | collective-permute-start | bytes 147464 | tf_op jit(solution)/shard_map/ppermute | solution.py:32
  30.8 7.9 %collective-permute-start.17 = (bf16[24,1024]{1,0:T(8,128)(2,1)S(1)}, bf16[24,1024]{1,0:T(8,128)(2,1)S(1)}, u32[]{:S(2)}, u32[]{:S(2)}) collective-permute-start(bf16[24,1024]{1,0:T(8,128)(2,1)S(1)} %get-tuple-element.47), channel_id=1, source_target_pairs={{0,12},{1,13},{2,14},{3,15},{4,8},{5,9},{6,10},{7,11},{8,4},{9,5},... | collective-permute-start | bytes 147464 | tf_op jit(solution)/shard_map/ppermute | solution.py:32
  32.6 9.1 %collective-permute-start.18 = (bf16[24,1024]{1,0:T(8,128)(2,1)S(1)}, bf16[24,1024]{1,0:T(8,128)(2,1)S(1)}, u32[]{:S(2)}, u32[]{:S(2)}) collective-permute-start(bf16[24,1024]{1,0:T(8,128)(2,1)S(1)} %get-tuple-element.48), channel_id=1, source_target_pairs={{0,10},{1,11},{2,8},{3,9},{4,14},{5,15},{6,12},{7,13},{8,2},{9,3},... | collective-permute-start | bytes 147464 | tf_op jit(solution)/shard_map/ppermute | solution.py:32
  35.8 6.3 %collective-permute-start.19 = (bf16[24,1024]{1,0:T(8,128)(2,1)S(1)}, bf16[24,1024]{1,0:T(8,128)(2,1)S(1)}, u32[]{:S(2)}, u32[]{:S(2)}) collective-permute-start(bf16[24,1024]{1,0:T(8,128)(2,1)S(1)} %get-tuple-element.49), channel_id=1, source_target_pairs={{0,8},{1,9},{2,10},{3,11},{4,12},{5,13},{6,14},{7,15},{8,0},{9,1},... | collective-permute-start | bytes 147464 | tf_op jit(solution)/shard_map/ppermute | solution.py:32
  35.9 7.1 %collective-permute-start.20 = (bf16[24,1024]{1,0:T(8,128)(2,1)S(1)}, bf16[24,1024]{1,0:T(8,128)(2,1)S(1)}, u32[]{:S(2)}, u32[]{:S(2)}) collective-permute-start(bf16[24,1024]{1,0:T(8,128)(2,1)S(1)} %get-tuple-element.50), channel_id=1, source_target_pairs={{0,6},{1,7},{2,4},{3,5},{4,2},{5,3},{6,0},{7,1},{8,14},{9,15},{10,... | collective-permute-start | bytes 147464 | tf_op jit(solution)/shard_map/ppermute | solution.py:32
  38.2 5.1 %collective-permute-start.21 = (bf16[24,1024]{1,0:T(8,128)(2,1)S(1)}, bf16[24,1024]{1,0:T(8,128)(2,1)S(1)}, u32[]{:S(2)}, u32[]{:S(2)}) collective-permute-start(bf16[24,1024]{1,0:T(8,128)(2,1)S(1)} %get-tuple-element.51), channel_id=1, source_target_pairs={{0,4},{1,5},{2,6},{3,7},{4,0},{5,1},{6,2},{7,3},{8,12},{9,13},{10,... | collective-permute-start | bytes 147464 | tf_op jit(solution)/shard_map/ppermute | solution.py:32
  38.7 4.5 %collective-permute-start.22 = (bf16[24,1024]{1,0:T(8,128)(2,1)S(1)}, bf16[24,1024]{1,0:T(8,128)(2,1)S(1)}, u32[]{:S(2)}, u32[]{:S(2)}) collective-permute-start(bf16[24,1024]{1,0:T(8,128)(2,1)S(1)} %get-tuple-element.52), channel_id=1, source_target_pairs={{0,2},{1,3},{2,0},{3,1},{4,6},{5,7},{6,4},{7,5},{8,10},{9,11},{10,... | collective-permute-start | bytes 147464 | tf_op jit(solution)/shard_map/ppermute | solution.py:32
  (2 other events, 47.5 us)

commit v8 on v7

--- a/solution.py
+++ b/solution.py
@@ -308,7 +308,7 @@
 
 def distances(chips):
     if chips == 8:
-        return [5, 3, 4, 6, 2, 1, 7, 0], [7, 6, 5, 4, 3, 2, 1, 0]
+        return [5, 3, 4, 6, 2, 1, 7, 0], [7, 6, 4, 5, 3, 2, 1, 0]
     order = list(range(chips - 1, -1, -1))
     return order, order
 

time: 44.2 us -> 44.3 us (level)
  transfers between devices with their start and end apart: 23 -> 23, of which waited for: 9 -> 10; matrix products, arithmetic and copies ran while one was open for 0% -> 0% of each run, Pallas kernels for 9% -> 9%
where the time goes in v8:
time: 44.3 us; the launch traced here: 44.1 us
  starting transfers between devices  27.8 us (63%)
  waiting for transfers between devices  9.09 us (21%)
  Pallas kernels  5.79 us (13%)
  between operations  1.4 us (3%)
    ppermute x23, starting transfers between devices, pairwise(): return lax.ppermute(array, 'patch', pairs)  27.8 us
    ppermute x23, waiting for transfers between devices, pairwise(): return lax.ppermute(array, 'patch', pairs)  9.09 us
    pallas_call x1, Pallas kernels, pack(): pl.pallas_call(partial(pack_kernel, order), in_specs=[pl.BlockSpec(memory...  2.32 us
    pallas_call x1, Pallas kernels, attend_refreshed(): pl.pallas_call(partial(refreshed_kernel, order, head_dim), in_specs=[pl.B...  0.98 us
    pallas_call x1, Pallas kernels, store(): pl.pallas_call(store_kernel, in_specs=[pl.BlockSpec(memory_space=pltpu.SM...  0.89 us
  transfers between devices with their start and end apart: 23, of which 10 were waited for; matrix products, arithmetic and copies ran while one was open for 0% of the time, Pallas kernels for 9%

profile of v8, /device:TPU:0, one launch (start us, length us, event | category | flops | bytes accessed | tf_op | source)
XLA Modules:
  0.0 44.1 jit_solution(6593340022036603103)
XLA Ops:
  1.8 2.3 %shard_map.77 = (bf16[24,2048]{1,0:T(8,128)(2,1)}, bf16[24,2048]{1,0:T(8,128)(2,1)}, bf16[24,2048]{1,0:T(8,128)(2,1)}, bf16[24,2048]{1,0:T(8,128)(2,1)}, bf16[24...) custom-call(s32[1]{0:T(128)S(6)} %copy.9.step_ref, ...), custom_call_target="tpu_custom_call" | custom-call | tf_op jit(solution)/shard_map/pallas_call | solution.py:103
  4.2 4.6 %collective-permute-start.1 = (bf16[24,2048]{1,0:T(8,128)(2,1)}, bf16[24,2048]{1,0:T(8,128)(2,1)S(1)}, u32[]{:S(2)}, u32[]{:S(2)}) collective-permute-start(bf16[24,2048]{1,0:T(8,128)(2,1)} %get-tuple-element.37), channel_id=1, source_target_pairs={{0,10},{1,11},{2,8},{3,9},{4,14},{5,15},{6,12},{7,13},{8,2},{9,3},... | collective-permute-start | bytes 294920 | tf_op jit(solution)/shard_map/ppermute | solution.py:32
  8.8 1.5 %collective-permute-start.2 = (bf16[24,2048]{1,0:T(8,128)(2,1)}, bf16[24,2048]{1,0:T(8,128)(2,1)S(1)}, u32[]{:S(2)}, u32[]{:S(2)}) collective-permute-start(bf16[24,2048]{1,0:T(8,128)(2,1)} %get-tuple-element.38), channel_id=1, source_target_pairs={{0,6},{1,7},{2,4},{3,5},{4,2},{5,3},{6,0},{7,1},{8,14},{9,15},{10,... | collective-permute-start | bytes 294920 | tf_op jit(solution)/shard_map/ppermute | solution.py:32
  10.6 2.5 %collective-permute-start.4 = (bf16[24,2048]{1,0:T(8,128)(2,1)}, bf16[24,2048]{1,0:T(8,128)(2,1)S(1)}, u32[]{:S(2)}, u32[]{:S(2)}) collective-permute-start(bf16[24,2048]{1,0:T(8,128)(2,1)} %get-tuple-element.40), channel_id=1, source_target_pairs={{0,12},{1,13},{2,14},{3,15},{4,8},{5,9},{6,10},{7,11},{8,4},{9,5},... | collective-permute-start | bytes 294920 | tf_op jit(solution)/shard_map/ppermute | solution.py:32
  13.1 0.7 %collective-permute-start.5 = (bf16[24,2048]{1,0:T(8,128)(2,1)}, bf16[24,2048]{1,0:T(8,128)(2,1)S(1)}, u32[]{:S(2)}, u32[]{:S(2)}) collective-permute-start(bf16[24,2048]{1,0:T(8,128)(2,1)} %get-tuple-element.41), channel_id=1, source_target_pairs={{0,4},{1,5},{2,6},{3,7},{4,0},{5,1},{6,2},{7,3},{8,12},{9,13},{10,... | collective-permute-start | bytes 294920 | tf_op jit(solution)/shard_map/ppermute | solution.py:32
  13.8 0.9 %collective-permute-done.1.refs_0_ = bf16[24,2048]{1,0:T(8,128)(2,1)S(1)} collective-permute-done((bf16[24,2048]{1,0:T(8,128)(2,1)}, bf16[24,2048]{1,0:T(8,128)(2,1)S(1)}, u32[]{:S(2)}, u32[]{:S(2)}) %collective-permute-start.1) | collective-permute-done | bytes 98336 | tf_op jit(solution)/shard_map/ppermute | solution.py:32
  14.6 1.9 %collective-permute-start.6 = (bf16[24,2048]{1,0:T(8,128)(2,1)}, bf16[24,2048]{1,0:T(8,128)(2,1)S(1)}, u32[]{:S(2)}, u32[]{:S(2)}) collective-permute-start(bf16[24,2048]{1,0:T(8,128)(2,1)} %get-tuple-element.42), channel_id=1, source_target_pairs={{0,2},{1,3},{2,0},{3,1},{4,6},{5,7},{6,4},{7,5},{8,10},{9,11},{10,... | collective-permute-start | bytes 294920 | tf_op jit(solution)/shard_map/ppermute | solution.py:32
  16.6 1.1 %collective-permute-done.2.refs_1_ = bf16[24,2048]{1,0:T(8,128)(2,1)S(1)} collective-permute-done((bf16[24,2048]{1,0:T(8,128)(2,1)}, bf16[24,2048]{1,0:T(8,128)(2,1)S(1)}, u32[]{:S(2)}, u32[]{:S(2)}) %collective-permute-start.2) | collective-permute-done | bytes 98336 | tf_op jit(solution)/shard_map/ppermute | solution.py:32
  17.7 2.5 %collective-permute-start.7 = (bf16[24,2048]{1,0:T(8,128)(2,1)}, bf16[24,2048]{1,0:T(8,128)(2,1)S(1)}, u32[]{:S(2)}, u32[]{:S(2)}) collective-permute-start(bf16[24,2048]{1,0:T(8,128)(2,1)} %get-tuple-element.43), channel_id=1, source_target_pairs={{0,14},{1,15},{2,12},{3,13},{4,10},{5,11},{6,8},{7,9},{8,6},{9,7},... | collective-permute-start | bytes 294920 | tf_op jit(solution)/shard_map/ppermute | solution.py:32
  20.2 1.2 %collective-permute-done.3.refs_2_ = bf16[24,2048]{1,0:T(8,128)(2,1)S(1)} collective-permute-done((bf16[24,2048]{1,0:T(8,128)(2,1)}, bf16[24,2048]{1,0:T(8,128)(2,1)S(1)}, u32[]{:S(2)}, u32[]{:S(2)}) %collective-permute-start.3) | collective-permute-done | bytes 98336 | tf_op jit(solution)/shard_map/ppermute | solution.py:32
  22.4 2.8 %collective-permute-done.7.refs_6_ = bf16[24,2048]{1,0:T(8,128)(2,1)S(1)} collective-permute-done((bf16[24,2048]{1,0:T(8,128)(2,1)}, bf16[24,2048]{1,0:T(8,128)(2,1)S(1)}, u32[]{:S(2)}, u32[]{:S(2)}) %collective-permute-start.7) | collective-permute-done | bytes 98336 | tf_op jit(solution)/shard_map/ppermute | solution.py:32
  26.3 0.8 %shard_map.78.refs_16_ = bf16[8,24,512]{2,1,0:T(8,128)(2,1)S(1)} custom-call(s32[1]{0:T(128)S(6)} %copy.9.step_ref, bf16[2,24,4096]{2,1,0:T(8,128)(2,1)S(1)} %copy-done.1, bf16[24,2048]{1,0:T(8,128)(2,1)S(1)} %collective-permute-done.1.refs_0_, bf16[24,2048]{1,0:T(8,128)(2,1)S(1)} %collective-permute-done.2.refs_1_, ...), custom_call_target="tpu_custom_call" | custom-call | tf_op jit(solution)/shard_map/pallas_call | solution.py:180
  27.2 1.0 %shard_map.79 = (bf16[24,1024]{1,0:T(8,128)(2,1)S(1)}, bf16[24,1024]{1,0:T(8,128)(2,1)S(1)}, bf16[24,1024]{1,0:T(8,128)(2,1)S(1)}, bf16[24,1024]{1,0:T(8,128)(2,...) custom-call(s32[1]{0:T(128)S(6)} %copy.9.step_ref, ...), custom_call_target="tpu_custom_call" | custom-call | tf_op jit(solution)/shard_map/pallas_call | solution.py:243
  28.2 2.6 %collective-permute-start.16 = (bf16[24,1024]{1,0:T(8,128)(2,1)S(1)}, bf16[24,1024]{1,0:T(8,128)(2,1)S(1)}, u32[]{:S(2)}, u32[]{:S(2)}) collective-permute-start(bf16[24,1024]{1,0:T(8,128)(2,1)S(1)} %get-tuple-element.46), channel_id=1, source_target_pairs={{0,14},{1,15},{2,12},{3,13},{4,10},{5,11},{6,8},{7,9},{8,6},{9,7},... | collective-permute-start | bytes 147464 | tf_op jit(solution)/shard_map/ppermute | solution.py:32
  30.8 1.8 %collective-permute-start.17 = (bf16[24,1024]{1,0:T(8,128)(2,1)S(1)}, bf16[24,1024]{1,0:T(8,128)(2,1)S(1)}, u32[]{:S(2)}, u32[]{:S(2)}) collective-permute-start(bf16[24,1024]{1,0:T(8,128)(2,1)S(1)} %get-tuple-element.47), channel_id=1, source_target_pairs={{0,12},{1,13},{2,14},{3,15},{4,8},{5,9},{6,10},{7,11},{8,4},{9,5},... | collective-permute-start | bytes 147464 | tf_op jit(solution)/shard_map/ppermute | solution.py:32
  32.6 3.1 %collective-permute-start.18 = (bf16[24,1024]{1,0:T(8,128)(2,1)S(1)}, bf16[24,1024]{1,0:T(8,128)(2,1)S(1)}, u32[]{:S(2)}, u32[]{:S(2)}) collective-permute-start(bf16[24,1024]{1,0:T(8,128)(2,1)S(1)} %get-tuple-element.48), channel_id=1, source_target_pairs={{0,8},{1,9},{2,10},{3,11},{4,12},{5,13},{6,14},{7,15},{8,0},{9,1},... | collective-permute-start | bytes 147464 | tf_op jit(solution)/shard_map/ppermute | solution.py:32
  35.9 2.3 %collective-permute-start.20 = (bf16[24,1024]{1,0:T(8,128)(2,1)S(1)}, bf16[24,1024]{1,0:T(8,128)(2,1)S(1)}, u32[]{:S(2)}, u32[]{:S(2)}) collective-permute-start(bf16[24,1024]{1,0:T(8,128)(2,1)S(1)} %get-tuple-element.50), channel_id=1, source_target_pairs={{0,6},{1,7},{2,4},{3,5},{4,2},{5,3},{6,0},{7,1},{8,14},{9,15},{10,... | collective-permute-start | bytes 147464 | tf_op jit(solution)/shard_map/ppermute | solution.py:32
  38.2 0.6 %collective-permute-start.21 = (bf16[24,1024]{1,0:T(8,128)(2,1)S(1)}, bf16[24,1024]{1,0:T(8,128)(2,1)S(1)}, u32[]{:S(2)}, u32[]{:S(2)}) collective-permute-start(bf16[24,1024]{1,0:T(8,128)(2,1)S(1)} %get-tuple-element.51), channel_id=1, source_target_pairs={{0,4},{1,5},{2,6},{3,7},{4,0},{5,1},{6,2},{7,3},{8,12},{9,13},{10,... | collective-permute-start | bytes 147464 | tf_op jit(solution)/shard_map/ppermute | solution.py:32
  38.7 0.7 %collective-permute-start.22 = (bf16[24,1024]{1,0:T(8,128)(2,1)S(1)}, bf16[24,1024]{1,0:T(8,128)(2,1)S(1)}, u32[]{:S(2)}, u32[]{:S(2)}) collective-permute-start(bf16[24,1024]{1,0:T(8,128)(2,1)S(1)} %get-tuple-element.52), channel_id=1, source_target_pairs={{0,2},{1,3},{2,0},{3,1},{4,6},{5,7},{6,4},{7,5},{8,10},{9,11},{10,... | collective-permute-start | bytes 147464 | tf_op jit(solution)/shard_map/ppermute | solution.py:32
  39.4 0.9 %shard_map.81 = bf16[2,2,384,256]{3,2,1,0:T(8,128)(2,1)} custom-call(s32[1]{0:T(128)S(6)} %copy.9.step_ref, bf16[2,2,384,256]{3,2,1,0:T(8,128)(2,1)S(1)} %bitcast.7, bf16[2,384,256]{2,1,0:T(8,128)(2,1)S(1)} %get-tuple-element.55.renewed_ref), custom_call_target="tpu_custom_call" | custom-call | tf_op jit(solution)/shard_map/pallas_call | solution.py:269
  40.3 1.3 %collective-permute-done.18.refs_2_ = bf16[24,1024]{1,0:T(8,128)(2,1)S(1)} collective-permute-done((bf16[24,1024]{1,0:T(8,128)(2,1)S(1)}, bf16[24,1024]{1,0:T(8,128)(2,1)S(1)}, u32[]{:S(2)}, u32[]{:S(2)}) %collective-permute-start.18) | collective-permute-done | bytes 49184 | tf_op jit(solution)/shard_map/ppermute | solution.py:32
  41.6 0.8 %collective-permute-done.19.refs_3_ = bf16[24,1024]{1,0:T(8,128)(2,1)S(1)} collective-permute-done((bf16[24,1024]{1,0:T(8,128)(2,1)S(1)}, bf16[24,1024]{1,0:T(8,128)(2,1)S(1)}, u32[]{:S(2)}, u32[]{:S(2)}) %collective-permute-start.19) | collective-permute-done | bytes 49184 | tf_op jit(solution)/shard_map/ppermute | solution.py:32
  42.4 0.5 %collective-permute-done.20.refs_4_ = bf16[24,1024]{1,0:T(8,128)(2,1)S(1)} collective-permute-done((bf16[24,1024]{1,0:T(8,128)(2,1)S(1)}, bf16[24,1024]{1,0:T(8,128)(2,1)S(1)}, u32[]{:S(2)}, u32[]{:S(2)}) %collective-permute-start.20) | collective-permute-done | bytes 49184 | tf_op jit(solution)/shard_map/ppermute | solution.py:32
  43.3 0.8 %shard_map.80 = bf16[2,24,4096]{2,1,0:T(8,128)(2,1)} custom-call(s32[1]{0:T(128)S(6)} %copy.9.step_ref, bf16[24,1024]{1,0:T(8,128)(2,1)S(1)} %collective-permute-done.16.refs_0_, bf16[24,1024]{1,0:T(8,128)(2,1)S(1)} %collective-permute-done.17.refs_1_, bf16[24,1024]{1,0:T(8,128)(2,1)S(1)} %collective-permute-done.18.refs_2_, ...), custom_call_target="tpu_custom_call" | custom-call | tf_op jit(solution)/shard_map/pallas_call | solution.py:299
  (33 shorter events, 3.5 us)
Async XLA Ops:
  0.6 3.5 %collective-permute-start = (bf16[2,2,384,256]{3,2,1,0:T(8,128)(2,1)}, bf16[2,2,384,256]{3,2,1,0:T(8,128)(2,1)S(1)}, u32[]{:S(2)}, u32[]{:S(2)}) collective-permute-start(bf16[2,2,384,256]{3,2,1,0:T(8,128)(2,1)} %bitcast.4), channel_id=1, source_target_pairs={{0,1},{1,0},{2,3},{3,2},{4,5},{5,4},{6,7},{7,6},{8,9},{9,8},{10,11... | collective-permute-start | bytes 2359304 | tf_op jit(solution)/shard_map/ppermute | solution.py:32
  1.8 24.4 %copy-start = (bf16[2,2,1,16,24,256]{5,4,3,2,1,0:T(8,128)(2,1)S(1)}, bf16[2,2,1,16,24,256]{5,4,3,2,1,0:T(8,128)(2,1)}, u32[]{:S(2)}) copy-start(bf16[2,2,1,16,24,256]{5,4,3,2,1,0:T(8,128)(2,1)} %param.9) | copy-start | bytes 2359300
  4.2 10.5 %collective-permute-start.1 = (bf16[24,2048]{1,0:T(8,128)(2,1)}, bf16[24,2048]{1,0:T(8,128)(2,1)S(1)}, u32[]{:S(2)}, u32[]{:S(2)}) collective-permute-start(bf16[24,2048]{1,0:T(8,128)(2,1)} %get-tuple-element.37), channel_id=1, source_target_pairs={{0,10},{1,11},{2,8},{3,9},{4,14},{5,15},{6,12},{7,13},{8,2},{9,3},... | collective-permute-start | bytes 294920 | tf_op jit(solution)/shard_map/ppermute | solution.py:32
  8.8 8.9 %collective-permute-start.2 = (bf16[24,2048]{1,0:T(8,128)(2,1)}, bf16[24,2048]{1,0:T(8,128)(2,1)S(1)}, u32[]{:S(2)}, u32[]{:S(2)}) collective-permute-start(bf16[24,2048]{1,0:T(8,128)(2,1)} %get-tuple-element.38), channel_id=1, source_target_pairs={{0,6},{1,7},{2,4},{3,5},{4,2},{5,3},{6,0},{7,1},{8,14},{9,15},{10,... | collective-permute-start | bytes 294920 | tf_op jit(solution)/shard_map/ppermute | solution.py:32
  10.3 11.1 %collective-permute-start.3 = (bf16[24,2048]{1,0:T(8,128)(2,1)}, bf16[24,2048]{1,0:T(8,128)(2,1)S(1)}, u32[]{:S(2)}, u32[]{:S(2)}) collective-permute-start(bf16[24,2048]{1,0:T(8,128)(2,1)} %get-tuple-element.39), channel_id=1, source_target_pairs={{0,8},{1,9},{2,10},{3,11},{4,12},{5,13},{6,14},{7,15},{8,0},{9,1},... | collective-permute-start | bytes 294920 | tf_op jit(solution)/shard_map/ppermute | solution.py:32
  10.6 10.8 %collective-permute-start.4 = (bf16[24,2048]{1,0:T(8,128)(2,1)}, bf16[24,2048]{1,0:T(8,128)(2,1)S(1)}, u32[]{:S(2)}, u32[]{:S(2)}) collective-permute-start(bf16[24,2048]{1,0:T(8,128)(2,1)} %get-tuple-element.40), channel_id=1, source_target_pairs={{0,12},{1,13},{2,14},{3,15},{4,8},{5,9},{6,10},{7,11},{8,4},{9,5},... | collective-permute-start | bytes 294920 | tf_op jit(solution)/shard_map/ppermute | solution.py:32
  13.1 8.8 %collective-permute-start.5 = (bf16[24,2048]{1,0:T(8,128)(2,1)}, bf16[24,2048]{1,0:T(8,128)(2,1)S(1)}, u32[]{:S(2)}, u32[]{:S(2)}) collective-permute-start(bf16[24,2048]{1,0:T(8,128)(2,1)} %get-tuple-element.41), channel_id=1, source_target_pairs={{0,4},{1,5},{2,6},{3,7},{4,0},{5,1},{6,2},{7,3},{8,12},{9,13},{10,... | collective-permute-start | bytes 294920 | tf_op jit(solution)/shard_map/ppermute | solution.py:32
  14.6 7.3 %collective-permute-start.6 = (bf16[24,2048]{1,0:T(8,128)(2,1)}, bf16[24,2048]{1,0:T(8,128)(2,1)S(1)}, u32[]{:S(2)}, u32[]{:S(2)}) collective-permute-start(bf16[24,2048]{1,0:T(8,128)(2,1)} %get-tuple-element.42), channel_id=1, source_target_pairs={{0,2},{1,3},{2,0},{3,1},{4,6},{5,7},{6,4},{7,5},{8,10},{9,11},{10,... | collective-permute-start | bytes 294920 | tf_op jit(solution)/shard_map/ppermute | solution.py:32
  17.7 7.5 %collective-permute-start.7 = (bf16[24,2048]{1,0:T(8,128)(2,1)}, bf16[24,2048]{1,0:T(8,128)(2,1)S(1)}, u32[]{:S(2)}, u32[]{:S(2)}) collective-permute-start(bf16[24,2048]{1,0:T(8,128)(2,1)} %get-tuple-element.43), channel_id=1, source_target_pairs={{0,14},{1,15},{2,12},{3,13},{4,10},{5,11},{6,8},{7,9},{8,6},{9,7},... | collective-permute-start | bytes 294920 | tf_op jit(solution)/shard_map/ppermute | solution.py:32
  21.4 3.8 %collective-permute-start.15 = (bf16[24,2048]{1,0:T(8,128)(2,1)}, bf16[24,2048]{1,0:T(8,128)(2,1)S(1)}, u32[]{:S(2)}, u32[]{:S(2)}) collective-permute-start(bf16[24,2048]{1,0:T(8,128)(2,1)} %get-tuple-element.44.refs_7_), channel_id=1, source_target_pairs={{0,1},{1,0},{2,3},{3,2},{4,5},{5,4},{6,7},{7,6},{8,9},{9,8},{10,11... | collective-permute-start | bytes 294920 | tf_op jit(solution)/shard_map/ppermute | solution.py:32
  21.4 4.3 %collective-permute-start.8 = (bf16[24,2048]{1,0:T(8,128)(2,1)S(1)}, bf16[24,2048]{1,0:T(8,128)(2,1)S(1)}, u32[]{:S(2)}, u32[]{:S(2)}) collective-permute-start(bf16[24,2048]{1,0:T(8,128)(2,1)S(1)} %collective-permute-done.1.refs_0_), channel_id=1, source_target_pairs={{0,1},{1,0},{2,3},{3,2},{4,5},{5,4},{6,7},{7,6},{8,9},{9,8},{10,11... | collective-permute-start | bytes 294920 | tf_op jit(solution)/shard_map/ppermute | solution.py:32
  21.9 3.9 %collective-permute-start.9 = (bf16[24,2048]{1,0:T(8,128)(2,1)S(1)}, bf16[24,2048]{1,0:T(8,128)(2,1)S(1)}, u32[]{:S(2)}, u32[]{:S(2)}) collective-permute-start(bf16[24,2048]{1,0:T(8,128)(2,1)S(1)} %collective-permute-done.2.refs_1_), channel_id=1, source_target_pairs={{0,1},{1,0},{2,3},{3,2},{4,5},{5,4},{6,7},{7,6},{8,9},{9,8},{10,11... | collective-permute-start | bytes 294920 | tf_op jit(solution)/shard_map/ppermute | solution.py:32
  22.0 5.1 %collective-permute-start.10 = (bf16[24,2048]{1,0:T(8,128)(2,1)S(1)}, bf16[24,2048]{1,0:T(8,128)(2,1)S(1)}, u32[]{:S(2)}, u32[]{:S(2)}) collective-permute-start(bf16[24,2048]{1,0:T(8,128)(2,1)S(1)} %collective-permute-done.3.refs_2_), channel_id=1, source_target_pairs={{0,1},{1,0},{2,3},{3,2},{4,5},{5,4},{6,7},{7,6},{8,9},{9,8},{10,11... | collective-permute-start | bytes 294920 | tf_op jit(solution)/shard_map/ppermute | solution.py:32
  25.2 1.9 %collective-permute-start.11 = (bf16[24,2048]{1,0:T(8,128)(2,1)S(1)}, bf16[24,2048]{1,0:T(8,128)(2,1)S(1)}, u32[]{:S(2)}, u32[]{:S(2)}) collective-permute-start(bf16[24,2048]{1,0:T(8,128)(2,1)S(1)} %collective-permute-done.4.refs_3_), channel_id=1, source_target_pairs={{0,1},{1,0},{2,3},{3,2},{4,5},{5,4},{6,7},{7,6},{8,9},{9,8},{10,11... | collective-permute-start | bytes 294920 | tf_op jit(solution)/shard_map/ppermute | solution.py:32
  25.2 1.9 %collective-permute-start.12 = (bf16[24,2048]{1,0:T(8,128)(2,1)S(1)}, bf16[24,2048]{1,0:T(8,128)(2,1)S(1)}, u32[]{:S(2)}, u32[]{:S(2)}) collective-permute-start(bf16[24,2048]{1,0:T(8,128)(2,1)S(1)} %collective-permute-done.5.refs_4_), channel_id=1, source_target_pairs={{0,1},{1,0},{2,3},{3,2},{4,5},{5,4},{6,7},{7,6},{8,9},{9,8},{10,11... | collective-permute-start | bytes 294920 | tf_op jit(solution)/shard_map/ppermute | solution.py:32
  25.7 1.4 %collective-permute-start.13 = (bf16[24,2048]{1,0:T(8,128)(2,1)S(1)}, bf16[24,2048]{1,0:T(8,128)(2,1)S(1)}, u32[]{:S(2)}, u32[]{:S(2)}) collective-permute-start(bf16[24,2048]{1,0:T(8,128)(2,1)S(1)} %collective-permute-done.6.refs_5_), channel_id=1, source_target_pairs={{0,1},{1,0},{2,3},{3,2},{4,5},{5,4},{6,7},{7,6},{8,9},{9,8},{10,11... | collective-permute-start | bytes 294920 | tf_op jit(solution)/shard_map/ppermute | solution.py:32
  25.8 1.4 %collective-permute-start.14 = (bf16[24,2048]{1,0:T(8,128)(2,1)S(1)}, bf16[24,2048]{1,0:T(8,128)(2,1)S(1)}, u32[]{:S(2)}, u32[]{:S(2)}) collective-permute-start(bf16[24,2048]{1,0:T(8,128)(2,1)S(1)} %collective-permute-done.7.refs_6_), channel_id=1, source_target_pairs={{0,1},{1,0},{2,3},{3,2},{4,5},{5,4},{6,7},{7,6},{8,9},{9,8},{10,11... | collective-permute-start | bytes 294920 | tf_op jit(solution)/shard_map/ppermute | solution.py:32
  28.2 10.0 %collective-permute-start.16 = (bf16[24,1024]{1,0:T(8,128)(2,1)S(1)}, bf16[24,1024]{1,0:T(8,128)(2,1)S(1)}, u32[]{:S(2)}, u32[]{:S(2)}) collective-permute-start(bf16[24,1024]{1,0:T(8,128)(2,1)S(1)} %get-tuple-element.46), channel_id=1, source_target_pairs={{0,14},{1,15},{2,12},{3,13},{4,10},{5,11},{6,8},{7,9},{8,6},{9,7},... | collective-permute-start | bytes 147464 | tf_op jit(solution)/shard_map/ppermute | solution.py:32
  30.8 7.9 %collective-permute-start.17 = (bf16[24,1024]{1,0:T(8,128)(2,1)S(1)}, bf16[24,1024]{1,0:T(8,128)(2,1)S(1)}, u32[]{:S(2)}, u32[]{:S(2)}) collective-permute-start(bf16[24,1024]{1,0:T(8,128)(2,1)S(1)} %get-tuple-element.47), channel_id=1, source_target_pairs={{0,12},{1,13},{2,14},{3,15},{4,8},{5,9},{6,10},{7,11},{8,4},{9,5},... | collective-permute-start | bytes 147464 | tf_op jit(solution)/shard_map/ppermute | solution.py:32
  32.6 9.0 %collective-permute-start.18 = (bf16[24,1024]{1,0:T(8,128)(2,1)S(1)}, bf16[24,1024]{1,0:T(8,128)(2,1)S(1)}, u32[]{:S(2)}, u32[]{:S(2)}) collective-permute-start(bf16[24,1024]{1,0:T(8,128)(2,1)S(1)} %get-tuple-element.48), channel_id=1, source_target_pairs={{0,8},{1,9},{2,10},{3,11},{4,12},{5,13},{6,14},{7,15},{8,0},{9,1},... | collective-permute-start | bytes 147464 | tf_op jit(solution)/shard_map/ppermute | solution.py:32
  35.8 6.6 %collective-permute-start.19 = (bf16[24,1024]{1,0:T(8,128)(2,1)S(1)}, bf16[24,1024]{1,0:T(8,128)(2,1)S(1)}, u32[]{:S(2)}, u32[]{:S(2)}) collective-permute-start(bf16[24,1024]{1,0:T(8,128)(2,1)S(1)} %get-tuple-element.49), channel_id=1, source_target_pairs={{0,10},{1,11},{2,8},{3,9},{4,14},{5,15},{6,12},{7,13},{8,2},{9,3},... | collective-permute-start | bytes 147464 | tf_op jit(solution)/shard_map/ppermute | solution.py:32
  35.9 7.1 %collective-permute-start.20 = (bf16[24,1024]{1,0:T(8,128)(2,1)S(1)}, bf16[24,1024]{1,0:T(8,128)(2,1)S(1)}, u32[]{:S(2)}, u32[]{:S(2)}) collective-permute-start(bf16[24,1024]{1,0:T(8,128)(2,1)S(1)} %get-tuple-element.50), channel_id=1, source_target_pairs={{0,6},{1,7},{2,4},{3,5},{4,2},{5,3},{6,0},{7,1},{8,14},{9,15},{10,... | collective-permute-start | bytes 147464 | tf_op jit(solution)/shard_map/ppermute | solution.py:32
  38.2 5.0 %collective-permute-start.21 = (bf16[24,1024]{1,0:T(8,128)(2,1)S(1)}, bf16[24,1024]{1,0:T(8,128)(2,1)S(1)}, u32[]{:S(2)}, u32[]{:S(2)}) collective-permute-start(bf16[24,1024]{1,0:T(8,128)(2,1)S(1)} %get-tuple-element.51), channel_id=1, source_target_pairs={{0,4},{1,5},{2,6},{3,7},{4,0},{5,1},{6,2},{7,3},{8,12},{9,13},{10,... | collective-permute-start | bytes 147464 | tf_op jit(solution)/shard_map/ppermute | solution.py:32
  38.7 4.6 %collective-permute-start.22 = (bf16[24,1024]{1,0:T(8,128)(2,1)S(1)}, bf16[24,1024]{1,0:T(8,128)(2,1)S(1)}, u32[]{:S(2)}, u32[]{:S(2)}) collective-permute-start(bf16[24,1024]{1,0:T(8,128)(2,1)S(1)} %get-tuple-element.52), channel_id=1, source_target_pairs={{0,2},{1,3},{2,0},{3,1},{4,6},{5,7},{6,4},{7,5},{8,10},{9,11},{10,... | collective-permute-start | bytes 147464 | tf_op jit(solution)/shard_map/ppermute | solution.py:32
  (2 other events, 47.5 us)
